TPU v7x, 32 devices: a whole 2x2x4 slice. The times are simulated.
32 devices in a mesh: section: 4 (over y, x), dp: 8 (over z, core).
Axes of the slice: x: 2, y: 2, z: 4, core: 2. Of those that a mesh axis runs over, the one named last changes fastest.
Arguments:
- inputs: bfloat16 [16, 512, 768], P('dp'), may hold values from -6 to 6
- evaluation_input: bfloat16 [16, 512, 768], P('dp'), may hold values from -6 to 6
- output_cotangent: bfloat16 [16, 512, 768], P('dp'), may hold values from -6 to 6
- packed_segment_lengths: int32 [16, 8], P('dp'), may hold values from 1 to 384, 512 in all within a row
- attention_in_weight: bfloat16 [4, 768, 2304], P('section', 'dp'), may hold values from -0.21875 to 0.21875
- attention_out_weight: bfloat16 [4, 768, 768], P('section', 'dp'), may hold values from -0.625 to 0.625
- feedforward_in_weight: bfloat16 [4, 768, 3072], P('section', 'dp'), may hold values from -0.21875 to 0.21875
- feedforward_out_weight: bfloat16 [4, 3072, 768], P('section', 'dp'), may hold values from -0.109375 to 0.109375
- adapter_down_weight: bfloat16 [4, 768, 16], P('section'), may hold values from -0.21875 to 0.21875
- adapter_up_weight: float32 [4, 2, 8, 768], P('section'), may hold values from -1 to 1
- projection_biases: float32 [4, 4, 768], P('section'), may hold values from -3 to 3
- feedforward_bias: float32 [4, 3072], P('section'), may hold values from -3 to 3
- layer_norm_gain: float32 [4, 2, 768], P('section'), may hold values from 0.5 to 1.5
- layer_norm_shift: float32 [4, 2, 768], P('section'), may hold values from -2 to 2
Outputs:
- activations: bfloat16 [4, 16, 512, 768], P('section', 'dp')
- input_grads: bfloat16 [4, 16, 512, 768], P('section', 'dp')
- adapter_grads: float32 [4, 2, 8, 768], P('section')
- joined_outputs: bfloat16 [4, 16, 512, 768], P('section', 'dp')
Inputs may be any that keep to these rules, and one draw needn't show every extreme that they name: `packed_segment_lengths`: each row's 8 segment lengths sum to 512, and some row has a segment of exactly 384 tokens.
All inputs are finite; a program needn't handle non-finite values.
Results may differ from a plain program's by a relative error of at most 0.028.
Values may be sent and summed in bfloat16 or wider, within the bound.
No kernel may reach another device: no remote copies, remote signals or barrier semaphores. Data moves between devices by JAX's collectives and lax.ppermute only.
A program may use at most 128 MiB of HBM per device.

v0:
```python
from functools import partial

import jax
import jax.numpy as jnp
from jax import lax
from jax.sharding import PartitionSpec as P

HEADS = 12


norm_eps = 1e-05
masked_score = -1e30


def passed_along(shard, axis, by):
    size = lax.axis_size(axis)
    pairs = [(i, i + by) for i in range(size) if 0 <= i + by < size]
    return lax.ppermute(shard, axis, pairs)


def normalize(value, gain, shift):
    centered = value - jnp.mean(value, axis=-1, keepdims=True)
    spread = jnp.mean(centered * centered, axis=-1, keepdims=True)
    return centered * lax.rsqrt(spread + norm_eps) * gain + shift


def segment_labels(lengths, length):
    ends = jnp.cumsum(lengths, axis=-1)
    places = jnp.arange(length, dtype=jnp.int32)
    return jnp.sum((places[None, :, None] >= ends[:, None, :]).astype(jnp.int32), axis=-1)


def split_heads(matrix):
    return matrix.reshape(matrix.shape[0], HEADS, matrix.shape[1] // HEADS)


def softmax_rows(query_rows, keys, allowed):
    scale = (query_rows.shape[1] // HEADS) ** (-0.5)
    scores = (
        jnp.einsum(
            "qhd,khd->hqk",
            split_heads(query_rows),
            split_heads(keys),
            preferred_element_type=jnp.float32,
        )
        * scale
    )
    scores = jnp.where(allowed[None], scores, masked_score)
    top = jnp.max(scores, axis=-1, keepdims=True)
    weights = jnp.exp(scores - top)
    return weights / jnp.sum(weights, axis=-1, keepdims=True)


def layer_forward(hidden_state, labels, frozen_weights, params, adapter_pair):
    input_weight, w_out, w_up, w_down = frozen_weights
    bias_rows, ffn_shift, gains, shifts = params
    width = w_out.shape[1]
    packed = jnp.dot(hidden_state, input_weight, preferred_element_type=jnp.float32)
    query_sum = packed[:, :width] + bias_rows[0]
    value_sum = packed[:, 2 * width :] + bias_rows[1]
    down_matrix = None
    if adapter_pair is not None:
        adapter_down_slice, adapter_up_slice = adapter_pair
        rank_index = adapter_up_slice.shape[1]
        down_matrix = jnp.dot(
            hidden_state, adapter_down_slice, preferred_element_type=jnp.float32
        ).astype(jnp.bfloat16)
        query_sum = query_sum + 2.0 * jnp.dot(
            down_matrix[:, :rank_index], adapter_up_slice[0], preferred_element_type=jnp.float32
        )
        value_sum = value_sum + 2.0 * jnp.dot(
            down_matrix[:, rank_index:], adapter_up_slice[1], preferred_element_type=jnp.float32
        )
    query_rows = query_sum.astype(jnp.bfloat16)
    keys = packed[:, width : 2 * width].astype(jnp.bfloat16)
    value_rows = value_sum.astype(jnp.bfloat16)
    allowed = labels[:, None] == labels[None, :]
    shares_full = softmax_rows(query_rows, keys, allowed)
    mixed = jnp.einsum(
        "hqk,khd->qhd",
        shares_full.astype(jnp.bfloat16),
        split_heads(value_rows),
        preferred_element_type=jnp.float32,
    )
    mixed = mixed.reshape(hidden_state.shape[0], width).astype(jnp.bfloat16)
    summed = hidden_state.astype(jnp.float32) + (
        jnp.dot(mixed, w_out, preferred_element_type=jnp.float32) + bias_rows[2]
    )
    first = normalize(summed, gains[0], shifts[0]).astype(jnp.bfloat16)
    inner = jnp.dot(first, w_up, preferred_element_type=jnp.float32) + ffn_shift
    activated = jax.nn.gelu(inner, approximate=False).astype(jnp.bfloat16)
    closing = first.astype(jnp.float32) + (
        jnp.dot(activated, w_down, preferred_element_type=jnp.float32) + bias_rows[3]
    )
    result = normalize(closing, gains[1], shifts[1]).astype(jnp.bfloat16)
    return (
        result,
        (down_matrix, query_rows, keys, value_rows, shares_full, summed, inner, closing),
    )


def layer_backward(hidden_state, labels, cotangent, frozen_weights, params, adapter_pair):
    input_weight, w_out, w_up, w_down = frozen_weights
    bias_rows, ffn_shift, gains, shifts = params
    adapter_down_slice, adapter_up_slice = adapter_pair
    rank_index = adapter_up_slice.shape[1]
    width = w_out.shape[1]
    length = hidden_state.shape[0]
    _, saved = layer_forward(hidden_state, labels, frozen_weights, params, adapter_pair)
    down_matrix, query_rows, keys, value_rows, shares_full, summed, inner, closing = saved
    _, closing_back = jax.vjp(partial(normalize, gain=gains[1], shift=shifts[1]), closing)
    d_closing = closing_back(cotangent.astype(jnp.float32))[0]
    d_branch = d_closing.astype(jnp.bfloat16)
    d_active = jnp.dot(d_branch, w_down.T, preferred_element_type=jnp.float32)
    _, gelu_back = jax.vjp(partial(jax.nn.gelu, approximate=False), inner)
    d_inner = gelu_back(d_active)[0].astype(jnp.bfloat16)
    _, summed_back = jax.vjp(partial(normalize, gain=gains[0], shift=shifts[0]), summed)
    d_summed = summed_back(
        d_closing + jnp.dot(d_inner, w_up.T, preferred_element_type=jnp.float32)
    )[0]
    d_attend = d_summed.astype(jnp.bfloat16)
    d_mixed = split_heads(
        jnp.dot(d_attend, w_out.T, preferred_element_type=jnp.float32).astype(jnp.bfloat16)
    )
    shares = shares_full.astype(jnp.bfloat16)
    value_gradient = jnp.einsum(
        "hqk,qhd->khd", shares, d_mixed, preferred_element_type=jnp.float32
    ).astype(jnp.bfloat16)
    d_shares = jnp.einsum(
        "qhd,khd->hqk", d_mixed, split_heads(value_rows), preferred_element_type=jnp.float32
    )
    d_scores = (
        shares_full * (d_shares - jnp.sum(d_shares * shares_full, axis=-1, keepdims=True))
    ).astype(jnp.bfloat16)
    scale = (width // HEADS) ** (-0.5)
    query_gradient = (
        jnp.einsum("hqk,khd->qhd", d_scores, split_heads(keys), preferred_element_type=jnp.float32)
        * scale
    ).astype(jnp.bfloat16)
    d_keys = (
        jnp.einsum(
            "hqk,qhd->khd", d_scores, split_heads(query_rows), preferred_element_type=jnp.float32
        )
        * scale
    ).astype(jnp.bfloat16)
    query_gradient = query_gradient.reshape(length, width)
    d_keys = d_keys.reshape(length, width)
    value_gradient = value_gradient.reshape(length, width)
    d_packed = jnp.concatenate([query_gradient, d_keys, value_gradient], axis=1)
    down_gradient = 2.0 * jnp.concatenate(
        [
            jnp.dot(query_gradient, adapter_up_slice[0].T, preferred_element_type=jnp.float32),
            jnp.dot(value_gradient, adapter_up_slice[1].T, preferred_element_type=jnp.float32),
        ],
        axis=1,
    )
    down_gradient = down_gradient.astype(jnp.bfloat16)
    hidden_gradient = d_summed + jnp.dot(
        d_packed, input_weight.T, preferred_element_type=jnp.float32
    )
    hidden_gradient = hidden_gradient + jnp.dot(
        down_gradient, adapter_down_slice.T, preferred_element_type=jnp.float32
    )
    d_upper = 2.0 * jnp.stack(
        [
            jnp.dot(
                down_matrix[:, :rank_index].T, query_gradient, preferred_element_type=jnp.float32
            ),
            jnp.dot(
                down_matrix[:, rank_index:].T, value_gradient, preferred_element_type=jnp.float32
            ),
        ]
    )
    return (hidden_gradient.astype(jnp.bfloat16), d_upper)


def merge_adapter_weight(weight_rows, adapter_rows, adapter_up_weight):
    width = weight_rows.shape[1] // 3
    rank_index = adapter_up_weight.shape[1]
    extra_query = 2.0 * jnp.dot(
        adapter_rows[:, :rank_index].astype(jnp.float32),
        adapter_up_weight[0],
        precision=lax.Precision.HIGHEST,
    )
    extra_value = 2.0 * jnp.dot(
        adapter_rows[:, rank_index:].astype(jnp.float32),
        adapter_up_weight[1],
        precision=lax.Precision.HIGHEST,
    )
    query_columns = (weight_rows[:, :width].astype(jnp.float32) + extra_query).astype(jnp.bfloat16)
    value_columns = (weight_rows[:, 2 * width :].astype(jnp.float32) + extra_value).astype(
        jnp.bfloat16
    )
    return jnp.concatenate(
        [query_columns, weight_rows[:, width : 2 * width], value_columns], axis=1
    )


def run_forward(sources, labels, frozen_weights, params, adapter_pair):
    sections = lax.axis_size("section")
    place = lax.axis_index("section")
    batches = sources.shape[0]
    blank = jnp.zeros(sources.shape[1:], jnp.bfloat16)

    def compute(entry, row_segment_labels):
        return layer_forward(entry, row_segment_labels, frozen_weights, params, adapter_pair)[0]

    def skipped(entry, row_segment_labels):
        return jnp.zeros_like(entry)

    def advance(step, state):
        arrived, outputs, kept = state
        order = step - place
        valid = (order >= 0) & (order < batches)
        slot = jnp.clip(order, 0, batches - 1)
        fresh = lax.dynamic_index_in_dim(sources, jnp.clip(step, 0, batches - 1), 0, keepdims=False)
        entry = jnp.where(place == 0, fresh, arrived)
        row_segment_labels = lax.dynamic_index_in_dim(labels, slot, 0, keepdims=False)
        result = lax.cond(valid, compute, skipped, entry, row_segment_labels)
        before = lax.dynamic_index_in_dim(outputs, slot, 0, keepdims=False)
        outputs = lax.dynamic_update_index_in_dim(
            outputs, jnp.where(valid, result, before), slot, 0
        )
        stored = lax.dynamic_index_in_dim(kept, slot, 0, keepdims=False)
        kept = lax.dynamic_update_index_in_dim(kept, jnp.where(valid, entry, stored), slot, 0)
        arrived = passed_along(result, "section", 1)
        return (arrived, outputs, kept)

    empty = jnp.zeros(sources.shape, jnp.bfloat16)
    state = lax.fori_loop(0, batches + sections - 1, advance, (blank, empty, empty))
    return (state[1], state[2])


def run_backward(kept, labels, cotangents, frozen_weights, params, adapter_pair):
    sections = lax.axis_size("section")
    place = lax.axis_index("section")
    batches = kept.shape[0]
    delay = sections - 1 - place
    blank = jnp.zeros(kept.shape[1:], jnp.bfloat16)
    adapter_up_slice = adapter_pair[1]
    upper_zero_block = jnp.zeros(
        (2, adapter_up_slice.shape[1], adapter_up_slice.shape[2]), jnp.float32
    )

    def compute(entry, section_input, row_segment_labels):
        return layer_backward(
            section_input, row_segment_labels, entry, frozen_weights, params, adapter_pair
        )

    def skipped(entry, section_input, row_segment_labels):
        return (jnp.zeros_like(entry), upper_zero_block)

    def retreat(step, state):
        arrived, grads, upper = state
        order = step - delay
        valid = (order >= 0) & (order < batches)
        slot = jnp.clip(order, 0, batches - 1)
        fresh = lax.dynamic_index_in_dim(
            cotangents, jnp.clip(step, 0, batches - 1), 0, keepdims=False
        )
        entry = jnp.where(place == sections - 1, fresh, arrived)
        section_input = lax.dynamic_index_in_dim(kept, slot, 0, keepdims=False)
        row_segment_labels = lax.dynamic_index_in_dim(labels, slot, 0, keepdims=False)
        hidden_gradient, d_upper = lax.cond(
            valid, compute, skipped, entry, section_input, row_segment_labels
        )
        before = lax.dynamic_index_in_dim(grads, slot, 0, keepdims=False)
        grads = lax.dynamic_update_index_in_dim(
            grads, jnp.where(valid, hidden_gradient, before), slot, 0
        )
        upper = upper + d_upper
        arrived = passed_along(hidden_gradient, "section", -1)
        return (arrived, grads, upper)

    empty = jnp.zeros(kept.shape, jnp.bfloat16)
    state = lax.fori_loop(0, batches + sections - 1, retreat, (blank, empty, upper_zero_block))
    return (state[1], state[2])


def body(
    inputs,
    evaluation_input,
    output_cotangent,
    packed_segment_lengths,
    attention_in_weight,
    attention_out_weight,
    feedforward_in_weight,
    feedforward_out_weight,
    adapter_down_weight,
    adapter_up_weight,
    projection_biases,
    feedforward_bias,
    layer_norm_gain,
    layer_norm_shift,
):
    labels = segment_labels(packed_segment_lengths, inputs.shape[1])
    params = (projection_biases[0], feedforward_bias[0], layer_norm_gain[0], layer_norm_shift[0])
    adapter_pair = (adapter_down_weight[0], adapter_up_weight[0].astype(jnp.bfloat16))
    frozen_weights = (
        lax.all_gather(attention_in_weight[0], "dp", axis=0, tiled=True),
        lax.all_gather(attention_out_weight[0], "dp", axis=0, tiled=True),
        lax.all_gather(feedforward_in_weight[0], "dp", axis=0, tiled=True),
        lax.all_gather(feedforward_out_weight[0], "dp", axis=0, tiled=True),
    )
    outputs, kept = run_forward(inputs, labels, frozen_weights, params, adapter_pair)
    grads, upper = run_backward(
        kept, labels, output_cotangent, frozen_weights, params, adapter_pair
    )
    merged_matrix = (
        merge_adapter_weight(frozen_weights[0], adapter_down_weight[0], adapter_up_weight[0]),
    ) + tuple(frozen_weights[1:])
    joined, _ = run_forward(evaluation_input, labels, merged_matrix, params, None)
    upper_total = lax.psum(upper, "dp")
    return (outputs[None], grads[None], upper_total[None], joined[None])


def solution(mesh):
    in_specs = (
        P("dp", None, None),
        P("dp", None, None),
        P("dp", None, None),
        P("dp", None),
        P("section", "dp", None),
        P("section", "dp", None),
        P("section", "dp", None),
        P("section", "dp", None),
        P("section", None, None),
        P("section", None, None, None),
        P("section", None, None),
        P("section", None),
        P("section", None, None),
        P("section", None, None),
    )
    out_specs = (
        P("section", "dp", None, None),
        P("section", "dp", None, None),
        P("section", None, None, None),
        P("section", "dp", None, None),
    )
    return jax.shard_map(body, mesh=mesh, in_specs=in_specs, out_specs=out_specs, check_vma=False)
```

profile of v0, /device:TPU:30, one launch (start us, length us, event | category | flops | bytes accessed | tf_op | source)
XLA Modules:
  0.0 1566.3 jit_solution(4980207777495891468)
XLA Ops:
  12.3 37.7 %all-gather.9.cloned.1.call-done = bf16[1,768,2304]{2,1,0:T(8,128)(2,1)} async-done(((bf16[1,96,2304]{2,1,0:T(8,128)(2,1)}), bf16[1,768,2304]{2,1,0:T(8,128)(2,1)}) %all-gather.9.cloned.1.call-update) | async-done | bytes 3538960 | tf_op jit(solution)/shard_map/all_gather | solution.py:300
  74.2 52.1 %all-gather.13.cloned.1.call-done = bf16[1,768,3072]{2,1,0:T(8,128)(2,1)} async-done(((bf16[1,96,3072]{2,1,0:T(8,128)(2,1)}), bf16[1,768,3072]{2,1,0:T(8,128)(2,1)}) %all-gather.13.cloned.1.call-update) | async-done | bytes 4718608 | tf_op jit(solution)/shard_map/all_gather | solution.py:302
  126.3 52.0 %all-gather.15.cloned.1.call-done = bf16[1,3072,768]{2,1,0:T(8,128)(2,1)} async-done(((bf16[1,384,768]{2,1,0:T(8,128)(2,1)}), bf16[1,3072,768]{2,1,0:T(8,128)(2,1)}) %all-gather.15.cloned.1.call-update) | async-done | bytes 4718608 | tf_op jit(solution)/shard_map/all_gather | solution.py:303
  180.9 379.9 %while.54 = (s32[]{:T(128)}, bf16[512,768]{1,0:T(8,128)(2,1)S(1)}, bf16[2,512,768]{2,1,0:T(8,128)(2,1)}, bf16[2,512,768]{2,1,0:T(8,128)(2,1)}, s32[]{:T(128)}, /...) while((s32[]{:T(128)}, bf16[512,768]{1,0:T(8,128)(2,1)S(1)}, ...), condition=%wide.region_11.12_spmd, body=%wide.region_2.11_spmd.sunk | while | flops 8217306624 | bytes 115116192 | solution.py:230
  206.1 18.0 %collective-permute-done = bf16[512,768]{1,0:T(8,128)(2,1)S(1)} collective-permute-done((bf16[512,768]{1,0:T(8,128)(2,1)S(1)}, bf16[512,768]{1,0:T(8,128)(2,1)S(1)}, u32[]{:S(2)}, u32[]{:S(2)}) %collective-permute-start) | collective-permute-done | bytes 786464 | tf_op jit(solution)/shard_map/while/body/eval_jaxpr/ppermute | solution.py:18
  255.9 160.2 %collective-permute-done = bf16[512,768]{1,0:T(8,128)(2,1)S(1)} collective-permute-done((bf16[512,768]{1,0:T(8,128)(2,1)S(1)}, bf16[512,768]{1,0:T(8,128)(2,1)S(1)}, u32[]{:S(2)}, u32[]{:S(2)}) %collective-permute-start) | collective-permute-done | bytes 786464 | tf_op jit(solution)/shard_map/while/body/eval_jaxpr/ppermute | solution.py:18
  419.8 48.9 %conditional.7 = (bf16[512,768]{1,0:T(8,128)(2,1)S(1)}) conditional(s32[]{:T(128)} %convert_element_type.393, () %tuple.185, (bf16[512,768]{1,0:T(8,128)(2,1)S(1)}, bf16[768,2304]{1,0:T(8,128)(2,1)}, f32[4,768]{1,0:T(4,128)S(1)}, bf16[768,16]{0,1:T(8,128)(2,1)S(1)}, bf16[2,8,768]{2,1,0:T(8,128)(2,1)S(1)}, /*index=5*/s32[2,512]{1,0:T(2,128)S(1)}, ...), branch_computations={%region_3.3_spmd, %region_4.10_spmd} | conditional | flops 8216126976 | bytes 102236256 | solution.py:219
  446.4 21.7 %fusion.221 = (f32[512]{0:T(512)S(1)}, f32[512,768]{1,0:T(8,128)S(1)}) fusion(f32[768]{0:T(1024)S(1)} %get-tuple-element.1695, bf16[3072,768]{1,0:T(8,128)(2,1)} %get-tuple-element.1322, bf16[768,3072]{1,0:T(8,128)(2,1)} %get-tuple-element.1320, f32[3072]{0:T(1024)S(1)} %bitcast.234, f32[512,768]{1,0:T(8,128)} %copy-done.6, ...), kind=kOutput, calls=%fused_computation.355 | convolution fusion | flops 4941151744 | bytes 12610560 | tf_op jit(solution)/shard_map/while/body/eval_jaxpr/cond/branch_1_fun/dot_general | solution.py:93
  492.9 48.9 %conditional.7 = (bf16[512,768]{1,0:T(8,128)(2,1)S(1)}) conditional(s32[]{:T(128)} %convert_element_type.393, () %tuple.185, (bf16[512,768]{1,0:T(8,128)(2,1)S(1)}, bf16[768,2304]{1,0:T(8,128)(2,1)}, f32[4,768]{1,0:T(4,128)S(1)}, bf16[768,16]{0,1:T(8,128)(2,1)S(1)}, bf16[2,8,768]{2,1,0:T(8,128)(2,1)S(1)}, /*index=5*/s32[2,512]{1,0:T(2,128)S(1)}, ...), branch_computations={%region_3.3_spmd, %region_4.10_spmd} | conditional | flops 8216126976 | bytes 102236256 | solution.py:219
  519.5 21.7 %fusion.221 = (f32[512]{0:T(512)S(1)}, f32[512,768]{1,0:T(8,128)S(1)}) fusion(f32[768]{0:T(1024)S(1)} %get-tuple-element.1695, bf16[3072,768]{1,0:T(8,128)(2,1)} %get-tuple-element.1322, bf16[768,3072]{1,0:T(8,128)(2,1)} %get-tuple-element.1320, f32[3072]{0:T(1024)S(1)} %bitcast.234, f32[512,768]{1,0:T(8,128)} %copy-done.6, ...), kind=kOutput, calls=%fused_computation.355 | convolution fusion | flops 4941151744 | bytes 12610560 | tf_op jit(solution)/shard_map/while/body/eval_jaxpr/cond/branch_1_fun/dot_general | solution.py:93
  562.1 528.9 %while.56 = (s32[]{:T(128)}, bf16[512,768]{1,0:T(8,128)(2,1)S(1)}, bf16[2,512,768]{2,1,0:T(8,128)(2,1)}, f32[2,8,768]{2,1,0:T(8,128)S(1)}, s32[]{:T(128)}, /*ind...) while((s32[]{:T(128)}, bf16[512,768]{1,0:T(8,128)(2,1)S(1)}, ...), condition=%wide.region_26.27_spmd.clone, body=%wide.region_12.26_spmd.clone.sunk | while | flops 17187028992 | bytes 431099584 | solution.py:276
  562.5 107.1 %conditional.9 = (bf16[512,768]{1,0:T(8,128)(2,1)}, f32[2,8,768]{2,1,0:T(8,128)S(1)}) conditional(s32[]{:T(128)} %convert_element_type.395, () %tuple.191, (pred[]{:T(512)}, s32[]{:T(128)}, bf16[2,512,768]{2,1,0:T(8,128)(2,1)}, bf16[512,768]{1,0:T(8,128)(2,1)S(1)}, f32[2,768]{1,0:T(2,128)}, /*index=5*/bf16[2,512,768]{2,1,0:T(8,128)(2,1)}, ...), branch_computations={%region_13.13_spmd, %region_14.25_spmd} | conditional | flops 17186611200 | bytes 423873280 | solution.py:264
  685.4 107.3 %conditional.9 = (bf16[512,768]{1,0:T(8,128)(2,1)}, f32[2,8,768]{2,1,0:T(8,128)S(1)}) conditional(s32[]{:T(128)} %convert_element_type.395, () %tuple.191, (pred[]{:T(512)}, s32[]{:T(128)}, bf16[2,512,768]{2,1,0:T(8,128)(2,1)}, bf16[512,768]{1,0:T(8,128)(2,1)S(1)}, f32[2,768]{1,0:T(2,128)}, /*index=5*/bf16[2,512,768]{2,1,0:T(8,128)(2,1)}, ...), branch_computations={%region_13.13_spmd, %region_14.25_spmd} | conditional | flops 17186611200 | bytes 423873280 | solution.py:264
  818.8 103.1 %collective-permute-start.2 = (bf16[512,768]{1,0:T(8,128)(2,1)}, bf16[512,768]{1,0:T(8,128)(2,1)S(1)}, u32[]{:S(2)}, u32[]{:S(2)}) collective-permute-start(bf16[512,768]{1,0:T(8,128)(2,1)} %get-tuple-element.2183), channel_id=1, source_target_pairs={{8,0},{16,8},{24,16},{9,1},{17,9},{25,17},{10,2},{18,10},{26,18},{... | collective-permute-start | bytes 2359304 | tf_op jit(solution)/shard_map/while/body/eval_jaxpr/ppermute | solution.py:18
  961.0 101.7 %collective-permute-start.2 = (bf16[512,768]{1,0:T(8,128)(2,1)}, bf16[512,768]{1,0:T(8,128)(2,1)S(1)}, u32[]{:S(2)}, u32[]{:S(2)}) collective-permute-start(bf16[512,768]{1,0:T(8,128)(2,1)} %get-tuple-element.2183), channel_id=1, source_target_pairs={{8,0},{16,8},{24,16},{9,1},{17,9},{25,17},{10,2},{18,10},{26,18},{... | collective-permute-start | bytes 2359304 | tf_op jit(solution)/shard_map/while/body/eval_jaxpr/ppermute | solution.py:18
  1091.0 25.8 %psum.7 = f32[1,2,8,768]{3,2,1,0:T(8,128)} all-reduce(f32[1,2,8,768]{3,2,1,0:T(8,128)S(1)} %bitcast.221), channel_id=1, replica_groups=mesh['section'=4,'dp'=8] {'dp'}, use_global_device_ids=true, to_apply=%region_27.28 | all-reduce | flops 12288 | bytes 98304 | tf_op jit(solution)/shard_map/psum | solution.py:313
  1118.1 441.5 %while.55 = (s32[]{:T(128)}, bf16[512,768]{1,0:T(8,128)(2,1)S(1)}, bf16[2,512,768]{2,1,0:T(8,128)(2,1)}, s32[]{:T(128)}, pred[]{:T(512)}, /*index=5*/bf16[2,512,...) while((s32[]{:T(128)}, bf16[512,768]{1,0:T(8,128)(2,1)S(1)}, ...), condition=%wide.region_37.38_spmd, body=%wide.region_28.0_spmd.sunk | while | flops 8190559744 | bytes 116407960 | solution.py:230
  1121.8 28.9 %collective-permute-done.1 = bf16[512,768]{1,0:T(8,128)(2,1)S(1)} collective-permute-done((bf16[512,768]{1,0:T(8,128)(2,1)S(1)}, bf16[512,768]{1,0:T(8,128)(2,1)S(1)}, u32[]{:S(2)}, u32[]{:S(2)}) %collective-permute-start.1) | collective-permute-done | bytes 786464 | tf_op jit(solution)/shard_map/while/body/eval_jaxpr/ppermute | solution.py:18
  1154.2 113.6 %collective-permute-done.1 = bf16[512,768]{1,0:T(8,128)(2,1)S(1)} collective-permute-done((bf16[512,768]{1,0:T(8,128)(2,1)S(1)}, bf16[512,768]{1,0:T(8,128)(2,1)S(1)}, u32[]{:S(2)}, u32[]{:S(2)}) %collective-permute-start.1) | collective-permute-done | bytes 786464 | tf_op jit(solution)/shard_map/while/body/eval_jaxpr/ppermute | solution.py:18
  1271.5 155.6 %collective-permute-done.1 = bf16[512,768]{1,0:T(8,128)(2,1)S(1)} collective-permute-done((bf16[512,768]{1,0:T(8,128)(2,1)S(1)}, bf16[512,768]{1,0:T(8,128)(2,1)S(1)}, u32[]{:S(2)}, u32[]{:S(2)}) %collective-permute-start.1) | collective-permute-done | bytes 786464 | tf_op jit(solution)/shard_map/while/body/eval_jaxpr/ppermute | solution.py:18
  1427.0 46.1 %conditional.8 = (bf16[512,768]{1,0:T(8,128)(2,1)S(1)}) conditional(s32[]{:T(128)} %convert_element_type.394, () %tuple.188, (pred[]{:T(512)}, s32[]{:T(128)}, bf16[2,512,768]{2,1,0:T(8,128)(2,1)}, bf16[512,768]{1,0:T(8,128)(2,1)S(1)}, bf16[768,2304]{1,0:T(8,128)(2,1)}, /*index=5*/f32[4,768]{1,0:T(4,128)S(1)}, s32[2,512]{1,0:T(2,128)S(1)}, ...), branch_computations={%region_29.29_spmd, %region_30.36_spmd} | conditional | flops 8190166528 | bytes 109329184 | solution.py:219
  1451.7 20.8 %fusion.224 = (f32[512]{0:T(512)S(1)}, f32[512,768]{1,0:T(8,128)S(1)}) fusion(f32[768]{0:T(1024)S(1)} %get-tuple-element.1711, bf16[3072,768]{1,0:T(8,128)(2,1)} %get-tuple-element.1394, bf16[768,3072]{1,0:T(8,128)(2,1)} %get-tuple-element.1392, f32[3072]{0:T(1024)S(1)} %bitcast.238, f32[512,768]{1,0:T(8,128)S(1)} %get-tuple-element.1842, ...), kind=kOutput, calls=%fused_computation.358 | convolution fusion | flops 4941151744 | bytes 12610560 | tf_op jit(solution)/shard_map/while/body/eval_jaxpr/cond/branch_1_fun/dot_general | solution.py:93
  1494.1 46.1 %conditional.8 = (bf16[512,768]{1,0:T(8,128)(2,1)S(1)}) conditional(s32[]{:T(128)} %convert_element_type.394, () %tuple.188, (pred[]{:T(512)}, s32[]{:T(128)}, bf16[2,512,768]{2,1,0:T(8,128)(2,1)}, bf16[512,768]{1,0:T(8,128)(2,1)S(1)}, bf16[768,2304]{1,0:T(8,128)(2,1)}, /*index=5*/f32[4,768]{1,0:T(4,128)S(1)}, s32[2,512]{1,0:T(2,128)S(1)}, ...), branch_computations={%region_29.29_spmd, %region_30.36_spmd} | conditional | flops 8190166528 | bytes 109329184 | solution.py:219
  1518.7 20.8 %fusion.224 = (f32[512]{0:T(512)S(1)}, f32[512,768]{1,0:T(8,128)S(1)}) fusion(f32[768]{0:T(1024)S(1)} %get-tuple-element.1711, bf16[3072,768]{1,0:T(8,128)(2,1)} %get-tuple-element.1394, bf16[768,3072]{1,0:T(8,128)(2,1)} %get-tuple-element.1392, f32[3072]{0:T(1024)S(1)} %bitcast.238, f32[512,768]{1,0:T(8,128)S(1)} %get-tuple-element.1842, ...), kind=kOutput, calls=%fused_computation.358 | convolution fusion | flops 4941151744 | bytes 12610560 | tf_op jit(solution)/shard_map/while/body/eval_jaxpr/cond/branch_1_fun/dot_general | solution.py:93
  (489 shorter events, 582.8 us)
Async XLA Ops:
  7.2 42.8 %all-gather.9.cloned.1.call-start = ((), (), s32[]{:S(2)}) async-start(), calls=%async_computation | async-start | bytes 3981312 | tf_op jit(solution)/shard_map/all_gather | solution.py:300
  7.9 66.3 %all-gather.11.cloned.1.call-start = ((), (), s32[]{:S(2)}) async-start(), calls=%async_computation.1 | async-start | bytes 1327104 | tf_op jit(solution)/shard_map/all_gather | solution.py:301
  8.6 117.6 %all-gather.13.cloned.1.call-start = ((), (), s32[]{:S(2)}) async-start(), calls=%async_computation.2 | async-start | bytes 5308416 | tf_op jit(solution)/shard_map/all_gather | solution.py:302
  9.4 168.9 %all-gather.15.cloned.1.call-start = ((), (), s32[]{:S(2)}) async-start(), calls=%async_computation.3 | async-start | bytes 5308416 | tf_op jit(solution)/shard_map/all_gather | solution.py:303
  58.3 122.6 %copy-start.16 = (f32[1,4,768]{2,1,0:T(4,128)S(1)}, f32[1,4,768]{2,1,0:T(4,128)}, u32[]{:S(2)}) copy-start(f32[1,4,768]{2,1,0:T(4,128)} %param.36) | copy-start | bytes 36868
  180.9 381.2 %copy-start.17 = (f32[2,8,768]{2,1,0:T(8,128)S(1)}, f32[2,8,768]{2,1,0:T(8,128)}, u32[]{:S(2)}) copy-start(f32[2,8,768]{2,1,0:T(8,128)} %custom-call) | copy-start | bytes 147460
  202.5 21.6 %collective-permute-start = (bf16[512,768]{1,0:T(8,128)(2,1)S(1)}, bf16[512,768]{1,0:T(8,128)(2,1)S(1)}, u32[]{:S(2)}, u32[]{:S(2)}) collective-permute-start(bf16[512,768]{1,0:T(8,128)(2,1)S(1)} %get-tuple-element.2372), channel_id=1, source_target_pairs={{0,8},{8,16},{16,24},{1,9},{9,17},{17,25},{2,10},{10,18},{18,26},{... | collective-permute-start | bytes 2359304 | tf_op jit(solution)/shard_map/while/body/eval_jaxpr/ppermute | solution.py:18
  227.9 20.8 %collective-permute-start = (bf16[512,768]{1,0:T(8,128)(2,1)S(1)}, bf16[512,768]{1,0:T(8,128)(2,1)S(1)}, u32[]{:S(2)}, u32[]{:S(2)}) collective-permute-start(bf16[512,768]{1,0:T(8,128)(2,1)S(1)} %get-tuple-element.2372), channel_id=1, source_target_pairs={{0,8},{8,16},{16,24},{1,9},{9,17},{17,25},{2,10},{10,18},{18,26},{... | collective-permute-start | bytes 2359304 | tf_op jit(solution)/shard_map/while/body/eval_jaxpr/ppermute | solution.py:18
  252.4 163.8 %collective-permute-start = (bf16[512,768]{1,0:T(8,128)(2,1)S(1)}, bf16[512,768]{1,0:T(8,128)(2,1)S(1)}, u32[]{:S(2)}, u32[]{:S(2)}) collective-permute-start(bf16[512,768]{1,0:T(8,128)(2,1)S(1)} %get-tuple-element.2372), channel_id=1, source_target_pairs={{0,8},{8,16},{16,24},{1,9},{9,17},{17,25},{2,10},{10,18},{18,26},{... | collective-permute-start | bytes 2359304 | tf_op jit(solution)/shard_map/while/body/eval_jaxpr/ppermute | solution.py:18
  468.7 20.5 %collective-permute-start = (bf16[512,768]{1,0:T(8,128)(2,1)S(1)}, bf16[512,768]{1,0:T(8,128)(2,1)S(1)}, u32[]{:S(2)}, u32[]{:S(2)}) collective-permute-start(bf16[512,768]{1,0:T(8,128)(2,1)S(1)} %get-tuple-element.2372), channel_id=1, source_target_pairs={{0,8},{8,16},{16,24},{1,9},{9,17},{17,25},{2,10},{10,18},{18,26},{... | collective-permute-start | bytes 2359304 | tf_op jit(solution)/shard_map/while/body/eval_jaxpr/ppermute | solution.py:18
  541.8 18.9 %collective-permute-start = (bf16[512,768]{1,0:T(8,128)(2,1)S(1)}, bf16[512,768]{1,0:T(8,128)(2,1)S(1)}, u32[]{:S(2)}, u32[]{:S(2)}) collective-permute-start(bf16[512,768]{1,0:T(8,128)(2,1)S(1)} %get-tuple-element.2372), channel_id=1, source_target_pairs={{0,8},{8,16},{16,24},{1,9},{9,17},{17,25},{2,10},{10,18},{18,26},{... | collective-permute-start | bytes 2359304 | tf_op jit(solution)/shard_map/while/body/eval_jaxpr/ppermute | solution.py:18
  591.7 26.6 %copy-start = (f32[512,768]{1,0:T(8,128)}, f32[512,768]{1,0:T(8,128)S(1)}, u32[]{:S(2)}) copy-start(f32[512,768]{1,0:T(8,128)S(1)} %get-tuple-element.1852) | copy-start | bytes 4718596 | tf_op jit(solution)/shard_map/while/body/eval_jaxpr/cond
  669.6 15.5 collective-permute-start.2
  712.5 18.4 %slice-start.5 = ((s8[4718592]{0:T(1024)(128)(4,1)}), s8[4194304]{0:T(1024)(128)(4,1)S(1)}, s32[]{:S(2)}) async-start(s8[4718592]{0:T(1024)(128)(4,1)} %bitcast.231), calls=%async_computation.9 | async-start | bytes 8388608 | tf_op jit(solution)/shard_map/while/body/eval_jaxpr/cond
  714.7 26.8 %copy-start = (f32[512,768]{1,0:T(8,128)}, f32[512,768]{1,0:T(8,128)S(1)}, u32[]{:S(2)}) copy-start(f32[512,768]{1,0:T(8,128)S(1)} %get-tuple-element.1852) | copy-start | bytes 4718596 | tf_op jit(solution)/shard_map/while/body/eval_jaxpr/cond
  792.7 17.3 %collective-permute-start.2 = (bf16[512,768]{1,0:T(8,128)(2,1)}, bf16[512,768]{1,0:T(8,128)(2,1)S(1)}, u32[]{:S(2)}, u32[]{:S(2)}) collective-permute-start(bf16[512,768]{1,0:T(8,128)(2,1)} %get-tuple-element.2183), channel_id=1, source_target_pairs={{8,0},{16,8},{24,16},{9,1},{17,9},{25,17},{10,2},{18,10},{26,18},{... | collective-permute-start | bytes 2359304 | tf_op jit(solution)/shard_map/while/body/eval_jaxpr/ppermute | solution.py:18
  818.8 115.5 %collective-permute-start.2 = (bf16[512,768]{1,0:T(8,128)(2,1)}, bf16[512,768]{1,0:T(8,128)(2,1)S(1)}, u32[]{:S(2)}, u32[]{:S(2)}) collective-permute-start(bf16[512,768]{1,0:T(8,128)(2,1)} %get-tuple-element.2183), channel_id=1, source_target_pairs={{8,0},{16,8},{24,16},{9,1},{17,9},{25,17},{10,2},{18,10},{26,18},{... | collective-permute-start | bytes 2359304 | tf_op jit(solution)/shard_map/while/body/eval_jaxpr/ppermute | solution.py:18
  935.2 24.8 %collective-permute-start.2 = (bf16[512,768]{1,0:T(8,128)(2,1)}, bf16[512,768]{1,0:T(8,128)(2,1)S(1)}, u32[]{:S(2)}, u32[]{:S(2)}) collective-permute-start(bf16[512,768]{1,0:T(8,128)(2,1)} %get-tuple-element.2183), channel_id=1, source_target_pairs={{8,0},{16,8},{24,16},{9,1},{17,9},{25,17},{10,2},{18,10},{26,18},{... | collective-permute-start | bytes 2359304 | tf_op jit(solution)/shard_map/while/body/eval_jaxpr/ppermute | solution.py:18
  961.0 112.5 %collective-permute-start.2 = (bf16[512,768]{1,0:T(8,128)(2,1)}, bf16[512,768]{1,0:T(8,128)(2,1)S(1)}, u32[]{:S(2)}, u32[]{:S(2)}) collective-permute-start(bf16[512,768]{1,0:T(8,128)(2,1)} %get-tuple-element.2183), channel_id=1, source_target_pairs={{8,0},{16,8},{24,16},{9,1},{17,9},{25,17},{10,2},{18,10},{26,18},{... | collective-permute-start | bytes 2359304 | tf_op jit(solution)/shard_map/while/body/eval_jaxpr/ppermute | solution.py:18
  1118.2 32.4 %collective-permute-start.1 = (bf16[512,768]{1,0:T(8,128)(2,1)S(1)}, bf16[512,768]{1,0:T(8,128)(2,1)S(1)}, u32[]{:S(2)}, u32[]{:S(2)}) collective-permute-start(bf16[512,768]{1,0:T(8,128)(2,1)S(1)} %get-tuple-element.2373), channel_id=1, source_target_pairs={{0,8},{8,16},{16,24},{1,9},{9,17},{17,25},{2,10},{10,18},{18,26},{... | collective-permute-start | bytes 2359304 | tf_op jit(solution)/shard_map/while/body/eval_jaxpr/ppermute | solution.py:18
  1150.7 117.2 %collective-permute-start.1 = (bf16[512,768]{1,0:T(8,128)(2,1)S(1)}, bf16[512,768]{1,0:T(8,128)(2,1)S(1)}, u32[]{:S(2)}, u32[]{:S(2)}) collective-permute-start(bf16[512,768]{1,0:T(8,128)(2,1)S(1)} %get-tuple-element.2373), channel_id=1, source_target_pairs={{0,8},{8,16},{16,24},{1,9},{9,17},{17,25},{2,10},{10,18},{18,26},{... | collective-permute-start | bytes 2359304 | tf_op jit(solution)/shard_map/while/body/eval_jaxpr/ppermute | solution.py:18
  1267.9 159.1 %collective-permute-start.1 = (bf16[512,768]{1,0:T(8,128)(2,1)S(1)}, bf16[512,768]{1,0:T(8,128)(2,1)S(1)}, u32[]{:S(2)}, u32[]{:S(2)}) collective-permute-start(bf16[512,768]{1,0:T(8,128)(2,1)S(1)} %get-tuple-element.2373), channel_id=1, source_target_pairs={{0,8},{8,16},{16,24},{1,9},{9,17},{17,25},{2,10},{10,18},{18,26},{... | collective-permute-start | bytes 2359304 | tf_op jit(solution)/shard_map/while/body/eval_jaxpr/ppermute | solution.py:18
  1473.2 20.9 %collective-permute-start.1 = (bf16[512,768]{1,0:T(8,128)(2,1)S(1)}, bf16[512,768]{1,0:T(8,128)(2,1)S(1)}, u32[]{:S(2)}, u32[]{:S(2)}) collective-permute-start(bf16[512,768]{1,0:T(8,128)(2,1)S(1)} %get-tuple-element.2373), channel_id=1, source_target_pairs={{0,8},{8,16},{16,24},{1,9},{9,17},{17,25},{2,10},{10,18},{18,26},{... | collective-permute-start | bytes 2359304 | tf_op jit(solution)/shard_map/while/body/eval_jaxpr/ppermute | solution.py:18
  1540.2 19.4 %collective-permute-start.1 = (bf16[512,768]{1,0:T(8,128)(2,1)S(1)}, bf16[512,768]{1,0:T(8,128)(2,1)S(1)}, u32[]{:S(2)}, u32[]{:S(2)}) collective-permute-start(bf16[512,768]{1,0:T(8,128)(2,1)S(1)} %get-tuple-element.2373), channel_id=1, source_target_pairs={{0,8},{8,16},{16,24},{1,9},{9,17},{17,25},{2,10},{10,18},{18,26},{... | collective-permute-start | bytes 2359304 | tf_op jit(solution)/shard_map/while/body/eval_jaxpr/ppermute | solution.py:18
  (94 other events, 462.1 us)
Sparse Core Ops, SparseCore 0:
  9.6 40.3 all-gather.8
  51.6 22.4 all-gather.10
  75.8 50.3 all-gather.12
  127.7 50.5 all-gather.14
where the time goes:
time: 1570 us
  waiting for transfers between devices  763 us (49%)
  matrix products  331 us (21%)
  starting transfers between devices  237 us (15%)
  local copies, waits for them, and re-layouts  79.7 us (5%)
  other arithmetic  69.2 us (4%)
  loops' own time  46.4 us (3%)
  blocking collectives  25.8 us (2%)
    ppermute x15, waiting for transfers between devices, passed_along(): return lax.ppermute(shard, axis, pairs)  607 us
    ppermute x15, starting transfers between devices, passed_along(): return lax.ppermute(shard, axis, pairs)  237 us
    dot_general x6, matrix products, layer_forward(): jnp.dot(activated, w_down, preferred_element_type=jnp.float32)  94.5 us
    all_gather x1, waiting for transfers between devices, body(): lax.all_gather(feedforward_in_weight[0], 'dp', axis=0, tiled=True)  52.1 us
    all_gather x1, waiting for transfers between devices, body(): lax.all_gather(feedforward_out_weight[0], 'dp', axis=0, tiled=True)  52 us
    sub x6, matrix products, softmax_rows(): weights = jnp.exp(scores - top)  46 us
    all_gather x1, waiting for transfers between devices, body(): lax.all_gather(attention_in_weight[0], 'dp', axis=0, tiled=True)  37.7 us
    dot_general x6, matrix products, layer_forward(): jnp.einsum('hqk,khd->qhd', shares_full.astype(jnp.bfloat16), split_heads(...  35.9 us
  transfers between devices with their start and end apart: 19, of which 19 were waited for; matrix products, arithmetic and copies ran while one was open for 3% of the time, Pallas kernels for 0%

commit v1 on v0

v1 whole, which is shorter than its diff:
```python
import functools

import jax
import jax.numpy as jnp
import numpy as np
from jax import lax
from jax.experimental import pallas as pl
from jax.experimental.pallas import tpu as pltpu
from jax.sharding import PartitionSpec as P

HEADS = 12
norm_eps = 1e-05
masked_score = -1e30
BF = jnp.bfloat16
F32 = jnp.float32
AXES = ("section", "dp")
SHARDS = 8
RING = (0, 1, 3, 2)
PARAM_ROWS = 32
VMEM_BYTES = 60 << 20
PLACES = 9
PARITY, STAGE, OWN_SHARD = 8, 9, 10
RATE_FIRST, RATE_SECOND = 12, 13


def dot(left, right, left_dim=1, right_dim=0):
    return lax.dot_general(
        left, right, (((left_dim,), (right_dim,)), ((), ())), preferred_element_type=F32
    )


def centre_and_scale(value):
    centered = value - jnp.mean(value, axis=-1, keepdims=True)
    spread = jnp.mean(centered * centered, axis=-1, keepdims=True)
    rate = lax.rsqrt(spread + norm_eps)
    return centered * rate, rate


def norm_backward(normal, rate, gain, cotangent):
    q = gain * cotangent
    along = jnp.mean(q * normal, axis=-1, keepdims=True)
    return (q - jnp.mean(q, axis=-1, keepdims=True) - normal * along) * rate


def pack_kernel(
    scal, w_in, w_out, w_up, w_down, down_t, up, biases, inner_bias, gains, shifts, part_a, part_b, mine, rows
):
    depth, width = w_out.shape
    rank = up.shape[1]
    mine[0:4, :] = biases[...]
    for block in range(4):
        mine[4 + block : 5 + block, :] = inner_bias[:, block * width : (block + 1) * width]
    mine[8:10, :] = gains[...]
    mine[10:12, :] = shifts[...]
    down_t32 = down_t[...].astype(F32)
    mine[12:28, :] = down_t32
    mine[28:32, :] = jnp.zeros((4, width), F32)
    rows[:, 0 : 2 * rank] = down_t32.T
    a = rows[pl.ds(pl.multiple_of(scal[OWN_SHARD] * depth, 8), depth), 0 : 2 * rank]
    for block in range(3):
        piece = w_in[:, block * width : (block + 1) * width]
        if block != 1:
            side = block // 2
            extra = a[:, side * rank : side * rank + 1] * up[side, 0:1, :]
            for i in range(1, rank):
                extra = extra + a[:, side * rank + i : side * rank + i + 1] * up[side, i : i + 1, :]
            piece = (piece.astype(F32) + 2.0 * extra).astype(BF)
        part_a[block * depth : (block + 1) * depth, :] = piece
    part_a[3 * depth : 4 * depth, :] = w_out[...]
    for block in range(4):
        piece = w_up[:, block * width : (block + 1) * width]
        if block < 2:
            part_a[(4 + block) * depth : (5 + block) * depth, :] = piece
        else:
            part_b[(block - 2) * depth : (block - 1) * depth, :] = piece
    part_b[2 * depth : 6 * depth, :] = w_down[...]


def pack(scal, w_in, w_out, w_up, w_down, down_t, up, biases, inner_bias, gains, shifts):
    depth, width = w_out.shape
    shape = jax.ShapeDtypeStruct
    part = shape((6 * depth, width), BF)
    smem = pl.BlockSpec(memory_space=pltpu.SMEM)
    vmem = pl.BlockSpec(memory_space=pltpu.VMEM)
    return pl.pallas_call(
        pack_kernel,
        out_shape=(part, part, shape((PARAM_ROWS, width), F32)),
        in_specs=[smem] + [vmem] * 10,
        out_specs=(vmem, vmem, vmem),
        scratch_shapes=[pltpu.VMEM((width, 128), F32)],
        compiler_params=pltpu.CompilerParams(vmem_limit_bytes=VMEM_BYTES),
        name="pack",
    )(scal, w_in, w_out, w_up, w_down, down_t, up, biases, inner_bias, gains, shifts)


def piece_of(pieces, parity, l, step, side, half):
    if step < 3:
        base = 0 if parity == l else 12
        return pieces[base + (step * 2 + side) * 2 + half]
    if l == 0:
        return pieces[24 + (0 if half == parity else 2) + side]
    return pieces[28 + side * 2 + half]


def block_view(w, l, place):
    width = w.shape[2]
    return w.at[l, pl.ds(place * width, (4 if place == 8 else 1) * width)]


def start_block(scal, pieces, w, sem, l, place):
    depth, width = w.shape[2] // 8, w.shape[2]
    half, block = (0, place) if place < 6 else (1, place - 6)
    rows = 4 * depth if place == 8 else depth
    for parity in range(2):

        @pl.when(scal[PARITY] == parity)
        def _():
            for i in range(8):
                source = piece_of(pieces, parity, l, i // 2, i % 2, half)
                at = pl.multiple_of(place * width + rows * scal[i], 16)
                pltpu.make_async_copy(
                    source.at[pl.ds(block * depth, rows)], w.at[l, pl.ds(at, rows)], sem.at[l, place]
                ).start()


def wait_block(w, sem, l, place):
    view = block_view(w, l, place)
    pltpu.make_async_copy(view, view, sem.at[l, place]).wait()


def take_params(scal, mine, theirs, prm):
    prm[scal[PARITY]] = mine[...]
    prm[1 - scal[PARITY]] = theirs[...]


def label_lanes(lens, row, length):
    places = lax.broadcasted_iota(jnp.int32, (length, 1), 0)
    label = jnp.zeros((length, 1), jnp.int32)
    end = jnp.int32(0)
    segments = lens.shape[1]
    for j in range(segments):
        end = end + lens[row, j]
        label = label + (places >= end).astype(jnp.int32)
    lane = lax.broadcasted_iota(jnp.int32, (1, 128), 1) % 64
    same = label == lane
    used = lane <= segments
    query_lanes = jnp.where(same, 1.0, 0.0).astype(BF)
    key_lanes = jnp.where(same | ~used, 0.0, masked_score).astype(BF)
    return query_lanes, key_lanes


def forward_layer(l, lens_lanes, x, w, prm, act, state, ready, after):
    length, width = x.shape[1:]
    quads = width // 256
    lane = lax.broadcasted_iota(jnp.int32, (1, 128), 1)
    value = x[l]
    for place in range(4):
        ready(place)
    after("begin")
    attended = None
    if state is not None:
        qkv, shares, mixed_out, n, gp, r = state
        rates = jnp.zeros((length, 128), F32)
    for quad in range(quads):
        cols = slice(256 * quad, 256 * quad + 256)
        query = (dot(value, w[l, 0:width, cols]) + prm[l, 0:1, cols]).astype(BF)
        keys = dot(value, w[l, width : 2 * width, cols]).astype(BF)
        values = (dot(value, w[l, 2 * width : 3 * width, cols]) + prm[l, 1:2, cols]).astype(BF)
        if state is not None:
            qkv[0, :, cols] = query
            qkv[1, :, cols] = keys
            qkv[2, :, cols] = values
        query_lanes, key_lanes = lens_lanes[0], lens_lanes[1]
        joined = []
        for pair in range(2):
            lanes = slice(128 * pair, 128 * pair + 128)
            scaled = query[:, lanes] * BF(0.125)
            parts = []
            for head in range(2):
                mine = (lane < 64) == (head == 0)
                scores = dot(
                    jnp.where(mine, scaled, query_lanes), jnp.where(mine, keys[:, lanes], key_lanes), 1, 1
                )
                top = jnp.max(scores, axis=1, keepdims=True)
                weights = jnp.exp(scores - top)
                share = weights.astype(BF)
                over = 1.0 / jnp.sum(weights, axis=1, keepdims=True)
                if state is not None:
                    which = quad * 4 + pair * 2 + head
                    shares[which] = share
                    rates = jnp.where(lane == which, over, rates)
                parts.append(dot(share, values[:, lanes]) * over)
            joined.append(jnp.where(lane < 64, parts[0], parts[1]).astype(BF))
        mixed = jnp.concatenate(joined, axis=1)
        if state is not None:
            mixed_out[:, cols] = mixed
        term = dot(mixed, w[l, pl.ds(3 * width + 256 * quad, 256), :])
        attended = term if attended is None else attended + term
        after(quad)
    after("attended")
    summed = value.astype(F32) + (attended + prm[l, 2:3, :])
    normal, rate_first = centre_and_scale(summed)
    first = (normal * prm[l, 8:9, :] + prm[l, 10:11, :]).astype(BF)
    if state is not None:
        n[0] = normal.astype(BF)
    for block in range(4):
        ready(4 + block)
        inner = dot(first, w[l, pl.ds((4 + block) * width, width), :]) + prm[l, 4 + block : 5 + block, :]
        below = 0.5 + 0.5 * lax.erf(inner * (2**-0.5))
        act[block] = (inner * below).astype(BF)
        if state is not None:
            bell = jnp.exp(-0.5 * inner * inner) * 0.3989422804014327
            gp[block] = (below + inner * bell).astype(BF)
        after(("inner", block))
    ready(8)
    branch = None
    for block in range(4):
        term = dot(act[block], w[l, pl.ds((8 + block) * width, width), :])
        branch = term if branch is None else branch + term
    closing = first.astype(F32) + (branch + prm[l, 3:4, :])
    normal, rate_second = centre_and_scale(closing)
    if state is not None:
        n[1] = normal.astype(BF)
        rates = jnp.where(lane == RATE_FIRST, rate_first, rates)
        r[...] = jnp.where(lane == RATE_SECOND, rate_second, rates)
    x[l + 1] = (normal * prm[l, 9:10, :] + prm[l, 11:12, :]).astype(BF)
    after("end")


def backward_layer(l, c_in, c_out, x, w, prm, d_qkv, d_up, state, ready, have, spent, after):
    qkv, shares, mixed, n, gp, r = state
    length, width = x.shape[1:]
    quads = width // 256
    lane = lax.broadcasted_iota(jnp.int32, (1, 128), 1)
    for part in ("n", "r", "gp"):
        have(part)
    ready(8)
    rates = r[...]
    rate_first = rates[:, RATE_FIRST : RATE_FIRST + 1]
    rate_second = rates[:, RATE_SECOND : RATE_SECOND + 1]
    d_closing = norm_backward(n[1].astype(F32), rate_second, prm[l, 9:10, :], c_in[...].astype(F32))
    d_branch = d_closing.astype(BF)
    total = d_closing
    for block in range(4):
        ready(4 + block)
        d_active = dot(d_branch, w[l, pl.ds((8 + block) * width, width), :], 1, 1)
        d_inner = (d_active * gp[block].astype(F32)).astype(BF)
        total = total + dot(d_inner, w[l, pl.ds((4 + block) * width, width), :], 1, 1)
        after(("inner", block))
    spent("gp")
    d_summed = norm_backward(n[0].astype(F32), rate_first, prm[l, 8:9, :], total)
    spent("n")
    ready(3)
    d_mixed = dot(d_summed.astype(BF), w[l, 3 * width : 4 * width, :], 1, 1).astype(BF)
    have("mixed")
    have("qkv")
    for quad in range(quads):
        have(quad)
        for pair in range(2):
            lanes = slice(256 * quad + 128 * pair, 256 * quad + 128 * pair + 128)
            query, keys, values = qkv[0, :, lanes], qkv[1, :, lanes], qkv[2, :, lanes]
            out_rows = d_mixed[:, lanes].astype(F32)
            along = out_rows * mixed[:, lanes].astype(F32)
            query_t = query.T
            d_query, d_keys, d_values = [], [], []
            for head in range(2):
                mine = (lane < 64) == (head == 0)
                which = quad * 4 + pair * 2 + head
                over = rates[:, which : which + 1]
                share = shares[which]
                scaled = jnp.where(mine, out_rows * over, 0.0).astype(BF)
                row_sum = jnp.sum(jnp.where(mine, along, 0.0), axis=1, keepdims=True) * over
                d_score = (share.astype(F32) * (dot(scaled, values, 1, 1) - row_sum)).astype(BF)
                rows = slice(64 * head, 64 * head + 64)
                d_query.append(dot(d_score, keys))
                d_keys.append(dot(query_t[rows], d_score))
                d_values.append(dot(scaled.T[rows], share))
            d_qkv[0, :, lanes] = (jnp.where(lane < 64, d_query[0], d_query[1]) * 0.125).astype(BF)
            d_qkv[1, :, lanes] = (jnp.concatenate(d_keys, axis=0) * 0.125).astype(BF).T
            d_qkv[2, :, lanes] = jnp.concatenate(d_values, axis=0).astype(BF).T
        spent(quad)
        after(quad)
    for part in ("r", "mixed", "qkv"):
        spent(part)
    have("x")
    down = dot(x[l], prm[l, 12:28, :].astype(BF), 1, 1).astype(BF)
    rank = down.shape[1] // 2
    d_up[l, 0:rank, :] = 2.0 * dot(down, d_qkv[0], 0, 0)[0:rank]
    d_up[l, rank : 2 * rank, :] = 2.0 * dot(down, d_qkv[2], 0, 0)[rank:]
    total = d_summed
    for kind in range(3):
        ready(kind)
        total = total + dot(d_qkv[kind], w[l, kind * width : (kind + 1) * width, :], 1, 1)
    c_out[...] = total.astype(BF)


def state_shapes(length, width):
    return [
        ((3, length, width), BF),
        ((HEADS, length, length), BF),
        ((length, width), BF),
        ((2, length, width), BF),
        ((4, length, width), BF),
        ((length, 128), F32),
    ]


def state_copy(state, kept, sem, l, part, load):
    if isinstance(part, int):
        inside, outside = state[1].at[pl.ds(4 * part, 4)], kept[1].at[l, pl.ds(4 * part, 4)]
        which = 5 + part
    else:
        i = {"qkv": 0, "mixed": 2, "n": 3, "gp": 4, "r": 5}[part]
        inside, outside = state[i], kept[i].at[l]
        which = {0: 0, 2: 1, 3: 2, 4: 3, 5: 4}[i]
    ends = (outside, inside) if load else (inside, outside)
    return pltpu.make_async_copy(*ends, sem.at[which])


EARLY_PARTS = ("qkv", "mixed", 0, 1, 2)
LATE_PARTS = ("n", "gp", "r")


def save_calls(state, kept, sem, l):
    def after(point):
        if point == "begin":

            @pl.when(l > 0)
            def _():
                for part in EARLY_PARTS:
                    state_copy(state, kept, sem, 0, part, False).wait()

        if point == "attended":

            @pl.when(l > 0)
            def _():
                for part in LATE_PARTS:
                    state_copy(state, kept, sem, 0, part, False).wait()

    return after


def first_kernel(scal, lens, source, mine, theirs, *refs):
    pieces, refs = refs[:32], refs[32:]
    w_all, out_first, out_second = refs[:3]
    kept, refs = refs[3:9], refs[9:]
    x, w, prm, lanes, act, wsem, osem, xsem, hsem, ssem = refs[:10]
    state = refs[10:]
    parity, stage = scal[PARITY], scal[STAGE]

    def out_copy(l, place):
        return pltpu.make_async_copy(block_view(w, l, place), block_view(w_all, l, place), osem.at[l, place])

    for place in range(4):
        start_block(scal, pieces, w, wsem, 0, place)

    @pl.when(stage != 0)
    def _():
        for l in range(2):
            for place in range(PLACES):
                if l or place > 3:
                    start_block(scal, pieces, w, wsem, l, place)
        for l in range(2):
            for place in range(PLACES):
                wait_block(w, wsem, l, place)
                out_copy(l, place).start()

    @pl.when(stage == 0)
    def _():
        fresh = pltpu.make_async_copy(source.at[parity], x.at[0], xsem)
        fresh.start()
        take_params(scal, mine, theirs, prm)
        query_lanes, key_lanes = label_lanes(lens, parity, x.shape[1])
        lanes[0] = query_lanes
        lanes[1] = key_lanes
        fresh.wait()

        def layer(l, carry):
            def ready(place):
                wait_block(w, wsem, l, place)
                out_copy(l, place).start()

            waits = save_calls(state, kept, ssem, l)

            def ahead(places, own):
                for i in range(2):
                    if own or i == 0:

                        @pl.when(l == i)
                        def _():
                            for place in places:
                                start_block(scal, pieces, w, wsem, i if own else 1, place)

            def after(point):
                waits(point)
                if point == 0:
                    ahead((4, 5), True)
                if point == 1:
                    ahead((6, 7), True)
                if point == 2:
                    ahead((8,), True)
                if point == "attended":
                    for part in EARLY_PARTS:
                        state_copy(state, kept, ssem, l, part, False).start()
                if isinstance(point, tuple):
                    ahead((point[1],), False)
                if point == "end":
                    for part in LATE_PARTS:
                        state_copy(state, kept, ssem, l, part, False).start()

            forward_layer(l, lanes, x, w, prm, act, state, ready, after)
            return carry

        lax.fori_loop(0, 2, layer, 0)
        outs = [
            pltpu.make_async_copy(x.at[1], out_first, hsem.at[0]),
            pltpu.make_async_copy(x.at[2], out_second, hsem.at[1]),
        ]
        for copy in outs:
            copy.start()
        for part in EARLY_PARTS + LATE_PARTS:
            state_copy(state, kept, ssem, 1, part, False).wait()
        for copy in outs:
            copy.wait()

    for l in range(2):
        for place in range(PLACES):
            out_copy(l, place).wait()


def load_weights(w_all, w, wsem, l, places):
    for place in places:
        pltpu.make_async_copy(block_view(w_all, l, place), block_view(w, l, place), wsem.at[l, place]).start()


def load_ahead(w_all, w, wsem, l, point):
    own = {"begin": (4,), 0: (5, 6), 1: (7,), 2: (8,)}.get(point, ())
    load_weights(w_all, w, wsem, l, own)
    if isinstance(point, tuple):

        @pl.when(l == 0)
        def _():
            load_weights(w_all, w, wsem, 1, (point[1],))


def middle_kernel(scal, lens, source, arrived, cotangent, early_first, early_second, mine, theirs, w_all, *refs):
    hop_up, hop_down, acts, acts_other, second, second_other, d_up = refs[:7]
    kept, refs = refs[7:13], refs[13:]
    x, w, prm, lanes, act, c, wsem, xsem, hsem, ssem = refs[:10]
    state = refs[10:]
    parity, stage = scal[PARITY], scal[STAGE]
    load_weights(w_all, w, wsem, 0, range(4))
    d_up[...] = jnp.zeros(d_up.shape, F32)
    take_params(scal, mine, theirs, prm)
    query_lanes, key_lanes = label_lanes(lens, parity, x.shape[1])
    lanes[0] = query_lanes
    lanes[1] = key_lanes

    def placed(first, last, own, other, at):
        for p in range(2):

            @pl.when(parity == p)
            def _():
                ends = (first, last) if p == 0 else (last, first)
                pltpu.make_async_copy(ends[0], own.at[p], hsem.at[at]).start()
                pltpu.make_async_copy(ends[1], other, hsem.at[at + 1]).start()

    def placed_wait(own, other, at):
        pltpu.make_async_copy(own.at[0], own.at[0], hsem.at[at]).wait()
        pltpu.make_async_copy(other, other, hsem.at[at + 1]).wait()

    def both(copies):
        for copy in copies:
            copy.start()
        for copy in copies:
            copy.wait()

    @pl.when(stage == 0)
    def _():
        both(
            [
                pltpu.make_async_copy(source.at[parity], x.at[0], xsem.at[0]),
                pltpu.make_async_copy(early_first, c.at[0], xsem.at[1]),
                pltpu.make_async_copy(early_second, c.at[1], xsem.at[2]),
            ]
        )
        placed(c.at[0], c.at[1], acts, acts_other, 0)

    @pl.when(stage != 0)
    def _():
        both(
            [
                pltpu.make_async_copy(arrived, x.at[0], xsem.at[0]),
                pltpu.make_async_copy(cotangent.at[parity], c.at[0], xsem.at[1]),
            ]
        )

    def layer(l, carry):
        def ready(place):
            wait_block(w, wsem, l, place)

        waits = save_calls(state, kept, ssem, l)

        def after(point):
            waits(point)
            load_ahead(w_all, w, wsem, l, point)
            if point in ("attended", "end"):

                @pl.when(l == 0)
                def _():
                    for part in EARLY_PARTS if point == "attended" else LATE_PARTS:
                        state_copy(state, kept, ssem, 0, part, False).start()

        forward_layer(l, lanes, x, w, prm, act, state, ready, after)
        return carry

    lax.fori_loop(0, 2, layer, 0)

    @pl.when(stage == 0)
    def _():
        up = pltpu.make_async_copy(x.at[2], hop_up, xsem.at[0])
        up.start()
        placed(x.at[1], x.at[2], second, second_other, 2)
        up.wait()

    @pl.when(stage != 0)
    def _():
        placed(x.at[1], x.at[2], acts, acts_other, 0)

        def gradient(i, carry):
            l = 1 - i

            def have(part):
                if part != "x":

                    @pl.when(i > 0)
                    def _():
                        state_copy(state, kept, ssem, 0, part, True).wait()

            def spent(part):
                @pl.when(i == 0)
                def _():
                    state_copy(state, kept, ssem, 0, part, True).start()

            backward_layer(
                l, c.at[i], c.at[1 - i], x, w, prm, act, d_up, state, lambda place: None, have, spent, lambda point: None
            )
            return carry

        lax.fori_loop(0, 2, gradient, 0)
        down = pltpu.make_async_copy(c.at[0], hop_down, xsem.at[0])
        down.start()
        placed(c.at[0], c.at[1], second, second_other, 2)
        down.wait()

    placed_wait(acts, acts_other, 0)
    placed_wait(second, second_other, 2)


def last_kernel(scal, lens, source, arrived_up, arrived_down, early_first, second, mine, theirs, w_all, *refs):
    kept, refs = refs[:6], refs[6:]
    joined, grads, other, d_up = refs[:4]
    x, w, prm, lanes, act, c, wsem, xsem, hsem, ssem = refs[4:14]
    state = refs[14:]
    parity, stage = scal[PARITY], scal[STAGE]
    take_params(scal, mine, theirs, prm)
    d_up[...] = jnp.zeros(d_up.shape, F32)

    def carry_in(room):
        return pltpu.make_async_copy(second.at[parity], room, hsem.at[3])

    def carry_out(room, earlier):
        return pltpu.make_async_copy(room, earlier.at[parity], hsem.at[2])

    def finish(first, last, own):
        for p in range(2):

            @pl.when(parity == p)
            def _():
                ends = (first, last) if p == 0 else (last, first)
                copies = [
                    pltpu.make_async_copy(ends[1], other, hsem.at[1]),
                    pltpu.make_async_copy(ends[0], own.at[p], hsem.at[0]),
                ]
                for copy in copies:
                    copy.start()
                for copy in copies:
                    copy.wait()

    @pl.when(stage == 0)
    def _():
        def load(l, part):
            return state_copy(state, kept, ssem, l, part, True)

        cot = pltpu.make_async_copy(arrived_down, c.at[0], xsem.at[0])
        start_x = pltpu.make_async_copy(source.at[parity], x.at[0], xsem.at[1])
        middle_x = pltpu.make_async_copy(early_first, x.at[1], xsem.at[2])
        cot.start()
        for part in ("n", "r"):
            load(1, part).start()
        load_weights(w_all, w, wsem, 1, (8,))
        load(1, "gp").start()
        load_weights(w_all, w, wsem, 1, (4, 5))
        cot.wait()

        def gradient(i, carry):
            l = 1 - i

            def have(part):
                if part != "x":
                    load(0, part).wait()
                    return

                @pl.when(i == 0)
                def _():
                    start_x.wait()
                    middle_x.wait()

            def spent(part):
                @pl.when(i == 0)
                def _():
                    load(0, part).start()

            def ready(place):
                wait_block(w, wsem, l, place)

            def after(point):
                key = point[1] if isinstance(point, tuple) else point + 4
                load_weights(w_all, w, wsem, l, ((6,), (7,), (3,), (), (0,), (1, 2), ())[key])

                @pl.when(i == 0)
                def _():
                    for part in (("mixed",), ("qkv",), (0,), (1,), (2,), (), ())[key]:
                        load(1, part).start()
                    if key == 4:
                        carry_in(x.at[2]).start()
                        start_x.start()
                        middle_x.start()
                    if key == 5:
                        load_weights(w_all, w, wsem, 0, (8,))
                        carry_in(x.at[2]).wait()
                        carry_out(x.at[2], joined).start()
                    if key == 6:
                        load_weights(w_all, w, wsem, 0, (4, 5))

            backward_layer(l, c.at[i], c.at[1 - i], x, w, prm, act, d_up, state, ready, have, spent, after)
            return carry

        lax.fori_loop(0, 2, gradient, 0)
        finish(c.at[0], c.at[1], grads)
        carry_out(x.at[2], joined).wait()

    @pl.when(stage != 0)
    def _():
        load_weights(w_all, w, wsem, 0, range(4))
        query_lanes, key_lanes = label_lanes(lens, parity, x.shape[1])
        lanes[0] = query_lanes
        lanes[1] = key_lanes
        copy = pltpu.make_async_copy(arrived_up, x.at[0], xsem.at[0])
        copy.start()
        copy.wait()
        carry_in(c.at[0]).start()
        carry_in(c.at[0]).wait()
        carry_out(c.at[0], grads).start()

        def layer(l, carry):
            forward_layer(
                l,
                lanes,
                x,
                w,
                prm,
                act,
                None,
                lambda place: wait_block(w, wsem, l, place),
                lambda point: load_ahead(w_all, w, wsem, l, point),
            )
            return carry

        lax.fori_loop(0, 2, layer, 0)
        finish(x.at[1], x.at[2], joined)
        carry_out(c.at[0], grads).wait()


def common_scratch(length, width, rows, extra):
    return (
        [
            pltpu.VMEM((3, length, width), BF),
            pltpu.VMEM((2, 12 * width, width), BF),
            pltpu.VMEM((2, PARAM_ROWS, width), F32),
            pltpu.VMEM((2, length, 128), BF),
            pltpu.VMEM((4, length, width), BF),
        ]
        + extra
        + [
            pltpu.SemaphoreType.DMA((3,)),
            pltpu.SemaphoreType.DMA((4,)),
            pltpu.SemaphoreType.DMA((8,)),
        ]
        + [pltpu.VMEM(dims, kind) for dims, kind in state_shapes(length, width)]
    )


def layers_cost(length, width, forwards, backwards):
    dense = 2 * length * width * width * 12
    heads = 2 * length * length * width
    return pl.CostEstimate(
        flops=2 * (forwards * (dense + 2 * heads) + backwards * (dense + 5 * heads)),
        bytes_accessed=2 * 12 * width * width * 2,
        transcendentals=0,
    )


def run_first(scal, lens, source, mine, theirs, pieces):
    _, length, width = source.shape
    shape = jax.ShapeDtypeStruct
    anywhere = pl.BlockSpec(memory_space=pl.ANY)
    smem = pl.BlockSpec(memory_space=pltpu.SMEM)
    vmem = pl.BlockSpec(memory_space=pltpu.VMEM)
    row = shape((length, width), BF)
    outs = [shape((2, 12 * width, width), BF), row, row]
    outs += [shape((2,) + dims, kind) for dims, kind in state_shapes(length, width)]
    scratch = common_scratch(
        length, width, 2, [pltpu.SemaphoreType.DMA((2, PLACES)), pltpu.SemaphoreType.DMA((2, PLACES))]
    )
    scratch[7] = pltpu.SemaphoreType.DMA
    return pl.pallas_call(
        first_kernel,
        out_shape=outs,
        in_specs=[smem, smem, anywhere, vmem, vmem] + [anywhere] * 32,
        out_specs=[anywhere] * len(outs),
        scratch_shapes=scratch,
        compiler_params=pltpu.CompilerParams(vmem_limit_bytes=VMEM_BYTES),
        cost_estimate=layers_cost(length, width, 1, 0),
        name="first",
    )(scal, lens, source, mine, theirs, *pieces)


def run_middle(scal, lens, source, arrived, cotangent, early_first, early_second, mine, theirs, w_all):
    _, length, width = source.shape
    shape = jax.ShapeDtypeStruct
    anywhere = pl.BlockSpec(memory_space=pl.ANY)
    smem = pl.BlockSpec(memory_space=pltpu.SMEM)
    vmem = pl.BlockSpec(memory_space=pltpu.VMEM)
    row, rows = shape((length, width), BF), shape((2, length, width), BF)
    outs = [row, row, rows, row, rows, row, shape((2, 16, width), F32)]
    outs += [shape((1,) + dims, kind) for dims, kind in state_shapes(length, width)]
    return pl.pallas_call(
        middle_kernel,
        out_shape=outs,
        in_specs=[smem, smem] + [anywhere] * 5 + [vmem, vmem, anywhere],
        out_specs=[anywhere] * 6 + [vmem] + [anywhere] * 6,
        scratch_shapes=common_scratch(
            length,
            width,
            2,
            [pltpu.VMEM((2, length, width), BF), pltpu.SemaphoreType.DMA((2, PLACES))],
        ),
        compiler_params=pltpu.CompilerParams(vmem_limit_bytes=VMEM_BYTES),
        cost_estimate=layers_cost(length, width, 1, 1),
        name="middle",
    )(scal, lens, source, arrived, cotangent, early_first, early_second, mine, theirs, w_all)


def run_last(scal, lens, source, arrived_up, arrived_down, early_first, second, mine, theirs, w_all, kept):
    _, length, width = source.shape
    shape = jax.ShapeDtypeStruct
    anywhere = pl.BlockSpec(memory_space=pl.ANY)
    smem = pl.BlockSpec(memory_space=pltpu.SMEM)
    vmem = pl.BlockSpec(memory_space=pltpu.VMEM)
    row, rows = shape((length, width), BF), shape((2, length, width), BF)
    return pl.pallas_call(
        last_kernel,
        out_shape=[rows, rows, row, shape((2, 16, width), F32)],
        in_specs=[smem, smem] + [anywhere] * 5 + [vmem, vmem] + [anywhere] * 7,
        out_specs=[anywhere] * 3 + [vmem],
        scratch_shapes=common_scratch(
            length,
            width,
            2,
            [pltpu.VMEM((2, length, width), BF), pltpu.SemaphoreType.DMA((2, PLACES))],
        ),
        compiler_params=pltpu.CompilerParams(vmem_limit_bytes=VMEM_BYTES),
        cost_estimate=layers_cost(length, width, 0, 1),
        name="last",
    )(scal, lens, source, arrived_up, arrived_down, early_first, second, mine, theirs, w_all, *kept)


def tables(sections, copies):
    group = copies // SHARDS
    out = np.zeros((sections * copies, 12), np.int32)
    for s in range(sections):
        for d in range(copies):
            shard = d // group
            place, side = RING.index(shard // 2), shard % 2
            row = out[s * copies + d]
            for step in range(4):
                node = RING[(place - step) % 4]
                row[2 * step], row[2 * step + 1] = 2 * node + side, 2 * node + 1 - side
            row[PARITY], row[STAGE], row[OWN_SHARD] = s % 2, s // 2, shard
    return out


def body(
    inputs,
    evaluation_input,
    output_cotangent,
    packed_segment_lengths,
    attention_in_weight,
    attention_out_weight,
    feedforward_in_weight,
    feedforward_out_weight,
    adapter_down_weight,
    adapter_up_weight,
    projection_biases,
    feedforward_bias,
    layer_norm_gain,
    layer_norm_shift,
):
    sections, copies = lax.axis_size("section"), lax.axis_size("dp")
    group = copies // SHARDS
    section, place = lax.axis_index("section"), lax.axis_index("dp")
    even = section % 2 == 0
    scal = lax.dynamic_index_in_dim(
        jnp.asarray(tables(sections, copies)), section * copies + place, 0, keepdims=False
    )

    def permuted(array, move):
        pairs = []
        for s in range(sections):
            for d in range(copies):
                target = move(s, d // group)
                if target is not None:
                    pairs.append((s * copies + d, target[0] * copies + target[1] * group + d % group))
        return lax.ppermute(array, AXES, pairs)

    ring_next = {RING[i]: RING[(i + 1) % 4] for i in range(4)}
    ring_last = {RING[i]: RING[i - 1] for i in range(4)}
    along = lambda s, q: (s, ring_next[q // 2] * 2 + q % 2)
    against = lambda s, q: (s, ring_last[q // 2] * 2 + q % 2)
    other_side = lambda s, q: (s, q ^ 1)
    partner = lambda s, q: (s ^ 1, q)
    upward = lambda s, q: (s + 2, q) if s < 2 else None
    downward = lambda s, q: (s - 2, q) if s >= 2 else None

    w_in, w_out, w_up, w_down = (
        attention_in_weight[0],
        attention_out_weight[0],
        feedforward_in_weight[0],
        feedforward_out_weight[0],
    )
    if group > 1:
        groups = [[q * group + i for i in range(group)] for q in range(SHARDS)]
        w_in, w_out, w_up, w_down = (
            lax.all_gather(piece, "dp", axis=0, tiled=True, axis_index_groups=groups)
            for piece in (w_in, w_out, w_up, w_down)
        )
    part_a, part_b, mine = pack(
        scal,
        w_in,
        w_out,
        w_up,
        w_down,
        adapter_down_weight[0].T,
        adapter_up_weight[0],
        projection_biases[0],
        feedforward_bias,
        layer_norm_gain[0],
        layer_norm_shift[0],
    )

    def held_back(array, until):
        return lax.optimization_barrier((array, until))[0]

    r0 = [part_a, part_b]
    x0, r1 = [None, None], [None, None]
    for half in range(2):
        x0[half] = permuted(r0[half], partner)
        r1[half] = permuted(r0[half], along)
    x1, r2 = [None, None], [None, None]
    for half in range(2):
        x1[half] = permuted(held_back(r1[half], x0[half]), partner)
        r2[half] = permuted(r1[half], along)
    z_first = permuted(held_back(jnp.where(even, r0[0], x0[1]), r2[0]), against)
    x2, z_second = [None, None], [None, None]
    for half in range(2):
        x2[half] = permuted(held_back(r2[half], x1[half]), partner)
        second_layer = jnp.where(even, x0[half], r0[half])
        z_second[half] = permuted(held_back(second_layer, z_first if half else r2[1]), against)
    x_first = permuted(held_back(z_first, x2[0]), partner)
    theirs = permuted(held_back(mine, r1[0]), partner)

    def swapped(halves):
        return halves + [permuted(half, other_side) for half in halves]

    pieces = []
    for halves in (r0, r1, r2, x0, x1, x2, [z_first], [x_first], z_second):
        pieces += swapped(halves)

    lens = packed_segment_lengths
    w_all, early_first, early_second, *kept = run_first(scal, lens, inputs, mine, theirs, pieces)
    arrived = permuted(early_second, upward)
    hop_up, hop_down, acts, acts_other, second, second_other, d_up_late, *_ = run_middle(
        scal,
        lens,
        evaluation_input,
        arrived,
        output_cotangent,
        early_first,
        early_second,
        mine,
        theirs,
        w_all,
    )
    arrived_down = permuted(hop_down, downward)
    arrived_up = permuted(hop_up, upward)
    acts_row = permuted(acts_other, partner)
    second_row = permuted(second_other, partner)
    joined, grads, last_other, d_up_early = run_last(
        scal, lens, inputs, arrived_up, arrived_down, early_first, second, mine, theirs, w_all, kept
    )
    last_other, d_up_early, acts_row, second_row = lax.optimization_barrier(
        (last_other, d_up_early, acts_row, second_row)
    )
    last_row = permuted(last_other, partner)
    early = section < 2
    row = 1 - section % 2

    def settled(rows, arrived_row):
        return lax.dynamic_update_slice(rows, arrived_row[None], (row, 0, 0))[None]

    activations = settled(acts, acts_row)
    joined = settled(joined, jnp.where(early, second_row, last_row))
    grads = settled(grads, jnp.where(early, last_row, second_row))

    total = jnp.where(early, d_up_early, d_up_late)
    step = 1
    while step < copies:
        total = total + lax.ppermute(total, "dp", [(d, d ^ step) for d in range(copies)])
        step *= 2
    total = jnp.where(even, total[0], total[1]) + permuted(jnp.where(even, total[1], total[0]), partner)
    total = total.reshape((1, 2, total.shape[0] // 2, total.shape[1]))
    return (activations, grads, total, joined)


def solution(mesh):
    in_specs = (
        P("dp", None, None),
        P("dp", None, None),
        P("dp", None, None),
        P("dp", None),
        P("section", "dp", None),
        P("section", "dp", None),
        P("section", "dp", None),
        P("section", "dp", None),
        P("section", None, None),
        P("section", None, None, None),
        P("section", None, None),
        P("section", None),
        P("section", None, None),
        P("section", None, None),
    )
    out_specs = (
        P("section", "dp", None, None),
        P("section", "dp", None, None),
        P("section", None, None, None),
        P("section", "dp", None, None),
    )
    return jax.shard_map(body, mesh=mesh, in_specs=in_specs, out_specs=out_specs, check_vma=False)
```

time: 1570 us -> 405 us (0.26)
  the two profiles are of different devices: /device:TPU:30 before, /device:TPU:0 now
where the time goes in v1:
time: 405 us; the launch traced here: 401 us
  waiting for transfers between devices  172 us (42%)
  Pallas kernels  135 us (33%)
  starting transfers between devices  79.5 us (20%)
  local copies, waits for them, and re-layouts  8.22 us (2%)
  other arithmetic  4.17 us (1%)
    ppermute x38, waiting for transfers between devices, permuted(): return lax.ppermute(array, AXES, pairs)  164 us
    ppermute x38, starting transfers between devices, permuted(): return lax.ppermute(array, AXES, pairs)  74.1 us
    pallas_call x1, Pallas kernels, run_last(): pl.pallas_call(last_kernel, out_shape=[rows, rows, row, shape((2, 16, wid...  46.3 us
    pallas_call x1, Pallas kernels, run_first(): pl.pallas_call(first_kernel, out_shape=outs, in_specs=[smem, smem, anywhe...  44.3 us
    pallas_call x1, Pallas kernels, run_middle(): pl.pallas_call(middle_kernel, out_shape=outs, in_specs=[smem, smem] + [an...  41.1 us
  transfers between devices with their start and end apart: 41, of which 19 were waited for; matrix products, arithmetic and copies ran while one was open for 1% of the time, Pallas kernels for 12%

profile of v1, /device:TPU:0, one launch (start us, length us, event | category | flops | bytes accessed | tf_op | source)
XLA Modules:
  0.0 400.5 jit_solution(9365717637791825480)
XLA Ops:
  1.8 3.4 pack.1
  5.2 2.9 collective-permute-start.11
  12.9 16.0 %collective-permute-done.11.refs_12_ = bf16[576,768]{1,0:T(8,128)(2,1)S(1)} collective-permute-done((bf16[576,768]{1,0:T(8,128)(2,1)}, bf16[576,768]{1,0:T(8,128)(2,1)S(1)}, u32[]{:S(2)}, u32[]{:S(2)}) %collective-permute-start.11) | collective-permute-done | bytes 884768 | tf_op jit(solution)/shard_map/ppermute | solution.py:835
  28.9 3.0 collective-permute-done.refs_4_
  33.3 14.5 %collective-permute-done.12.refs_13_ = bf16[576,768]{1,0:T(8,128)(2,1)S(1)} collective-permute-done((bf16[576,768]{1,0:T(8,128)(2,1)}, bf16[576,768]{1,0:T(8,128)(2,1)S(1)}, u32[]{:S(2)}, u32[]{:S(2)}) %collective-permute-start.12) | collective-permute-done | bytes 884768 | tf_op jit(solution)/shard_map/ppermute | solution.py:835
  47.8 3.0 collective-permute-done.4.refs_5_
  51.0 15.8 %collective-permute-done.15.refs_16_ = bf16[576,768]{1,0:T(8,128)(2,1)S(1)} collective-permute-done((bf16[576,768]{1,0:T(8,128)(2,1)S(1)}, bf16[576,768]{1,0:T(8,128)(2,1)S(1)}, u32[]{:S(2)}, u32[]{:S(2)}) %collective-permute-start.15) | collective-permute-done | bytes 884768 | tf_op jit(solution)/shard_map/ppermute | solution.py:835
  73.3 13.7 %collective-permute-done.1.theirs = f32[32,768]{1,0:T(8,128)S(1)} collective-permute-done((f32[32,768]{1,0:T(8,128)}, f32[32,768]{1,0:T(8,128)S(1)}, u32[]{:S(2)}, u32[]{:S(2)}) %collective-permute-start.1) | collective-permute-done | bytes 98336 | tf_op jit(solution)/shard_map/ppermute | solution.py:835
  92.2 17.1 %collective-permute-done.19.refs_20_ = bf16[576,768]{1,0:T(8,128)(2,1)S(1)} collective-permute-done((bf16[576,768]{1,0:T(8,128)(2,1)}, bf16[576,768]{1,0:T(8,128)(2,1)S(1)}, u32[]{:S(2)}, u32[]{:S(2)}) %collective-permute-start.19) | collective-permute-done | bytes 884768 | tf_op jit(solution)/shard_map/ppermute | solution.py:835
  111.2 3.4 collective-permute-start.27
  116.6 16.9 %collective-permute-done.20.refs_21_ = bf16[576,768]{1,0:T(8,128)(2,1)S(1)} collective-permute-done((bf16[576,768]{1,0:T(8,128)(2,1)}, bf16[576,768]{1,0:T(8,128)(2,1)S(1)}, u32[]{:S(2)}, u32[]{:S(2)}) %collective-permute-start.20) | collective-permute-done | bytes 884768 | tf_op jit(solution)/shard_map/ppermute | solution.py:835
  133.5 3.4 collective-permute-start.28
  137.5 13.3 %collective-permute-done.25.refs_26_ = bf16[576,768]{1,0:T(8,128)(2,1)S(1)} collective-permute-done((bf16[576,768]{1,0:T(8,128)(2,1)S(1)}, bf16[576,768]{1,0:T(8,128)(2,1)S(1)}, u32[]{:S(2)}, u32[]{:S(2)}) %collective-permute-start.25) | collective-permute-done | bytes 884768 | tf_op jit(solution)/shard_map/ppermute | solution.py:835
  155.4 44.3 %first.1 = (bf16[2,9216,768]{2,1,0:T(8,128)(2,1)}, bf16[512,768]{1,0:T(8,128)(2,1)}, bf16[512,768]{1,0:T(8,128)(2,1)}, bf16[2,3,512,768]{3,2,1,0:T(8,128)(2,1)},...) custom-call(s32[12]{0:T(128)} %fusion.1.scal, ...), custom_call_target="tpu_custom_call" | custom-call | flops 16106127360 | bytes 28311552 | tf_op jit(solution)/shard_map/first/pallas_call | solution.py:727
  201.1 17.7 %collective-permute-done.31.arrived = bf16[512,768]{1,0:T(8,128)(2,1)S(1)} collective-permute-done((bf16[512,768]{1,0:T(8,128)(2,1)}, bf16[512,768]{1,0:T(8,128)(2,1)S(1)}, u32[]{:S(2)}, u32[]{:S(2)}) %collective-permute-start.31) | collective-permute-done | bytes 786464 | tf_op jit(solution)/shard_map/ppermute | solution.py:835
  219.7 41.1 %middle.1 = (bf16[512,768]{1,0:T(8,128)(2,1)}, bf16[512,768]{1,0:T(8,128)(2,1)}, bf16[2,512,768]{2,1,0:T(8,128)(2,1)}, bf16[512,768]{1,0:T(8,128)(2,1)}, bf16[2,...) custom-call(s32[12]{0:T(128)} %fusion.1.scal, ...), custom_call_target="tpu_custom_call" | custom-call | flops 34628173824 | bytes 28311552 | tf_op jit(solution)/shard_map/middle/pallas_call | solution.py:748
  260.8 37.8 %collective-permute-start.32 = (bf16[512,768]{1,0:T(8,128)(2,1)}, bf16[512,768]{1,0:T(8,128)(2,1)S(1)}, u32[]{:S(2)}, u32[]{:S(2)}) collective-permute-start(bf16[512,768]{1,0:T(8,128)(2,1)} %get-tuple-element.56), channel_id=1, source_target_pairs={{0,16},{1,17},{2,18},{3,19},{4,20},{5,21},{6,22},{7,23},{8,24},{9,... | collective-permute-start | bytes 2359304 | tf_op jit(solution)/shard_map/ppermute | solution.py:835
  302.0 13.6 %collective-permute-done.32.arrived_up = bf16[512,768]{1,0:T(8,128)(2,1)S(1)} collective-permute-done((bf16[512,768]{1,0:T(8,128)(2,1)}, bf16[512,768]{1,0:T(8,128)(2,1)S(1)}, u32[]{:S(2)}, u32[]{:S(2)}) %collective-permute-start.32) | collective-permute-done | bytes 786464 | tf_op jit(solution)/shard_map/ppermute | solution.py:835
  315.6 4.1 %collective-permute-done.33.arrived_down = bf16[512,768]{1,0:T(8,128)(2,1)S(1)} collective-permute-done((bf16[512,768]{1,0:T(8,128)(2,1)}, bf16[512,768]{1,0:T(8,128)(2,1)S(1)}, u32[]{:S(2)}, u32[]{:S(2)}) %collective-permute-start.33) | collective-permute-done | bytes 786464 | tf_op jit(solution)/shard_map/ppermute | solution.py:835
  320.6 46.3 %last.1 = (bf16[2,512,768]{2,1,0:T(8,128)(2,1)}, bf16[2,512,768]{2,1,0:T(8,128)(2,1)}, bf16[512,768]{1,0:T(8,128)(2,1)}, f32[2,16,768]{2,1,0:T(8,128)}) custom-call(s32[12]{0:T(128)} %fusion.1.scal, s32[2,8]{1,0:T(2,128)} %lens.5, bf16[2,512,768]{2,1,0:T(8,128)(2,1)} %source.5, bf16[512,768]{1,0:T(8,128)(2,1)} %copy-done.28, bf16[512,768]{1,0:T(8,128)(2,1)} %copy-done.29, ...), custom_call_target="tpu_custom_call" | custom-call | flops 18522046464 | bytes 28311552 | tf_op jit(solution)/shard_map/last/pallas_call | solution.py:772
  371.6 3.1 collective-permute-done.38
  374.8 2.8 collective-permute-start.39
  378.7 3.5 collective-permute-done.39
  385.2 12.1 %collective-permute-done.40 = f32[16,768]{1,0:T(8,128)S(1)} collective-permute-done((f32[16,768]{1,0:T(8,128)S(1)}, f32[16,768]{1,0:T(8,128)S(1)}, u32[]{:S(2)}, u32[]{:S(2)}) %collective-permute-start.40) | collective-permute-done | bytes 49184 | tf_op jit(solution)/shard_map/ppermute | solution.py:835
  (136 shorter events, 46.6 us)
Async XLA Ops:
  5.2 23.6 %collective-permute-start.11 = (bf16[576,768]{1,0:T(8,128)(2,1)}, bf16[576,768]{1,0:T(8,128)(2,1)S(1)}, u32[]{:S(2)}, u32[]{:S(2)}) collective-permute-start(bf16[576,768]{1,0:T(8,128)(2,1)} %get-tuple-element.41.refs_0_), channel_id=1, source_target_pairs={{0,8},{1,9},{2,10},{3,11},{4,12},{5,13},{6,14},{7,15},{8,0},{9,1},... | collective-permute-start | bytes 2654216 | tf_op jit(solution)/shard_map/ppermute | solution.py:835
  8.2 23.7 %collective-permute-start = (bf16[576,768]{1,0:T(8,128)(2,1)}, bf16[576,768]{1,0:T(8,128)(2,1)S(1)}, u32[]{:S(2)}, u32[]{:S(2)}) collective-permute-start(bf16[576,768]{1,0:T(8,128)(2,1)} %get-tuple-element.41.refs_0_), channel_id=1, source_target_pairs={{0,2},{1,3},{2,6},{3,7},{4,0},{5,1},{6,4},{7,5},{8,10},{9,11},{10,... | collective-permute-start | bytes 2654216 | tf_op jit(solution)/shard_map/ppermute | solution.py:835
  9.8 38.1 %collective-permute-start.12 = (bf16[576,768]{1,0:T(8,128)(2,1)}, bf16[576,768]{1,0:T(8,128)(2,1)S(1)}, u32[]{:S(2)}, u32[]{:S(2)}) collective-permute-start(bf16[576,768]{1,0:T(8,128)(2,1)} %get-tuple-element.43.refs_1_), channel_id=1, source_target_pairs={{0,8},{1,9},{2,10},{3,11},{4,12},{5,13},{6,14},{7,15},{8,0},{9,1},... | collective-permute-start | bytes 2654216 | tf_op jit(solution)/shard_map/ppermute | solution.py:835
  10.3 40.5 %collective-permute-start.4 = (bf16[576,768]{1,0:T(8,128)(2,1)}, bf16[576,768]{1,0:T(8,128)(2,1)S(1)}, u32[]{:S(2)}, u32[]{:S(2)}) collective-permute-start(bf16[576,768]{1,0:T(8,128)(2,1)} %get-tuple-element.43.refs_1_), channel_id=1, source_target_pairs={{0,2},{1,3},{2,6},{3,7},{4,0},{5,1},{6,4},{7,5},{8,10},{9,11},{10,... | collective-permute-start | bytes 2654216 | tf_op jit(solution)/shard_map/ppermute | solution.py:835
  31.9 34.9 %collective-permute-start.15 = (bf16[576,768]{1,0:T(8,128)(2,1)S(1)}, bf16[576,768]{1,0:T(8,128)(2,1)S(1)}, u32[]{:S(2)}, u32[]{:S(2)}) collective-permute-start(bf16[576,768]{1,0:T(8,128)(2,1)S(1)} %collective-permute-done.refs_4_), channel_id=1, source_target_pairs={{0,8},{1,9},{2,10},{3,11},{4,12},{5,13},{6,14},{7,15},{8,0},{9,1},... | collective-permute-start | bytes 2654216 | tf_op jit(solution)/shard_map/ppermute | solution.py:835
  32.1 37.8 %collective-permute-start.7 = (bf16[576,768]{1,0:T(8,128)(2,1)S(1)}, bf16[576,768]{1,0:T(8,128)(2,1)}, u32[]{:S(2)}, u32[]{:S(2)}) collective-permute-start(bf16[576,768]{1,0:T(8,128)(2,1)S(1)} %collective-permute-done.refs_4_), channel_id=1, source_target_pairs={{0,2},{1,3},{2,6},{3,7},{4,0},{5,1},{6,4},{7,5},{8,10},{9,11},{10,... | collective-permute-start | bytes 2654216 | tf_op jit(solution)/shard_map/ppermute | solution.py:835
  33.3 39.4 %collective-permute-start.2 = (bf16[576,768]{1,0:T(8,128)(2,1)}, bf16[576,768]{1,0:T(8,128)(2,1)}, u32[]{:S(2)}, u32[]{:S(2)}) collective-permute-start(bf16[576,768]{1,0:T(8,128)(2,1)} %get-tuple-element.41.refs_0_), channel_id=1, source_target_pairs={{0,1},{1,0},{2,3},{3,2},{4,5},{5,4},{6,7},{7,6},{8,9},{9,8},{10,11... | collective-permute-start | bytes 2654216 | tf_op jit(solution)/shard_map/ppermute | solution.py:835
  47.8 25.0 %collective-permute-start.3 = (bf16[576,768]{1,0:T(8,128)(2,1)}, bf16[576,768]{1,0:T(8,128)(2,1)}, u32[]{:S(2)}, u32[]{:S(2)}) collective-permute-start(bf16[576,768]{1,0:T(8,128)(2,1)} %get-tuple-element.43.refs_1_), channel_id=1, source_target_pairs={{0,1},{1,0},{2,3},{3,2},{4,5},{5,4},{6,7},{7,6},{8,9},{9,8},{10,11... | collective-permute-start | bytes 2654216 | tf_op jit(solution)/shard_map/ppermute | solution.py:835
  50.8 36.2 %collective-permute-start.16 = (bf16[576,768]{1,0:T(8,128)(2,1)S(1)}, bf16[576,768]{1,0:T(8,128)(2,1)}, u32[]{:S(2)}, u32[]{:S(2)}) collective-permute-start(bf16[576,768]{1,0:T(8,128)(2,1)S(1)} %collective-permute-done.4.refs_5_), channel_id=1, source_target_pairs={{0,8},{1,9},{2,10},{3,11},{4,12},{5,13},{6,14},{7,15},{8,0},{9,1},... | collective-permute-start | bytes 2654216 | tf_op jit(solution)/shard_map/ppermute | solution.py:835
  67.7 21.2 %collective-permute-start.8 = (bf16[576,768]{1,0:T(8,128)(2,1)S(1)}, bf16[576,768]{1,0:T(8,128)(2,1)}, u32[]{:S(2)}, u32[]{:S(2)}) collective-permute-start(bf16[576,768]{1,0:T(8,128)(2,1)S(1)} %collective-permute-done.4.refs_5_), channel_id=1, source_target_pairs={{0,2},{1,3},{2,6},{3,7},{4,0},{5,1},{6,4},{7,5},{8,10},{9,11},{10,... | collective-permute-start | bytes 2654216 | tf_op jit(solution)/shard_map/ppermute | solution.py:835
  87.0 22.3 %collective-permute-start.19 = (bf16[576,768]{1,0:T(8,128)(2,1)}, bf16[576,768]{1,0:T(8,128)(2,1)S(1)}, u32[]{:S(2)}, u32[]{:S(2)}) collective-permute-start(bf16[576,768]{1,0:T(8,128)(2,1)} %collective-permute-done.7.refs_8_), channel_id=1, source_target_pairs={{0,8},{1,9},{2,10},{3,11},{4,12},{5,13},{6,14},{7,15},{8,0},{9,1},... | collective-permute-start | bytes 2654216 | tf_op jit(solution)/shard_map/ppermute | solution.py:835
  88.8 21.8 %collective-permute-start.23 = (bf16[576,768]{1,0:T(8,128)(2,1)S(1)}, bf16[576,768]{1,0:T(8,128)(2,1)S(1)}, u32[]{:S(2)}, u32[]{:S(2)}) collective-permute-start(bf16[576,768]{1,0:T(8,128)(2,1)S(1)} %get-tuple-element.48), channel_id=1, source_target_pairs={{0,4},{1,5},{2,0},{3,1},{4,6},{5,7},{6,2},{7,3},{8,12},{9,13},{10,... | collective-permute-start | bytes 2654216 | tf_op jit(solution)/shard_map/ppermute | solution.py:835
  91.6 23.1 %collective-permute-start.17 = (bf16[576,768]{1,0:T(8,128)(2,1)S(1)}, bf16[576,768]{1,0:T(8,128)(2,1)S(1)}, u32[]{:S(2)}, u32[]{:S(2)}) collective-permute-start(bf16[576,768]{1,0:T(8,128)(2,1)S(1)} %copy-done.8), channel_id=1, source_target_pairs={{0,1},{1,0},{2,3},{3,2},{4,5},{5,4},{6,7},{7,6},{8,9},{9,8},{10,11... | collective-permute-start | bytes 2654216 | tf_op jit(solution)/shard_map/ppermute | solution.py:835
  92.1 22.5 %collective-permute-start.9 = (bf16[576,768]{1,0:T(8,128)(2,1)}, bf16[576,768]{1,0:T(8,128)(2,1)S(1)}, u32[]{:S(2)}, u32[]{:S(2)}) collective-permute-start(bf16[576,768]{1,0:T(8,128)(2,1)} %collective-permute-done.7.refs_8_), channel_id=1, source_target_pairs={{0,1},{1,0},{2,3},{3,2},{4,5},{5,4},{6,7},{7,6},{8,9},{9,8},{10,11... | collective-permute-start | bytes 2654216 | tf_op jit(solution)/shard_map/ppermute | solution.py:835
  110.7 22.8 %collective-permute-start.20 = (bf16[576,768]{1,0:T(8,128)(2,1)}, bf16[576,768]{1,0:T(8,128)(2,1)S(1)}, u32[]{:S(2)}, u32[]{:S(2)}) collective-permute-start(bf16[576,768]{1,0:T(8,128)(2,1)} %collective-permute-done.8.refs_9_), channel_id=1, source_target_pairs={{0,8},{1,9},{2,10},{3,11},{4,12},{5,13},{6,14},{7,15},{8,0},{9,1},... | collective-permute-start | bytes 2654216 | tf_op jit(solution)/shard_map/ppermute | solution.py:835
  111.2 25.6 %collective-permute-start.27 = (bf16[576,768]{1,0:T(8,128)(2,1)S(1)}, bf16[576,768]{1,0:T(8,128)(2,1)S(1)}, u32[]{:S(2)}, u32[]{:S(2)}) collective-permute-start(bf16[576,768]{1,0:T(8,128)(2,1)S(1)} %get-tuple-element.50), channel_id=1, source_target_pairs={{0,4},{1,5},{2,0},{3,1},{4,6},{5,7},{6,2},{7,3},{8,12},{9,13},{10,... | collective-permute-start | bytes 2654216 | tf_op jit(solution)/shard_map/ppermute | solution.py:835
  114.6 22.3 %collective-permute-start.10 = (bf16[576,768]{1,0:T(8,128)(2,1)}, bf16[576,768]{1,0:T(8,128)(2,1)S(1)}, u32[]{:S(2)}, u32[]{:S(2)}) collective-permute-start(bf16[576,768]{1,0:T(8,128)(2,1)} %collective-permute-done.8.refs_9_), channel_id=1, source_target_pairs={{0,1},{1,0},{2,3},{3,2},{4,5},{5,4},{6,7},{7,6},{8,9},{9,8},{10,11... | collective-permute-start | bytes 2654216 | tf_op jit(solution)/shard_map/ppermute | solution.py:835
  114.6 22.8 %collective-permute-start.21 = (bf16[576,768]{1,0:T(8,128)(2,1)S(1)}, bf16[576,768]{1,0:T(8,128)(2,1)S(1)}, u32[]{:S(2)}, u32[]{:S(2)}) collective-permute-start(bf16[576,768]{1,0:T(8,128)(2,1)S(1)} %collective-permute-done.19.refs_20_), channel_id=1, source_target_pairs={{0,1},{1,0},{2,3},{3,2},{4,5},{5,4},{6,7},{7,6},{8,9},{9,8},{10,11... | collective-permute-start | bytes 2654216 | tf_op jit(solution)/shard_map/ppermute | solution.py:835
  115.1 35.6 %collective-permute-start.25 = (bf16[576,768]{1,0:T(8,128)(2,1)S(1)}, bf16[576,768]{1,0:T(8,128)(2,1)S(1)}, u32[]{:S(2)}, u32[]{:S(2)}) collective-permute-start(bf16[576,768]{1,0:T(8,128)(2,1)S(1)} %collective-permute-done.23.refs_24_), channel_id=1, source_target_pairs={{0,8},{1,9},{2,10},{3,11},{4,12},{5,13},{6,14},{7,15},{8,0},{9,1},... | collective-permute-start | bytes 2654216 | tf_op jit(solution)/shard_map/ppermute | solution.py:835
  260.8 54.8 %collective-permute-start.32 = (bf16[512,768]{1,0:T(8,128)(2,1)}, bf16[512,768]{1,0:T(8,128)(2,1)S(1)}, u32[]{:S(2)}, u32[]{:S(2)}) collective-permute-start(bf16[512,768]{1,0:T(8,128)(2,1)} %get-tuple-element.56), channel_id=1, source_target_pairs={{0,16},{1,17},{2,18},{3,19},{4,20},{5,21},{6,22},{7,23},{8,24},{9,... | collective-permute-start | bytes 2359304 | tf_op jit(solution)/shard_map/ppermute | solution.py:835
  298.6 21.0 %collective-permute-start.33 = (bf16[512,768]{1,0:T(8,128)(2,1)}, bf16[512,768]{1,0:T(8,128)(2,1)S(1)}, u32[]{:S(2)}, u32[]{:S(2)}) collective-permute-start(bf16[512,768]{1,0:T(8,128)(2,1)} %get-tuple-element.57), channel_id=1, source_target_pairs={{16,0},{17,1},{18,2},{19,3},{20,4},{21,5},{22,6},{23,7},{24,8},{25... | collective-permute-start | bytes 2359304 | tf_op jit(solution)/shard_map/ppermute | solution.py:835
  299.9 66.9 %collective-permute-start.34 = (bf16[512,768]{1,0:T(8,128)(2,1)}, bf16[512,768]{1,0:T(8,128)(2,1)S(1)}, u32[]{:S(2)}, u32[]{:S(2)}) collective-permute-start(bf16[512,768]{1,0:T(8,128)(2,1)} %get-tuple-element.67), channel_id=1, source_target_pairs={{0,8},{1,9},{2,10},{3,11},{4,12},{5,13},{6,14},{7,15},{8,0},{9,1},... | collective-permute-start | bytes 2359304 | tf_op jit(solution)/shard_map/ppermute | solution.py:835
  301.9 65.0 %collective-permute-start.35 = (bf16[512,768]{1,0:T(8,128)(2,1)}, bf16[512,768]{1,0:T(8,128)(2,1)S(1)}, u32[]{:S(2)}, u32[]{:S(2)}) collective-permute-start(bf16[512,768]{1,0:T(8,128)(2,1)} %get-tuple-element.68), channel_id=1, source_target_pairs={{0,8},{1,9},{2,10},{3,11},{4,12},{5,13},{6,14},{7,15},{8,0},{9,1},... | collective-permute-start | bytes 2359304 | tf_op jit(solution)/shard_map/ppermute | solution.py:835
  377.6 20.4 %collective-permute-start.36 = (bf16[512,768]{1,0:T(8,128)(2,1)}, bf16[512,768]{1,0:T(8,128)(2,1)S(1)}, u32[]{:S(2)}, u32[]{:S(2)}) collective-permute-start(bf16[512,768]{1,0:T(8,128)(2,1)} %get-tuple-element.71), channel_id=1, source_target_pairs={{0,8},{1,9},{2,10},{3,11},{4,12},{5,13},{6,14},{7,15},{8,0},{9,1},... | collective-permute-start | bytes 2359304 | tf_op jit(solution)/shard_map/ppermute | solution.py:835
  (49 other events, 1042.2 us)

commit v2 on v1

--- a/solution.py
+++ b/solution.py
@@ -17,7 +17,7 @@
 SHARDS = 8
 RING = (0, 1, 3, 2)
 PARAM_ROWS = 32
-VMEM_BYTES = 60 << 20
+VMEM_BYTES = 62 << 20
 PLACES = 9
 PARITY, STAGE, OWN_SHARD = 8, 9, 10
 RATE_FIRST, RATE_SECOND = 12, 13
@@ -184,16 +184,18 @@
                 top = jnp.max(scores, axis=1, keepdims=True)
                 weights = jnp.exp(scores - top)
                 share = weights.astype(BF)
-                over = 1.0 / jnp.sum(weights, axis=1, keepdims=True)
+                part = dot(share, jnp.where(mine, values[:, lanes], BF(1)))
+                other = 64 - 64 * head
+                over = 1.0 / part[:, other : other + 1]
                 if state is not None:
                     which = quad * 4 + pair * 2 + head
                     shares[which] = share
                     rates = jnp.where(lane == which, over, rates)
-                parts.append(dot(share, values[:, lanes]) * over)
-            joined.append(jnp.where(lane < 64, parts[0], parts[1]).astype(BF))
-        mixed = jnp.concatenate(joined, axis=1)
-        if state is not None:
-            mixed_out[:, cols] = mixed
+                parts.append(part * over)
+            joined.append(jnp.where(lane < 64, parts[0], parts[1]))
+            if state is not None:
+                mixed_out[:, 256 * quad + 128 * pair : 256 * quad + 128 * pair + 128] = joined[pair]
+        mixed = jnp.concatenate(joined, axis=1).astype(BF)
         term = dot(mixed, w[l, pl.ds(3 * width + 256 * quad, 256), :])
         attended = term if attended is None else attended + term
         after(quad)
@@ -260,7 +262,7 @@
             lanes = slice(256 * quad + 128 * pair, 256 * quad + 128 * pair + 128)
             query, keys, values = qkv[0, :, lanes], qkv[1, :, lanes], qkv[2, :, lanes]
             out_rows = d_mixed[:, lanes].astype(F32)
-            along = out_rows * mixed[:, lanes].astype(F32)
+            mixed_rows = mixed[:, lanes]
             query_t = query.T
             d_query, d_keys, d_values = [], [], []
             for head in range(2):
@@ -269,7 +271,7 @@
                 over = rates[:, which : which + 1]
                 share = shares[which]
                 scaled = jnp.where(mine, out_rows * over, 0.0).astype(BF)
-                row_sum = jnp.sum(jnp.where(mine, along, 0.0), axis=1, keepdims=True) * over
+                row_sum = jnp.sum(scaled.astype(F32) * mixed_rows, axis=1, keepdims=True)
                 d_score = (share.astype(F32) * (dot(scaled, values, 1, 1) - row_sum)).astype(BF)
                 rows = slice(64 * head, 64 * head + 64)
                 d_query.append(dot(d_score, keys))
@@ -298,7 +300,7 @@
     return [
         ((3, length, width), BF),
         ((HEADS, length, length), BF),
-        ((length, width), BF),
+        ((length, width), F32),
         ((2, length, width), BF),
         ((4, length, width), BF),
         ((length, 128), F32),
@@ -318,7 +320,9 @@
 
 
 EARLY_PARTS = ("qkv", "mixed", 0, 1, 2)
-LATE_PARTS = ("n", "gp", "r")
+INNER_PARTS = ("gp",)
+END_PARTS = ("n", "r")
+BATCHES = {"attended": EARLY_PARTS, ("inner", 3): INNER_PARTS, "end": END_PARTS}
 
 
 def save_calls(state, kept, sem, l):
@@ -334,7 +338,7 @@
 
             @pl.when(l > 0)
             def _():
-                for part in LATE_PARTS:
+                for part in INNER_PARTS + END_PARTS:
                     state_copy(state, kept, sem, 0, part, False).wait()
 
     return after
@@ -399,14 +403,10 @@
                     ahead((6, 7), True)
                 if point == 2:
                     ahead((8,), True)
-                if point == "attended":
-                    for part in EARLY_PARTS:
-                        state_copy(state, kept, ssem, l, part, False).start()
+                for part in BATCHES.get(point, ()):
+                    state_copy(state, kept, ssem, l, part, False).start()
                 if isinstance(point, tuple):
                     ahead((point[1],), False)
-                if point == "end":
-                    for part in LATE_PARTS:
-                        state_copy(state, kept, ssem, l, part, False).start()
 
             forward_layer(l, lanes, x, w, prm, act, state, ready, after)
             return carry
@@ -418,7 +418,7 @@
         ]
         for copy in outs:
             copy.start()
-        for part in EARLY_PARTS + LATE_PARTS:
+        for part in EARLY_PARTS + INNER_PARTS + END_PARTS:
             state_copy(state, kept, ssem, 1, part, False).wait()
         for copy in outs:
             copy.wait()
@@ -504,11 +504,11 @@
         def after(point):
             waits(point)
             load_ahead(w_all, w, wsem, l, point)
-            if point in ("attended", "end"):
+            if point in BATCHES:
 
                 @pl.when(l == 0)
                 def _():
-                    for part in EARLY_PARTS if point == "attended" else LATE_PARTS:
+                    for part in BATCHES[point]:
                         state_copy(state, kept, ssem, 0, part, False).start()
 
         forward_layer(l, lanes, x, w, prm, act, state, ready, after)
@@ -881,14 +881,14 @@
     for half in range(2):
         x1[half] = permuted(held_back(r1[half], x0[half]), partner)
         r2[half] = permuted(r1[half], along)
-    z_first = permuted(held_back(jnp.where(even, r0[0], x0[1]), r2[0]), against)
+    z_first = permuted(held_back(jnp.where(even, r0[0], x0[1]), x1[0]), against)
     x2, z_second = [None, None], [None, None]
     for half in range(2):
         x2[half] = permuted(held_back(r2[half], x1[half]), partner)
         second_layer = jnp.where(even, x0[half], r0[half])
         z_second[half] = permuted(held_back(second_layer, z_first if half else r2[1]), against)
-    x_first = permuted(held_back(z_first, x2[0]), partner)
-    theirs = permuted(held_back(mine, r1[0]), partner)
+    x_first = permuted(held_back(z_first, x2[1]), partner)
+    theirs = permuted(held_back(mine, x2[1]), partner)
 
     def swapped(halves):
         return halves + [permuted(half, other_side) for half in halves]
@@ -934,11 +934,13 @@
     grads = settled(grads, jnp.where(early, last_row, second_row))
 
     total = jnp.where(early, d_up_early, d_up_late)
+    total = jnp.where(even, total[0], total[1]) + permuted(jnp.where(even, total[1], total[0]), partner)
+    for flips in ((1,), (2, 4, 6)):
+        total = sum([permuted(total, lambda s, q, flip=flip: (s, q ^ flip)) for flip in flips], total)
     step = 1
-    while step < copies:
+    while step < group:
         total = total + lax.ppermute(total, "dp", [(d, d ^ step) for d in range(copies)])
         step *= 2
-    total = jnp.where(even, total[0], total[1]) + permuted(jnp.where(even, total[1], total[0]), partner)
     total = total.reshape((1, 2, total.shape[0] // 2, total.shape[1]))
     return (activations, grads, total, joined)
 

time: 405 us -> 393 us (0.970)
  waiting for transfers between devices: 172 us -> 166 us
    ppermute x3 -> x0, waiting for transfers between devices: 7.91 us -> none  [body(): lax.ppermute(total, 'dp', [(d, d ^ step) for d in range(copies)])]
    ppermute x3 -> x0, starting transfers between devices: 5.33 us -> none  [body(): lax.ppermute(total, 'dp', [(d, d ^ step) for d in range(copies)])]
    ppermute x38 -> x42, starting transfers between devices: 74.1 us -> 75.5 us  [permuted(): return lax.ppermute(array, AXES, pairs)]
    ppermute x38 -> x42, waiting for transfers between devices: 164 us -> 166 us  [permuted(): return lax.ppermute(array, AXES, pairs)]
  transfers between devices with their start and end apart: 41 -> 42, of which waited for: 19 -> 21; matrix products, arithmetic and copies ran while one was open for 1% -> 1% of each run, Pallas kernels for 12% -> 12%
where the time goes in v2:
time: 393 us; the launch traced here: 388 us
  waiting for transfers between devices  166 us (42%)
  Pallas kernels  135 us (34%)
  starting transfers between devices  75.5 us (19%)
  local copies, waits for them, and re-layouts  6.61 us (2%)
  other arithmetic  4.29 us (1%)
    ppermute x42, waiting for transfers between devices, permuted(): return lax.ppermute(array, AXES, pairs)  166 us
    ppermute x42, starting transfers between devices, permuted(): return lax.ppermute(array, AXES, pairs)  75.5 us
    pallas_call x1, Pallas kernels, run_last(): pl.pallas_call(last_kernel, out_shape=[rows, rows, row, shape((2, 16, wid...  45.8 us
    pallas_call x1, Pallas kernels, run_first(): pl.pallas_call(first_kernel, out_shape=outs, in_specs=[smem, smem, anywhe...  44.1 us
    pallas_call x1, Pallas kernels, run_middle(): pl.pallas_call(middle_kernel, out_shape=outs, in_specs=[smem, smem] + [an...  41.6 us
  transfers between devices with their start and end apart: 42, of which 21 were waited for; matrix products, arithmetic and copies ran while one was open for 1% of the time, Pallas kernels for 12%

profile of v2, /device:TPU:0, one launch (start us, length us, event | category | flops | bytes accessed | tf_op | source)
XLA Modules:
  0.0 388.1 jit_solution(16957837854594372226)
XLA Ops:
  1.8 3.4 pack.1
  5.2 2.9 collective-permute-start.2
  12.9 16.0 %collective-permute-done.2.refs_13_ = bf16[576,768]{1,0:T(8,128)(2,1)S(1)} collective-permute-done((bf16[576,768]{1,0:T(8,128)(2,1)}, bf16[576,768]{1,0:T(8,128)(2,1)S(1)}, u32[]{:S(2)}, u32[]{:S(2)}) %collective-permute-start.2) | collective-permute-done | bytes 884768 | tf_op jit(solution)/shard_map/ppermute | solution.py:835
  28.9 3.0 collective-permute-done.refs_5_
  33.3 14.5 %collective-permute-done.14.refs_12_ = bf16[576,768]{1,0:T(8,128)(2,1)S(1)} collective-permute-done((bf16[576,768]{1,0:T(8,128)(2,1)}, bf16[576,768]{1,0:T(8,128)(2,1)S(1)}, u32[]{:S(2)}, u32[]{:S(2)}) %collective-permute-start.14) | collective-permute-done | bytes 884768 | tf_op jit(solution)/shard_map/ppermute | solution.py:835
  47.8 3.0 collective-permute-done.8.refs_4_
  50.8 15.1 %collective-permute-done.3.refs_17_ = bf16[576,768]{1,0:T(8,128)(2,1)S(1)} collective-permute-done((bf16[576,768]{1,0:T(8,128)(2,1)S(1)}, bf16[576,768]{1,0:T(8,128)(2,1)S(1)}, u32[]{:S(2)}, u32[]{:S(2)}) %collective-permute-start.3) | collective-permute-done | bytes 884768 | tf_op jit(solution)/shard_map/ppermute | solution.py:835
  69.9 17.0 %collective-permute-done.17.refs_16_ = bf16[576,768]{1,0:T(8,128)(2,1)S(1)} collective-permute-done((bf16[576,768]{1,0:T(8,128)(2,1)S(1)}, bf16[576,768]{1,0:T(8,128)(2,1)S(1)}, u32[]{:S(2)}, u32[]{:S(2)}) %collective-permute-start.17) | collective-permute-done | bytes 884768 | tf_op jit(solution)/shard_map/ppermute | solution.py:835
  90.8 2.6 collective-permute-start.23
  94.1 14.2 %collective-permute-done.4.refs_21_ = bf16[576,768]{1,0:T(8,128)(2,1)} collective-permute-done((bf16[576,768]{1,0:T(8,128)(2,1)}, bf16[576,768]{1,0:T(8,128)(2,1)}, u32[]{:S(2)}, u32[]{:S(2)}) %collective-permute-start.4) | collective-permute-done | bytes 884768 | tf_op jit(solution)/shard_map/ppermute | solution.py:835
  110.5 3.4 collective-permute-start.27
  115.0 16.1 %collective-permute-done.20.refs_20_ = bf16[576,768]{1,0:T(8,128)(2,1)S(1)} collective-permute-done((bf16[576,768]{1,0:T(8,128)(2,1)}, bf16[576,768]{1,0:T(8,128)(2,1)S(1)}, u32[]{:S(2)}, u32[]{:S(2)}) %collective-permute-start.20) | collective-permute-done | bytes 884768 | tf_op jit(solution)/shard_map/ppermute | solution.py:835
  134.9 13.9 %collective-permute-done.5.theirs = f32[32,768]{1,0:T(8,128)S(1)} collective-permute-done((f32[32,768]{1,0:T(8,128)S(1)}, f32[32,768]{1,0:T(8,128)S(1)}, u32[]{:S(2)}, u32[]{:S(2)}) %collective-permute-start.5) | collective-permute-done | bytes 98336 | tf_op jit(solution)/shard_map/ppermute | solution.py:835
  149.4 3.1 collective-permute-done.28.refs_29_
  155.2 44.1 %first.1 = (bf16[2,9216,768]{2,1,0:T(8,128)(2,1)}, bf16[512,768]{1,0:T(8,128)(2,1)}, bf16[512,768]{1,0:T(8,128)(2,1)}, bf16[2,3,512,768]{3,2,1,0:T(8,128)(2,1)},...) custom-call(s32[12]{0:T(128)} %fusion.scal, ...), custom_call_target="tpu_custom_call" | custom-call | flops 16106127360 | bytes 28311552 | tf_op jit(solution)/shard_map/first/pallas_call | solution.py:727
  200.7 17.7 %collective-permute-done.31.arrived = bf16[512,768]{1,0:T(8,128)(2,1)S(1)} collective-permute-done((bf16[512,768]{1,0:T(8,128)(2,1)}, bf16[512,768]{1,0:T(8,128)(2,1)S(1)}, u32[]{:S(2)}, u32[]{:S(2)}) %collective-permute-start.31) | collective-permute-done | bytes 786464 | tf_op jit(solution)/shard_map/ppermute | solution.py:835
  219.3 41.6 %middle.1 = (bf16[512,768]{1,0:T(8,128)(2,1)}, bf16[512,768]{1,0:T(8,128)(2,1)}, bf16[2,512,768]{2,1,0:T(8,128)(2,1)}, bf16[512,768]{1,0:T(8,128)(2,1)}, bf16[2,...) custom-call(s32[12]{0:T(128)} %fusion.scal, ...), custom_call_target="tpu_custom_call" | custom-call | flops 34628173824 | bytes 28311552 | tf_op jit(solution)/shard_map/middle/pallas_call | solution.py:748
  260.9 37.4 %collective-permute-start.32 = (bf16[512,768]{1,0:T(8,128)(2,1)}, bf16[512,768]{1,0:T(8,128)(2,1)S(1)}, u32[]{:S(2)}, u32[]{:S(2)}) collective-permute-start(bf16[512,768]{1,0:T(8,128)(2,1)} %get-tuple-element.56), channel_id=1, source_target_pairs={{0,16},{1,17},{2,18},{3,19},{4,20},{5,21},{6,22},{7,23},{8,24},{9,... | collective-permute-start | bytes 2359304 | tf_op jit(solution)/shard_map/ppermute | solution.py:835
  301.7 13.5 %collective-permute-done.32.arrived_up = bf16[512,768]{1,0:T(8,128)(2,1)S(1)} collective-permute-done((bf16[512,768]{1,0:T(8,128)(2,1)}, bf16[512,768]{1,0:T(8,128)(2,1)S(1)}, u32[]{:S(2)}, u32[]{:S(2)}) %collective-permute-start.32) | collective-permute-done | bytes 786464 | tf_op jit(solution)/shard_map/ppermute | solution.py:835
  315.3 4.2 %collective-permute-done.33.arrived_down = bf16[512,768]{1,0:T(8,128)(2,1)} collective-permute-done((bf16[512,768]{1,0:T(8,128)(2,1)}, bf16[512,768]{1,0:T(8,128)(2,1)}, u32[]{:S(2)}, u32[]{:S(2)}) %collective-permute-start.33) | collective-permute-done | bytes 786464 | tf_op jit(solution)/shard_map/ppermute | solution.py:835
  319.4 45.8 %last.1 = (bf16[2,512,768]{2,1,0:T(8,128)(2,1)}, bf16[2,512,768]{2,1,0:T(8,128)(2,1)}, bf16[512,768]{1,0:T(8,128)(2,1)}, f32[2,16,768]{2,1,0:T(8,128)}) custom-call(s32[12]{0:T(128)} %fusion.scal, s32[2,8]{1,0:T(2,128)} %lens.5, bf16[2,512,768]{2,1,0:T(8,128)(2,1)} %source.5, bf16[512,768]{1,0:T(8,128)(2,1)} %copy-done.28, ...), custom_call_target="tpu_custom_call" | custom-call | flops 18522046464 | bytes 28311552 | tf_op jit(solution)/shard_map/last/pallas_call | solution.py:772
  368.3 2.6 collective-permute-done.37
  378.3 2.8 collective-permute-done.40
  381.7 3.9 collective-permute-done.36
  (137 shorter events, 44.9 us)
Async XLA Ops:
  5.2 23.6 %collective-permute-start.2 = (bf16[576,768]{1,0:T(8,128)(2,1)}, bf16[576,768]{1,0:T(8,128)(2,1)S(1)}, u32[]{:S(2)}, u32[]{:S(2)}) collective-permute-start(bf16[576,768]{1,0:T(8,128)(2,1)} %get-tuple-element.41.refs_1_), channel_id=1, source_target_pairs={{0,8},{1,9},{2,10},{3,11},{4,12},{5,13},{6,14},{7,15},{8,0},{9,1},... | collective-permute-start | bytes 2654216 | tf_op jit(solution)/shard_map/ppermute | solution.py:835
  8.2 23.7 %collective-permute-start = (bf16[576,768]{1,0:T(8,128)(2,1)}, bf16[576,768]{1,0:T(8,128)(2,1)S(1)}, u32[]{:S(2)}, u32[]{:S(2)}) collective-permute-start(bf16[576,768]{1,0:T(8,128)(2,1)} %get-tuple-element.41.refs_1_), channel_id=1, source_target_pairs={{0,2},{1,3},{2,6},{3,7},{4,0},{5,1},{6,4},{7,5},{8,10},{9,11},{10,... | collective-permute-start | bytes 2654216 | tf_op jit(solution)/shard_map/ppermute | solution.py:835
  9.7 38.1 %collective-permute-start.14 = (bf16[576,768]{1,0:T(8,128)(2,1)}, bf16[576,768]{1,0:T(8,128)(2,1)S(1)}, u32[]{:S(2)}, u32[]{:S(2)}) collective-permute-start(bf16[576,768]{1,0:T(8,128)(2,1)} %get-tuple-element.45.refs_0_), channel_id=1, source_target_pairs={{0,8},{1,9},{2,10},{3,11},{4,12},{5,13},{6,14},{7,15},{8,0},{9,1},... | collective-permute-start | bytes 2654216 | tf_op jit(solution)/shard_map/ppermute | solution.py:835
  10.3 40.5 %collective-permute-start.8 = (bf16[576,768]{1,0:T(8,128)(2,1)}, bf16[576,768]{1,0:T(8,128)(2,1)S(1)}, u32[]{:S(2)}, u32[]{:S(2)}) collective-permute-start(bf16[576,768]{1,0:T(8,128)(2,1)} %get-tuple-element.45.refs_0_), channel_id=1, source_target_pairs={{0,2},{1,3},{2,6},{3,7},{4,0},{5,1},{6,4},{7,5},{8,10},{9,11},{10,... | collective-permute-start | bytes 2654216 | tf_op jit(solution)/shard_map/ppermute | solution.py:835
  31.9 34.1 %collective-permute-start.3 = (bf16[576,768]{1,0:T(8,128)(2,1)S(1)}, bf16[576,768]{1,0:T(8,128)(2,1)S(1)}, u32[]{:S(2)}, u32[]{:S(2)}) collective-permute-start(bf16[576,768]{1,0:T(8,128)(2,1)S(1)} %collective-permute-done.refs_5_), channel_id=1, source_target_pairs={{0,8},{1,9},{2,10},{3,11},{4,12},{5,13},{6,14},{7,15},{8,0},{9,1},... | collective-permute-start | bytes 2654216 | tf_op jit(solution)/shard_map/ppermute | solution.py:835
  32.1 36.4 %collective-permute-start.1 = (bf16[576,768]{1,0:T(8,128)(2,1)S(1)}, bf16[576,768]{1,0:T(8,128)(2,1)}, u32[]{:S(2)}, u32[]{:S(2)}) collective-permute-start(bf16[576,768]{1,0:T(8,128)(2,1)S(1)} %collective-permute-done.refs_5_), channel_id=1, source_target_pairs={{0,2},{1,3},{2,6},{3,7},{4,0},{5,1},{6,4},{7,5},{8,10},{9,11},{10,... | collective-permute-start | bytes 2654216 | tf_op jit(solution)/shard_map/ppermute | solution.py:835
  33.3 36.0 %collective-permute-start.7 = (bf16[576,768]{1,0:T(8,128)(2,1)}, bf16[576,768]{1,0:T(8,128)(2,1)S(1)}, u32[]{:S(2)}, u32[]{:S(2)}) collective-permute-start(bf16[576,768]{1,0:T(8,128)(2,1)} %get-tuple-element.41.refs_1_), channel_id=1, source_target_pairs={{0,1},{1,0},{2,3},{3,2},{4,5},{5,4},{6,7},{7,6},{8,9},{9,8},{10,11... | collective-permute-start | bytes 2654216 | tf_op jit(solution)/shard_map/ppermute | solution.py:835
  47.8 21.5 %collective-permute-start.6 = (bf16[576,768]{1,0:T(8,128)(2,1)}, bf16[576,768]{1,0:T(8,128)(2,1)S(1)}, u32[]{:S(2)}, u32[]{:S(2)}) collective-permute-start(bf16[576,768]{1,0:T(8,128)(2,1)} %get-tuple-element.45.refs_0_), channel_id=1, source_target_pairs={{0,1},{1,0},{2,3},{3,2},{4,5},{5,4},{6,7},{7,6},{8,9},{9,8},{10,11... | collective-permute-start | bytes 2654216 | tf_op jit(solution)/shard_map/ppermute | solution.py:835
  65.9 20.9 %collective-permute-start.17 = (bf16[576,768]{1,0:T(8,128)(2,1)S(1)}, bf16[576,768]{1,0:T(8,128)(2,1)S(1)}, u32[]{:S(2)}, u32[]{:S(2)}) collective-permute-start(bf16[576,768]{1,0:T(8,128)(2,1)S(1)} %collective-permute-done.8.refs_4_), channel_id=1, source_target_pairs={{0,8},{1,9},{2,10},{3,11},{4,12},{5,13},{6,14},{7,15},{8,0},{9,1},... | collective-permute-start | bytes 2654216 | tf_op jit(solution)/shard_map/ppermute | solution.py:835
  68.4 22.4 %collective-permute-start.11 = (bf16[576,768]{1,0:T(8,128)(2,1)S(1)}, bf16[576,768]{1,0:T(8,128)(2,1)}, u32[]{:S(2)}, u32[]{:S(2)}) collective-permute-start(bf16[576,768]{1,0:T(8,128)(2,1)S(1)} %collective-permute-done.8.refs_4_), channel_id=1, source_target_pairs={{0,2},{1,3},{2,6},{3,7},{4,0},{5,1},{6,4},{7,5},{8,10},{9,11},{10,... | collective-permute-start | bytes 2654216 | tf_op jit(solution)/shard_map/ppermute | solution.py:835
  69.3 24.2 %collective-permute-start.10 = (bf16[576,768]{1,0:T(8,128)(2,1)S(1)}, bf16[576,768]{1,0:T(8,128)(2,1)}, u32[]{:S(2)}, u32[]{:S(2)}) collective-permute-start(bf16[576,768]{1,0:T(8,128)(2,1)S(1)} %collective-permute-done.refs_5_), channel_id=1, source_target_pairs={{0,1},{1,0},{2,3},{3,2},{4,5},{5,4},{6,7},{7,6},{8,9},{9,8},{10,11... | collective-permute-start | bytes 2654216 | tf_op jit(solution)/shard_map/ppermute | solution.py:835
  69.3 24.2 %collective-permute-start.15 = (bf16[576,768]{1,0:T(8,128)(2,1)S(1)}, bf16[576,768]{1,0:T(8,128)(2,1)}, u32[]{:S(2)}, u32[]{:S(2)}) collective-permute-start(bf16[576,768]{1,0:T(8,128)(2,1)S(1)} %collective-permute-done.14.refs_12_), channel_id=1, source_target_pairs={{0,1},{1,0},{2,3},{3,2},{4,5},{5,4},{6,7},{7,6},{8,9},{9,8},{10,11... | collective-permute-start | bytes 2654216 | tf_op jit(solution)/shard_map/ppermute | solution.py:835
  69.8 24.2 %collective-permute-start.9 = (bf16[576,768]{1,0:T(8,128)(2,1)S(1)}, bf16[576,768]{1,0:T(8,128)(2,1)}, u32[]{:S(2)}, u32[]{:S(2)}) collective-permute-start(bf16[576,768]{1,0:T(8,128)(2,1)S(1)} %collective-permute-done.8.refs_4_), channel_id=1, source_target_pairs={{0,1},{1,0},{2,3},{3,2},{4,5},{5,4},{6,7},{7,6},{8,9},{9,8},{10,11... | collective-permute-start | bytes 2654216 | tf_op jit(solution)/shard_map/ppermute | solution.py:835
  93.5 20.5 %collective-permute-start.13 = (bf16[576,768]{1,0:T(8,128)(2,1)}, bf16[576,768]{1,0:T(8,128)(2,1)S(1)}, u32[]{:S(2)}, u32[]{:S(2)}) collective-permute-start(bf16[576,768]{1,0:T(8,128)(2,1)} %collective-permute-done.1.refs_9_), channel_id=1, source_target_pairs={{0,1},{1,0},{2,3},{3,2},{4,5},{5,4},{6,7},{7,6},{8,9},{9,8},{10,11... | collective-permute-start | bytes 2654216 | tf_op jit(solution)/shard_map/ppermute | solution.py:835
  108.3 22.8 %collective-permute-start.20 = (bf16[576,768]{1,0:T(8,128)(2,1)}, bf16[576,768]{1,0:T(8,128)(2,1)S(1)}, u32[]{:S(2)}, u32[]{:S(2)}) collective-permute-start(bf16[576,768]{1,0:T(8,128)(2,1)} %collective-permute-done.11.refs_8_), channel_id=1, source_target_pairs={{0,8},{1,9},{2,10},{3,11},{4,12},{5,13},{6,14},{7,15},{8,0},{9,1},... | collective-permute-start | bytes 2654216 | tf_op jit(solution)/shard_map/ppermute | solution.py:835
  110.5 22.8 %collective-permute-start.12 = (bf16[576,768]{1,0:T(8,128)(2,1)}, bf16[576,768]{1,0:T(8,128)(2,1)S(1)}, u32[]{:S(2)}, u32[]{:S(2)}) collective-permute-start(bf16[576,768]{1,0:T(8,128)(2,1)} %collective-permute-done.11.refs_8_), channel_id=1, source_target_pairs={{0,1},{1,0},{2,3},{3,2},{4,5},{5,4},{6,7},{7,6},{8,9},{9,8},{10,11... | collective-permute-start | bytes 2654216 | tf_op jit(solution)/shard_map/ppermute | solution.py:835
  110.5 24.3 %collective-permute-start.27 = (bf16[576,768]{1,0:T(8,128)(2,1)S(1)}, bf16[576,768]{1,0:T(8,128)(2,1)S(1)}, u32[]{:S(2)}, u32[]{:S(2)}) collective-permute-start(bf16[576,768]{1,0:T(8,128)(2,1)S(1)} %get-tuple-element.50), channel_id=1, source_target_pairs={{0,4},{1,5},{2,0},{3,1},{4,6},{5,7},{6,2},{7,3},{8,12},{9,13},{10,... | collective-permute-start | bytes 2654216 | tf_op jit(solution)/shard_map/ppermute | solution.py:835
  114.0 34.8 %collective-permute-start.22 = (bf16[576,768]{1,0:T(8,128)(2,1)}, bf16[576,768]{1,0:T(8,128)(2,1)S(1)}, u32[]{:S(2)}, u32[]{:S(2)}) collective-permute-start(bf16[576,768]{1,0:T(8,128)(2,1)} %collective-permute-done.4.refs_21_), channel_id=1, source_target_pairs={{0,1},{1,0},{2,3},{3,2},{4,5},{5,4},{6,7},{7,6},{8,9},{9,8},{10,11... | collective-permute-start | bytes 2654216 | tf_op jit(solution)/shard_map/ppermute | solution.py:835
  114.2 35.1 %collective-permute-start.25 = (bf16[576,768]{1,0:T(8,128)(2,1)S(1)}, bf16[576,768]{1,0:T(8,128)(2,1)S(1)}, u32[]{:S(2)}, u32[]{:S(2)}) collective-permute-start(bf16[576,768]{1,0:T(8,128)(2,1)S(1)} %collective-permute-done.23.refs_24_), channel_id=1, source_target_pairs={{0,8},{1,9},{2,10},{3,11},{4,12},{5,13},{6,14},{7,15},{8,0},{9,1},... | collective-permute-start | bytes 2654216 | tf_op jit(solution)/shard_map/ppermute | solution.py:835
  131.1 21.4 %collective-permute-start.28 = (bf16[576,768]{1,0:T(8,128)(2,1)S(1)}, bf16[576,768]{1,0:T(8,128)(2,1)S(1)}, u32[]{:S(2)}, u32[]{:S(2)}) collective-permute-start(bf16[576,768]{1,0:T(8,128)(2,1)S(1)} %get-tuple-element.51), channel_id=1, source_target_pairs={{0,4},{1,5},{2,0},{3,1},{4,6},{5,7},{6,2},{7,3},{8,12},{9,13},{10,... | collective-permute-start | bytes 2654216 | tf_op jit(solution)/shard_map/ppermute | solution.py:835
  260.9 54.4 %collective-permute-start.32 = (bf16[512,768]{1,0:T(8,128)(2,1)}, bf16[512,768]{1,0:T(8,128)(2,1)S(1)}, u32[]{:S(2)}, u32[]{:S(2)}) collective-permute-start(bf16[512,768]{1,0:T(8,128)(2,1)} %get-tuple-element.56), channel_id=1, source_target_pairs={{0,16},{1,17},{2,18},{3,19},{4,20},{5,21},{6,22},{7,23},{8,24},{9,... | collective-permute-start | bytes 2359304 | tf_op jit(solution)/shard_map/ppermute | solution.py:835
  298.3 21.1 %collective-permute-start.33 = (bf16[512,768]{1,0:T(8,128)(2,1)}, bf16[512,768]{1,0:T(8,128)(2,1)}, u32[]{:S(2)}, u32[]{:S(2)}) collective-permute-start(bf16[512,768]{1,0:T(8,128)(2,1)} %get-tuple-element.57), channel_id=1, source_target_pairs={{16,0},{17,1},{18,2},{19,3},{20,4},{21,5},{22,6},{23,7},{24,8},{25... | collective-permute-start | bytes 2359304 | tf_op jit(solution)/shard_map/ppermute | solution.py:835
  299.6 65.6 %collective-permute-start.34 = (bf16[512,768]{1,0:T(8,128)(2,1)}, bf16[512,768]{1,0:T(8,128)(2,1)S(1)}, u32[]{:S(2)}, u32[]{:S(2)}) collective-permute-start(bf16[512,768]{1,0:T(8,128)(2,1)} %get-tuple-element.67), channel_id=1, source_target_pairs={{0,8},{1,9},{2,10},{3,11},{4,12},{5,13},{6,14},{7,15},{8,0},{9,1},... | collective-permute-start | bytes 2359304 | tf_op jit(solution)/shard_map/ppermute | solution.py:835
  300.5 64.7 %collective-permute-start.35 = (bf16[512,768]{1,0:T(8,128)(2,1)}, bf16[512,768]{1,0:T(8,128)(2,1)S(1)}, u32[]{:S(2)}, u32[]{:S(2)}) collective-permute-start(bf16[512,768]{1,0:T(8,128)(2,1)} %get-tuple-element.68), channel_id=1, source_target_pairs={{0,8},{1,9},{2,10},{3,11},{4,12},{5,13},{6,14},{7,15},{8,0},{9,1},... | collective-permute-start | bytes 2359304 | tf_op jit(solution)/shard_map/ppermute | solution.py:835
  (50 other events, 851.6 us)

commit v3 on v2

--- a/solution.py
+++ b/solution.py
@@ -18,7 +18,7 @@
 RING = (0, 1, 3, 2)
 PARAM_ROWS = 32
 VMEM_BYTES = 62 << 20
-PLACES = 9
+PARTS = 3
 PARITY, STAGE, OWN_SHARD = 8, 9, 10
 RATE_FIRST, RATE_SECOND = 12, 13
 
@@ -102,30 +102,45 @@
     return pieces[28 + side * 2 + half]
 
 
-def block_view(w, l, place):
-    width = w.shape[2]
-    return w.at[l, pl.ds(place * width, (4 if place == 8 else 1) * width)]
-
-
-def start_block(scal, pieces, w, sem, l, place):
-    depth, width = w.shape[2] // 8, w.shape[2]
-    half, block = (0, place) if place < 6 else (1, place - 6)
-    rows = 4 * depth if place == 8 else depth
+def rows_of(w, l, block):
+    depth = w.shape[2] // 12
+    return jnp.concatenate([w[l, j, depth * block : depth * (block + 1), :] for j in range(SHARDS)], axis=0)
+
+
+def down_of(w, l, block=None):
+    depth = w.shape[2] // 12
+    shards = range(SHARDS) if block is None else (2 * block, 2 * block + 1)
+    return jnp.concatenate([w[l, j, 8 * depth :, :] for j in shards], axis=0)
+
+
+def part_view(w, l, part):
+    rows = w.shape[2] // PARTS
+    return w.at[l, :, pl.ds(part * rows, rows)]
+
+
+def start_part(scal, pieces, w, sem, l, part):
+    half_rows = w.shape[2] // 2
+    rows = w.shape[2] // PARTS
+    begin, end = part * rows, (part + 1) * rows
     for parity in range(2):
 
         @pl.when(scal[PARITY] == parity)
         def _():
             for i in range(8):
-                source = piece_of(pieces, parity, l, i // 2, i % 2, half)
-                at = pl.multiple_of(place * width + rows * scal[i], 16)
-                pltpu.make_async_copy(
-                    source.at[pl.ds(block * depth, rows)], w.at[l, pl.ds(at, rows)], sem.at[l, place]
-                ).start()
-
-
-def wait_block(w, sem, l, place):
-    view = block_view(w, l, place)
-    pltpu.make_async_copy(view, view, sem.at[l, place]).wait()
+                for half in range(2):
+                    low, high = max(begin, half * half_rows), min(end, (half + 1) * half_rows)
+                    if low < high:
+                        source = piece_of(pieces, parity, l, i // 2, i % 2, half)
+                        pltpu.make_async_copy(
+                            source.at[pl.ds(low - half * half_rows, high - low)],
+                            w.at[l, scal[i], pl.ds(low, high - low)],
+                            sem.at[l, part],
+                        ).start()
+
+
+def wait_part(w, sem, l, part):
+    view = part_view(w, l, part)
+    pltpu.make_async_copy(view, view, sem.at[l, part]).wait()
 
 
 def take_params(scal, mine, theirs, prm):
@@ -151,92 +166,89 @@
 
 def forward_layer(l, lens_lanes, x, w, prm, act, state, ready, after):
     length, width = x.shape[1:]
-    quads = width // 256
     lane = lax.broadcasted_iota(jnp.int32, (1, 128), 1)
+    low = lane < 64
     value = x[l]
-    for place in range(4):
-        ready(place)
+    ready(0)
     after("begin")
-    attended = None
+    query = (dot(value, rows_of(w, l, 0)) + prm[l, 0:1, :]).astype(BF)
+    keys = dot(value, rows_of(w, l, 1)).astype(BF)
+    values = (dot(value, rows_of(w, l, 2)) + prm[l, 1:2, :]).astype(BF)
     if state is not None:
         qkv, shares, mixed_out, n, gp, r = state
         rates = jnp.zeros((length, 128), F32)
-    for quad in range(quads):
-        cols = slice(256 * quad, 256 * quad + 256)
-        query = (dot(value, w[l, 0:width, cols]) + prm[l, 0:1, cols]).astype(BF)
-        keys = dot(value, w[l, width : 2 * width, cols]).astype(BF)
-        values = (dot(value, w[l, 2 * width : 3 * width, cols]) + prm[l, 1:2, cols]).astype(BF)
+        qkv[0] = query
+        qkv[1] = keys
+        qkv[2] = values
+    query_lanes, key_lanes = lens_lanes[0], lens_lanes[1]
+    ones = jnp.ones((length, 128), BF)
+    mixed = []
+    for pair in range(width // 128):
+        lanes = slice(128 * pair, 128 * pair + 128)
+        scaled = query[:, lanes] * BF(0.125)
+        upper = jnp.concatenate([jnp.where(low, scaled, BF(0)), query_lanes], axis=1)
+        lower = jnp.concatenate([jnp.where(low, BF(0), scaled), query_lanes], axis=1)
+        scores = dot(
+            jnp.concatenate([upper, lower], axis=0), jnp.concatenate([keys[:, lanes], key_lanes], axis=1), 1, 1
+        )
+        top = jnp.max(scores, axis=1, keepdims=True)
+        share = jnp.exp(scores - top).astype(BF)
+        part = dot(share, jnp.concatenate([values[:, lanes], ones], axis=1))
+        over = 1.0 / part[:, 128:129]
+        part = part[:, 0:128] * over
+        joined = jnp.where(low, part[:length], part[length:])
         if state is not None:
-            qkv[0, :, cols] = query
-            qkv[1, :, cols] = keys
-            qkv[2, :, cols] = values
-        query_lanes, key_lanes = lens_lanes[0], lens_lanes[1]
-        joined = []
-        for pair in range(2):
-            lanes = slice(128 * pair, 128 * pair + 128)
-            scaled = query[:, lanes] * BF(0.125)
-            parts = []
-            for head in range(2):
-                mine = (lane < 64) == (head == 0)
-                scores = dot(
-                    jnp.where(mine, scaled, query_lanes), jnp.where(mine, keys[:, lanes], key_lanes), 1, 1
-                )
-                top = jnp.max(scores, axis=1, keepdims=True)
-                weights = jnp.exp(scores - top)
-                share = weights.astype(BF)
-                part = dot(share, jnp.where(mine, values[:, lanes], BF(1)))
-                other = 64 - 64 * head
-                over = 1.0 / part[:, other : other + 1]
-                if state is not None:
-                    which = quad * 4 + pair * 2 + head
-                    shares[which] = share
-                    rates = jnp.where(lane == which, over, rates)
-                parts.append(part * over)
-            joined.append(jnp.where(lane < 64, parts[0], parts[1]))
+            shares[2 * pair] = share[:length]
+            shares[2 * pair + 1] = share[length:]
+            mixed_out[:, lanes] = joined
+            rates = jnp.where(lane == 2 * pair, over[:length], rates)
+            rates = jnp.where(lane == 2 * pair + 1, over[length:], rates)
+        mixed.append(joined.astype(BF))
+        if pair % 2:
+            after(pair // 2)
+    mixed = jnp.concatenate(mixed, axis=1)
+    ready(1)
+    ready(2)
+    after("attended")
+    halves = [slice(0, length // 2), slice(length // 2, length)]
+    firsts, rates_first = [], []
+    for rows in halves:
+        attended = dot(mixed[rows], rows_of(w, l, 3))
+        summed = value[rows].astype(F32) + (attended + prm[l, 2:3, :])
+        normal, rate = centre_and_scale(summed)
+        firsts.append((normal * prm[l, 8:9, :] + prm[l, 10:11, :]).astype(BF))
+        rates_first.append(rate)
+        if state is not None:
+            n[0, rows] = normal.astype(BF)
+    for block in range(4):
+        for rows, first in zip(halves, firsts):
+            inner = dot(first, rows_of(w, l, 4 + block))
+            inner = inner + prm[l, 4 + block : 5 + block, :]
+            below = 0.5 + 0.5 * lax.erf(inner * (2**-0.5))
+            act[rows, block * width : (block + 1) * width] = (inner * below).astype(BF)
             if state is not None:
-                mixed_out[:, 256 * quad + 128 * pair : 256 * quad + 128 * pair + 128] = joined[pair]
-        mixed = jnp.concatenate(joined, axis=1).astype(BF)
-        term = dot(mixed, w[l, pl.ds(3 * width + 256 * quad, 256), :])
-        attended = term if attended is None else attended + term
-        after(quad)
-    after("attended")
-    summed = value.astype(F32) + (attended + prm[l, 2:3, :])
-    normal, rate_first = centre_and_scale(summed)
-    first = (normal * prm[l, 8:9, :] + prm[l, 10:11, :]).astype(BF)
-    if state is not None:
-        n[0] = normal.astype(BF)
-    for block in range(4):
-        ready(4 + block)
-        inner = dot(first, w[l, pl.ds((4 + block) * width, width), :]) + prm[l, 4 + block : 5 + block, :]
-        below = 0.5 + 0.5 * lax.erf(inner * (2**-0.5))
-        act[block] = (inner * below).astype(BF)
+                bell = jnp.exp(-0.5 * inner * inner) * 0.3989422804014327
+                gp[block, rows] = (below + inner * bell).astype(BF)
+    after("inner")
+    for rows, first, rate_first in zip(halves, firsts, rates_first):
+        branch = dot(act[rows, :], down_of(w, l))
+        closing = first.astype(F32) + (branch + prm[l, 3:4, :])
+        normal, rate_second = centre_and_scale(closing)
         if state is not None:
-            bell = jnp.exp(-0.5 * inner * inner) * 0.3989422804014327
-            gp[block] = (below + inner * bell).astype(BF)
-        after(("inner", block))
-    ready(8)
-    branch = None
-    for block in range(4):
-        term = dot(act[block], w[l, pl.ds((8 + block) * width, width), :])
-        branch = term if branch is None else branch + term
-    closing = first.astype(F32) + (branch + prm[l, 3:4, :])
-    normal, rate_second = centre_and_scale(closing)
-    if state is not None:
-        n[1] = normal.astype(BF)
-        rates = jnp.where(lane == RATE_FIRST, rate_first, rates)
-        r[...] = jnp.where(lane == RATE_SECOND, rate_second, rates)
-    x[l + 1] = (normal * prm[l, 9:10, :] + prm[l, 11:12, :]).astype(BF)
+            n[1, rows] = normal.astype(BF)
+            own = jnp.where(lane == RATE_FIRST, rate_first, rates[rows])
+            r[rows] = jnp.where(lane == RATE_SECOND, rate_second, own)
+        x[l + 1, rows] = (normal * prm[l, 9:10, :] + prm[l, 11:12, :]).astype(BF)
     after("end")
 
 
 def backward_layer(l, c_in, c_out, x, w, prm, d_qkv, d_up, state, ready, have, spent, after):
     qkv, shares, mixed, n, gp, r = state
     length, width = x.shape[1:]
-    quads = width // 256
     lane = lax.broadcasted_iota(jnp.int32, (1, 128), 1)
     for part in ("n", "r", "gp"):
         have(part)
-    ready(8)
+    ready(2)
     rates = r[...]
     rate_first = rates[:, RATE_FIRST : RATE_FIRST + 1]
     rate_second = rates[:, RATE_SECOND : RATE_SECOND + 1]
@@ -244,55 +256,55 @@
     d_branch = d_closing.astype(BF)
     total = d_closing
     for block in range(4):
-        ready(4 + block)
-        d_active = dot(d_branch, w[l, pl.ds((8 + block) * width, width), :], 1, 1)
+        d_active = dot(d_branch, down_of(w, l, block), 1, 1)
         d_inner = (d_active * gp[block].astype(F32)).astype(BF)
-        total = total + dot(d_inner, w[l, pl.ds((4 + block) * width, width), :], 1, 1)
+        if block == 0:
+            ready(1)
+        total = total + dot(d_inner, rows_of(w, l, 4 + block), 1, 1)
         after(("inner", block))
     spent("gp")
     d_summed = norm_backward(n[0].astype(F32), rate_first, prm[l, 8:9, :], total)
     spent("n")
-    ready(3)
-    d_mixed = dot(d_summed.astype(BF), w[l, 3 * width : 4 * width, :], 1, 1).astype(BF)
+    ready(0)
+    d_mixed = dot(d_summed.astype(BF), rows_of(w, l, 3), 1, 1).astype(BF)
     have("mixed")
     have("qkv")
-    for quad in range(quads):
-        have(quad)
-        for pair in range(2):
-            lanes = slice(256 * quad + 128 * pair, 256 * quad + 128 * pair + 128)
-            query, keys, values = qkv[0, :, lanes], qkv[1, :, lanes], qkv[2, :, lanes]
-            out_rows = d_mixed[:, lanes].astype(F32)
-            mixed_rows = mixed[:, lanes]
-            query_t = query.T
-            d_query, d_keys, d_values = [], [], []
-            for head in range(2):
-                mine = (lane < 64) == (head == 0)
-                which = quad * 4 + pair * 2 + head
-                over = rates[:, which : which + 1]
-                share = shares[which]
-                scaled = jnp.where(mine, out_rows * over, 0.0).astype(BF)
-                row_sum = jnp.sum(scaled.astype(F32) * mixed_rows, axis=1, keepdims=True)
-                d_score = (share.astype(F32) * (dot(scaled, values, 1, 1) - row_sum)).astype(BF)
-                rows = slice(64 * head, 64 * head + 64)
-                d_query.append(dot(d_score, keys))
-                d_keys.append(dot(query_t[rows], d_score))
-                d_values.append(dot(scaled.T[rows], share))
-            d_qkv[0, :, lanes] = (jnp.where(lane < 64, d_query[0], d_query[1]) * 0.125).astype(BF)
-            d_qkv[1, :, lanes] = (jnp.concatenate(d_keys, axis=0) * 0.125).astype(BF).T
-            d_qkv[2, :, lanes] = jnp.concatenate(d_values, axis=0).astype(BF).T
-        spent(quad)
-        after(quad)
+    low = lane < 64
+    for pair in range(width // 128):
+        if pair % 2 == 0:
+            have(pair // 2)
+        lanes = slice(128 * pair, 128 * pair + 128)
+        query, keys, values = qkv[0, :, lanes], qkv[1, :, lanes], qkv[2, :, lanes]
+        out_rows = d_mixed[:, lanes].astype(F32)
+        upper = jnp.where(low, out_rows * rates[:, 2 * pair : 2 * pair + 1], 0.0)
+        lower = jnp.where(low, 0.0, out_rows * rates[:, 2 * pair + 1 : 2 * pair + 2])
+        scaled = jnp.concatenate([upper, lower], axis=0).astype(BF)
+        mixed_rows = mixed[:, lanes]
+        mixed_rows = jnp.concatenate([mixed_rows, mixed_rows], axis=0)
+        row_sum = jnp.sum(scaled.astype(F32) * mixed_rows, axis=1, keepdims=True)
+        share = jnp.concatenate([shares[2 * pair], shares[2 * pair + 1]], axis=0)
+        d_score = (share.astype(F32) * (dot(scaled, values, 1, 1) - row_sum)).astype(BF)
+        d_query = dot(d_score, keys)
+        queries = jnp.concatenate([jnp.where(low, query, BF(0)), jnp.where(low, BF(0), query)], axis=0)
+        d_keys = dot(queries.T, d_score)
+        d_values = dot(scaled.T, share)
+        d_query = jnp.where(low, d_query[:length], d_query[length:])
+        d_qkv[:, lanes] = (d_query * 0.125).astype(BF)
+        d_qkv[:, width + 128 * pair : width + 128 * pair + 128] = (d_keys * 0.125).astype(BF).T
+        d_qkv[:, 2 * width + 128 * pair : 2 * width + 128 * pair + 128] = d_values.astype(BF).T
+        if pair % 2:
+            spent(pair // 2)
+            after(pair // 2)
     for part in ("r", "mixed", "qkv"):
         spent(part)
     have("x")
     down = dot(x[l], prm[l, 12:28, :].astype(BF), 1, 1).astype(BF)
     rank = down.shape[1] // 2
-    d_up[l, 0:rank, :] = 2.0 * dot(down, d_qkv[0], 0, 0)[0:rank]
-    d_up[l, rank : 2 * rank, :] = 2.0 * dot(down, d_qkv[2], 0, 0)[rank:]
+    d_up[l, 0:rank, :] = 2.0 * dot(down, d_qkv[:, 0:width], 0, 0)[0:rank]
+    d_up[l, rank : 2 * rank, :] = 2.0 * dot(down, d_qkv[:, 2 * width : 3 * width], 0, 0)[rank:]
     total = d_summed
     for kind in range(3):
-        ready(kind)
-        total = total + dot(d_qkv[kind], w[l, kind * width : (kind + 1) * width, :], 1, 1)
+        total = total + dot(d_qkv[:, kind * width : (kind + 1) * width], rows_of(w, l, kind), 1, 1)
     c_out[...] = total.astype(BF)
 
 
@@ -322,7 +334,7 @@
 EARLY_PARTS = ("qkv", "mixed", 0, 1, 2)
 INNER_PARTS = ("gp",)
 END_PARTS = ("n", "r")
-BATCHES = {"attended": EARLY_PARTS, ("inner", 3): INNER_PARTS, "end": END_PARTS}
+BATCHES = {0: ("qkv", 0), 1: (1,), 2: (2, "mixed"), "inner": INNER_PARTS, "end": END_PARTS}
 
 
 def save_calls(state, kept, sem, l):
@@ -353,20 +365,19 @@
     parity, stage = scal[PARITY], scal[STAGE]
 
     def out_copy(l, place):
-        return pltpu.make_async_copy(block_view(w, l, place), block_view(w_all, l, place), osem.at[l, place])
-
-    for place in range(4):
-        start_block(scal, pieces, w, wsem, 0, place)
+        return pltpu.make_async_copy(part_view(w, l, place), part_view(w_all, l, place), osem.at[l, place])
+
+    start_part(scal, pieces, w, wsem, 0, 0)
 
     @pl.when(stage != 0)
     def _():
         for l in range(2):
-            for place in range(PLACES):
-                if l or place > 3:
-                    start_block(scal, pieces, w, wsem, l, place)
+            for place in range(PARTS):
+                if l or place:
+                    start_part(scal, pieces, w, wsem, l, place)
         for l in range(2):
-            for place in range(PLACES):
-                wait_block(w, wsem, l, place)
+            for place in range(PARTS):
+                wait_part(w, wsem, l, place)
                 out_copy(l, place).start()
 
     @pl.when(stage == 0)
@@ -381,8 +392,7 @@
 
         def layer(l, carry):
             def ready(place):
-                wait_block(w, wsem, l, place)
-                out_copy(l, place).start()
+                wait_part(w, wsem, l, place)
 
             waits = save_calls(state, kept, ssem, l)
 
@@ -393,20 +403,18 @@
                         @pl.when(l == i)
                         def _():
                             for place in places:
-                                start_block(scal, pieces, w, wsem, i if own else 1, place)
+                                start_part(scal, pieces, w, wsem, i if own else 1, place)
 
             def after(point):
                 waits(point)
-                if point == 0:
-                    ahead((4, 5), True)
-                if point == 1:
-                    ahead((6, 7), True)
-                if point == 2:
-                    ahead((8,), True)
+                if point in OWN_AHEAD:
+                    ahead(OWN_AHEAD[point], True)
+                if point in NEXT_AHEAD:
+                    ahead(NEXT_AHEAD[point], False)
+                for place in OUT_AT.get(point, ()):
+                    out_copy(l, place).start()
                 for part in BATCHES.get(point, ()):
                     state_copy(state, kept, ssem, l, part, False).start()
-                if isinstance(point, tuple):
-                    ahead((point[1],), False)
 
             forward_layer(l, lanes, x, w, prm, act, state, ready, after)
             return carry
@@ -424,23 +432,28 @@
             copy.wait()
 
     for l in range(2):
-        for place in range(PLACES):
+        for place in range(PARTS):
             out_copy(l, place).wait()
+
+
+OWN_AHEAD = {"begin": (1,), 1: (2,)}
+NEXT_AHEAD = {"attended": (0,)}
+OUT_AT = {0: (0,), "attended": (1,), "inner": (2,)}
 
 
 def load_weights(w_all, w, wsem, l, places):
     for place in places:
-        pltpu.make_async_copy(block_view(w_all, l, place), block_view(w, l, place), wsem.at[l, place]).start()
+        pltpu.make_async_copy(part_view(w_all, l, place), part_view(w, l, place), wsem.at[l, place]).start()
 
 
 def load_ahead(w_all, w, wsem, l, point):
-    own = {"begin": (4,), 0: (5, 6), 1: (7,), 2: (8,)}.get(point, ())
-    load_weights(w_all, w, wsem, l, own)
-    if isinstance(point, tuple):
+    load_weights(w_all, w, wsem, l, OWN_AHEAD.get(point, ()))
+    following = NEXT_AHEAD.get(point, ())
+    if following:
 
         @pl.when(l == 0)
         def _():
-            load_weights(w_all, w, wsem, 1, (point[1],))
+            load_weights(w_all, w, wsem, 1, following)
 
 
 def middle_kernel(scal, lens, source, arrived, cotangent, early_first, early_second, mine, theirs, w_all, *refs):
@@ -449,7 +462,7 @@
     x, w, prm, lanes, act, c, wsem, xsem, hsem, ssem = refs[:10]
     state = refs[10:]
     parity, stage = scal[PARITY], scal[STAGE]
-    load_weights(w_all, w, wsem, 0, range(4))
+    load_weights(w_all, w, wsem, 0, (0,))
     d_up[...] = jnp.zeros(d_up.shape, F32)
     take_params(scal, mine, theirs, prm)
     query_lanes, key_lanes = label_lanes(lens, parity, x.shape[1])
@@ -497,7 +510,7 @@
 
     def layer(l, carry):
         def ready(place):
-            wait_block(w, wsem, l, place)
+            wait_part(w, wsem, l, place)
 
         waits = save_calls(state, kept, ssem, l)
 
@@ -598,9 +611,9 @@
         cot.start()
         for part in ("n", "r"):
             load(1, part).start()
-        load_weights(w_all, w, wsem, 1, (8,))
+        load_weights(w_all, w, wsem, 1, (2,))
         load(1, "gp").start()
-        load_weights(w_all, w, wsem, 1, (4, 5))
+        load_weights(w_all, w, wsem, 1, (1,))
         cot.wait()
 
         def gradient(i, carry):
@@ -622,11 +635,11 @@
                     load(0, part).start()
 
             def ready(place):
-                wait_block(w, wsem, l, place)
+                wait_part(w, wsem, l, place)
 
             def after(point):
                 key = point[1] if isinstance(point, tuple) else point + 4
-                load_weights(w_all, w, wsem, l, ((6,), (7,), (3,), (), (0,), (1, 2), ())[key])
+                load_weights(w_all, w, wsem, l, ((), (0,), (), (), (), (), ())[key])
 
                 @pl.when(i == 0)
                 def _():
@@ -637,11 +650,11 @@
                         start_x.start()
                         middle_x.start()
                     if key == 5:
-                        load_weights(w_all, w, wsem, 0, (8,))
+                        load_weights(w_all, w, wsem, 0, (2,))
                         carry_in(x.at[2]).wait()
                         carry_out(x.at[2], joined).start()
                     if key == 6:
-                        load_weights(w_all, w, wsem, 0, (4, 5))
+                        load_weights(w_all, w, wsem, 0, (1,))
 
             backward_layer(l, c.at[i], c.at[1 - i], x, w, prm, act, d_up, state, ready, have, spent, after)
             return carry
@@ -652,7 +665,7 @@
 
     @pl.when(stage != 0)
     def _():
-        load_weights(w_all, w, wsem, 0, range(4))
+        load_weights(w_all, w, wsem, 0, (0,))
         query_lanes, key_lanes = label_lanes(lens, parity, x.shape[1])
         lanes[0] = query_lanes
         lanes[1] = key_lanes
@@ -672,7 +685,7 @@
                 prm,
                 act,
                 None,
-                lambda place: wait_block(w, wsem, l, place),
+                lambda place: wait_part(w, wsem, l, place),
                 lambda point: load_ahead(w_all, w, wsem, l, point),
             )
             return carry
@@ -686,10 +699,10 @@
     return (
         [
             pltpu.VMEM((3, length, width), BF),
-            pltpu.VMEM((2, 12 * width, width), BF),
+            pltpu.VMEM((2, SHARDS, 12 * width // SHARDS, width), BF),
             pltpu.VMEM((2, PARAM_ROWS, width), F32),
             pltpu.VMEM((2, length, 128), BF),
-            pltpu.VMEM((4, length, width), BF),
+            pltpu.VMEM((length, 4 * width), BF),
         ]
         + extra
         + [
@@ -718,10 +731,10 @@
     smem = pl.BlockSpec(memory_space=pltpu.SMEM)
     vmem = pl.BlockSpec(memory_space=pltpu.VMEM)
     row = shape((length, width), BF)
-    outs = [shape((2, 12 * width, width), BF), row, row]
+    outs = [shape((2, SHARDS, 12 * width // SHARDS, width), BF), row, row]
     outs += [shape((2,) + dims, kind) for dims, kind in state_shapes(length, width)]
     scratch = common_scratch(
-        length, width, 2, [pltpu.SemaphoreType.DMA((2, PLACES)), pltpu.SemaphoreType.DMA((2, PLACES))]
+        length, width, 2, [pltpu.SemaphoreType.DMA((2, PARTS)), pltpu.SemaphoreType.DMA((2, PARTS))]
     )
     scratch[7] = pltpu.SemaphoreType.DMA
     return pl.pallas_call(
@@ -754,7 +767,7 @@
             length,
             width,
             2,
-            [pltpu.VMEM((2, length, width), BF), pltpu.SemaphoreType.DMA((2, PLACES))],
+            [pltpu.VMEM((2, length, width), BF), pltpu.SemaphoreType.DMA((2, PARTS))],
         ),
         compiler_params=pltpu.CompilerParams(vmem_limit_bytes=VMEM_BYTES),
         cost_estimate=layers_cost(length, width, 1, 1),
@@ -778,7 +791,7 @@
             length,
             width,
             2,
-            [pltpu.VMEM((2, length, width), BF), pltpu.SemaphoreType.DMA((2, PLACES))],
+            [pltpu.VMEM((2, length, width), BF), pltpu.SemaphoreType.DMA((2, PARTS))],
         ),
         compiler_params=pltpu.CompilerParams(vmem_limit_bytes=VMEM_BYTES),
         cost_estimate=layers_cost(length, width, 0, 1),

time: 393 us -> 386 us (0.982); the launches traced: 388 us -> 387 us
    pallas_call x1, Pallas kernels: 41.6 us -> 46.9 us  [run_middle(): pl.pallas_call(middle_kernel, out_shape=outs, in_specs=[smem, smem] + [an...]
    pallas_call x1, Pallas kernels: 44.1 us -> 40 us  [run_first(): pl.pallas_call(first_kernel, out_shape=outs, in_specs=[smem, smem, anywhe...]
  transfers between devices with their start and end apart: 42 -> 42, of which waited for: 21 -> 21; matrix products, arithmetic and copies ran while one was open for 1% -> 1% of each run, Pallas kernels for 12% -> 11%
where the time goes in v3:
time: 386 us; the launch traced here: 387 us
  waiting for transfers between devices  165 us (43%)
  Pallas kernels  133 us (34%)
  starting transfers between devices  76.3 us (20%)
  local copies, waits for them, and re-layouts  6.61 us (2%)
  other arithmetic  4.29 us (1%)
    ppermute x42, waiting for transfers between devices, permuted(): return lax.ppermute(array, AXES, pairs)  165 us
    ppermute x42, starting transfers between devices, permuted(): return lax.ppermute(array, AXES, pairs)  76.3 us
    pallas_call x1, Pallas kernels, run_middle(): pl.pallas_call(middle_kernel, out_shape=outs, in_specs=[smem, smem] + [an...  46.9 us
    pallas_call x1, Pallas kernels, run_last(): pl.pallas_call(last_kernel, out_shape=[rows, rows, row, shape((2, 16, wid...  42.7 us
    pallas_call x1, Pallas kernels, run_first(): pl.pallas_call(first_kernel, out_shape=outs, in_specs=[smem, smem, anywhe...  40 us
  transfers between devices with their start and end apart: 42, of which 21 were waited for; matrix products, arithmetic and copies ran while one was open for 1% of the time, Pallas kernels for 11%

profile of v3, /device:TPU:0, one launch (start us, length us, event | category | flops | bytes accessed | tf_op | source)
XLA Modules:
  0.0 386.7 jit_solution(5351391829290576959)
XLA Ops:
  1.8 3.4 pack.1
  5.2 2.9 collective-permute-start.2
  12.9 16.0 %collective-permute-done.2.refs_13_ = bf16[576,768]{1,0:T(8,128)(2,1)S(1)} collective-permute-done((bf16[576,768]{1,0:T(8,128)(2,1)}, bf16[576,768]{1,0:T(8,128)(2,1)S(1)}, u32[]{:S(2)}, u32[]{:S(2)}) %collective-permute-start.2) | collective-permute-done | bytes 884768 | tf_op jit(solution)/shard_map/ppermute | solution.py:848
  28.9 3.0 collective-permute-done.refs_5_
  33.3 14.5 %collective-permute-done.14.refs_12_ = bf16[576,768]{1,0:T(8,128)(2,1)S(1)} collective-permute-done((bf16[576,768]{1,0:T(8,128)(2,1)}, bf16[576,768]{1,0:T(8,128)(2,1)S(1)}, u32[]{:S(2)}, u32[]{:S(2)}) %collective-permute-start.14) | collective-permute-done | bytes 884768 | tf_op jit(solution)/shard_map/ppermute | solution.py:848
  47.8 3.0 collective-permute-done.8.refs_4_
  50.8 15.1 %collective-permute-done.3.refs_17_ = bf16[576,768]{1,0:T(8,128)(2,1)S(1)} collective-permute-done((bf16[576,768]{1,0:T(8,128)(2,1)S(1)}, bf16[576,768]{1,0:T(8,128)(2,1)S(1)}, u32[]{:S(2)}, u32[]{:S(2)}) %collective-permute-start.3) | collective-permute-done | bytes 884768 | tf_op jit(solution)/shard_map/ppermute | solution.py:848
  69.9 17.0 %collective-permute-done.17.refs_16_ = bf16[576,768]{1,0:T(8,128)(2,1)S(1)} collective-permute-done((bf16[576,768]{1,0:T(8,128)(2,1)S(1)}, bf16[576,768]{1,0:T(8,128)(2,1)S(1)}, u32[]{:S(2)}, u32[]{:S(2)}) %collective-permute-start.17) | collective-permute-done | bytes 884768 | tf_op jit(solution)/shard_map/ppermute | solution.py:848
  90.8 2.6 collective-permute-start.23
  94.1 14.2 %collective-permute-done.4.refs_21_ = bf16[576,768]{1,0:T(8,128)(2,1)} collective-permute-done((bf16[576,768]{1,0:T(8,128)(2,1)}, bf16[576,768]{1,0:T(8,128)(2,1)}, u32[]{:S(2)}, u32[]{:S(2)}) %collective-permute-start.4) | collective-permute-done | bytes 884768 | tf_op jit(solution)/shard_map/ppermute | solution.py:848
  110.5 3.4 collective-permute-start.27
  115.0 16.1 %collective-permute-done.20.refs_20_ = bf16[576,768]{1,0:T(8,128)(2,1)S(1)} collective-permute-done((bf16[576,768]{1,0:T(8,128)(2,1)}, bf16[576,768]{1,0:T(8,128)(2,1)S(1)}, u32[]{:S(2)}, u32[]{:S(2)}) %collective-permute-start.20) | collective-permute-done | bytes 884768 | tf_op jit(solution)/shard_map/ppermute | solution.py:848
  134.9 13.9 %collective-permute-done.5.theirs = f32[32,768]{1,0:T(8,128)S(1)} collective-permute-done((f32[32,768]{1,0:T(8,128)S(1)}, f32[32,768]{1,0:T(8,128)S(1)}, u32[]{:S(2)}, u32[]{:S(2)}) %collective-permute-start.5) | collective-permute-done | bytes 98336 | tf_op jit(solution)/shard_map/ppermute | solution.py:848
  149.4 3.1 collective-permute-done.28.refs_29_
  155.2 40.0 %first.1 = (bf16[2,8,1152,768]{3,2,1,0:T(8,128)(2,1)}, bf16[512,768]{1,0:T(8,128)(2,1)}, bf16[512,768]{1,0:T(8,128)(2,1)}, bf16[2,3,512,768]{3,2,1,0:T(8,128)(2,...) custom-call(s32[12]{0:T(128)} %fusion.scal, ...), custom_call_target="tpu_custom_call" | custom-call | flops 16106127360 | bytes 28311552 | tf_op jit(solution)/shard_map/first/pallas_call | solution.py:740
  196.6 17.7 %collective-permute-done.31.arrived = bf16[512,768]{1,0:T(8,128)(2,1)S(1)} collective-permute-done((bf16[512,768]{1,0:T(8,128)(2,1)}, bf16[512,768]{1,0:T(8,128)(2,1)S(1)}, u32[]{:S(2)}, u32[]{:S(2)}) %collective-permute-start.31) | collective-permute-done | bytes 786464 | tf_op jit(solution)/shard_map/ppermute | solution.py:848
  215.2 46.9 %middle.1 = (bf16[512,768]{1,0:T(8,128)(2,1)}, bf16[512,768]{1,0:T(8,128)(2,1)}, bf16[2,512,768]{2,1,0:T(8,128)(2,1)}, bf16[512,768]{1,0:T(8,128)(2,1)}, bf16[2,...) custom-call(s32[12]{0:T(128)} %fusion.scal, ...), custom_call_target="tpu_custom_call" | custom-call | flops 34628173824 | bytes 28311552 | tf_op jit(solution)/shard_map/middle/pallas_call | solution.py:761
  262.1 38.2 %collective-permute-start.32 = (bf16[512,768]{1,0:T(8,128)(2,1)}, bf16[512,768]{1,0:T(8,128)(2,1)S(1)}, u32[]{:S(2)}, u32[]{:S(2)}) collective-permute-start(bf16[512,768]{1,0:T(8,128)(2,1)} %get-tuple-element.56), channel_id=1, source_target_pairs={{0,16},{1,17},{2,18},{3,19},{4,20},{5,21},{6,22},{7,23},{8,24},{9,... | collective-permute-start | bytes 2359304 | tf_op jit(solution)/shard_map/ppermute | solution.py:848
  303.7 13.5 %collective-permute-done.32.arrived_up = bf16[512,768]{1,0:T(8,128)(2,1)S(1)} collective-permute-done((bf16[512,768]{1,0:T(8,128)(2,1)}, bf16[512,768]{1,0:T(8,128)(2,1)S(1)}, u32[]{:S(2)}, u32[]{:S(2)}) %collective-permute-start.32) | collective-permute-done | bytes 786464 | tf_op jit(solution)/shard_map/ppermute | solution.py:848
  317.2 4.2 %collective-permute-done.33.arrived_down = bf16[512,768]{1,0:T(8,128)(2,1)} collective-permute-done((bf16[512,768]{1,0:T(8,128)(2,1)}, bf16[512,768]{1,0:T(8,128)(2,1)}, u32[]{:S(2)}, u32[]{:S(2)}) %collective-permute-start.33) | collective-permute-done | bytes 786464 | tf_op jit(solution)/shard_map/ppermute | solution.py:848
  321.4 42.7 %last.1 = (bf16[2,512,768]{2,1,0:T(8,128)(2,1)}, bf16[2,512,768]{2,1,0:T(8,128)(2,1)}, bf16[512,768]{1,0:T(8,128)(2,1)}, f32[2,16,768]{2,1,0:T(8,128)}) custom-call(s32[12]{0:T(128)} %fusion.scal, s32[2,8]{1,0:T(2,128)} %lens.5, bf16[2,512,768]{2,1,0:T(8,128)(2,1)} %source.5, bf16[512,768]{1,0:T(8,128)(2,1)} %copy-done.28, ...), custom_call_target="tpu_custom_call" | custom-call | flops 18522046464 | bytes 28311552 | tf_op jit(solution)/shard_map/last/pallas_call | solution.py:785
  367.2 2.7 collective-permute-done.37
  377.2 2.8 collective-permute-done.40
  380.5 3.6 collective-permute-done.36
  (137 shorter events, 44.9 us)
Async XLA Ops:
  5.2 23.6 %collective-permute-start.2 = (bf16[576,768]{1,0:T(8,128)(2,1)}, bf16[576,768]{1,0:T(8,128)(2,1)S(1)}, u32[]{:S(2)}, u32[]{:S(2)}) collective-permute-start(bf16[576,768]{1,0:T(8,128)(2,1)} %get-tuple-element.41.refs_1_), channel_id=1, source_target_pairs={{0,8},{1,9},{2,10},{3,11},{4,12},{5,13},{6,14},{7,15},{8,0},{9,1},... | collective-permute-start | bytes 2654216 | tf_op jit(solution)/shard_map/ppermute | solution.py:848
  8.2 23.7 %collective-permute-start = (bf16[576,768]{1,0:T(8,128)(2,1)}, bf16[576,768]{1,0:T(8,128)(2,1)S(1)}, u32[]{:S(2)}, u32[]{:S(2)}) collective-permute-start(bf16[576,768]{1,0:T(8,128)(2,1)} %get-tuple-element.41.refs_1_), channel_id=1, source_target_pairs={{0,2},{1,3},{2,6},{3,7},{4,0},{5,1},{6,4},{7,5},{8,10},{9,11},{10,... | collective-permute-start | bytes 2654216 | tf_op jit(solution)/shard_map/ppermute | solution.py:848
  9.7 38.1 %collective-permute-start.14 = (bf16[576,768]{1,0:T(8,128)(2,1)}, bf16[576,768]{1,0:T(8,128)(2,1)S(1)}, u32[]{:S(2)}, u32[]{:S(2)}) collective-permute-start(bf16[576,768]{1,0:T(8,128)(2,1)} %get-tuple-element.45.refs_0_), channel_id=1, source_target_pairs={{0,8},{1,9},{2,10},{3,11},{4,12},{5,13},{6,14},{7,15},{8,0},{9,1},... | collective-permute-start | bytes 2654216 | tf_op jit(solution)/shard_map/ppermute | solution.py:848
  10.3 40.5 %collective-permute-start.8 = (bf16[576,768]{1,0:T(8,128)(2,1)}, bf16[576,768]{1,0:T(8,128)(2,1)S(1)}, u32[]{:S(2)}, u32[]{:S(2)}) collective-permute-start(bf16[576,768]{1,0:T(8,128)(2,1)} %get-tuple-element.45.refs_0_), channel_id=1, source_target_pairs={{0,2},{1,3},{2,6},{3,7},{4,0},{5,1},{6,4},{7,5},{8,10},{9,11},{10,... | collective-permute-start | bytes 2654216 | tf_op jit(solution)/shard_map/ppermute | solution.py:848
  31.9 34.1 %collective-permute-start.3 = (bf16[576,768]{1,0:T(8,128)(2,1)S(1)}, bf16[576,768]{1,0:T(8,128)(2,1)S(1)}, u32[]{:S(2)}, u32[]{:S(2)}) collective-permute-start(bf16[576,768]{1,0:T(8,128)(2,1)S(1)} %collective-permute-done.refs_5_), channel_id=1, source_target_pairs={{0,8},{1,9},{2,10},{3,11},{4,12},{5,13},{6,14},{7,15},{8,0},{9,1},... | collective-permute-start | bytes 2654216 | tf_op jit(solution)/shard_map/ppermute | solution.py:848
  32.1 36.4 %collective-permute-start.1 = (bf16[576,768]{1,0:T(8,128)(2,1)S(1)}, bf16[576,768]{1,0:T(8,128)(2,1)}, u32[]{:S(2)}, u32[]{:S(2)}) collective-permute-start(bf16[576,768]{1,0:T(8,128)(2,1)S(1)} %collective-permute-done.refs_5_), channel_id=1, source_target_pairs={{0,2},{1,3},{2,6},{3,7},{4,0},{5,1},{6,4},{7,5},{8,10},{9,11},{10,... | collective-permute-start | bytes 2654216 | tf_op jit(solution)/shard_map/ppermute | solution.py:848
  33.3 36.0 %collective-permute-start.7 = (bf16[576,768]{1,0:T(8,128)(2,1)}, bf16[576,768]{1,0:T(8,128)(2,1)S(1)}, u32[]{:S(2)}, u32[]{:S(2)}) collective-permute-start(bf16[576,768]{1,0:T(8,128)(2,1)} %get-tuple-element.41.refs_1_), channel_id=1, source_target_pairs={{0,1},{1,0},{2,3},{3,2},{4,5},{5,4},{6,7},{7,6},{8,9},{9,8},{10,11... | collective-permute-start | bytes 2654216 | tf_op jit(solution)/shard_map/ppermute | solution.py:848
  47.8 21.5 %collective-permute-start.6 = (bf16[576,768]{1,0:T(8,128)(2,1)}, bf16[576,768]{1,0:T(8,128)(2,1)S(1)}, u32[]{:S(2)}, u32[]{:S(2)}) collective-permute-start(bf16[576,768]{1,0:T(8,128)(2,1)} %get-tuple-element.45.refs_0_), channel_id=1, source_target_pairs={{0,1},{1,0},{2,3},{3,2},{4,5},{5,4},{6,7},{7,6},{8,9},{9,8},{10,11... | collective-permute-start | bytes 2654216 | tf_op jit(solution)/shard_map/ppermute | solution.py:848
  65.9 20.9 %collective-permute-start.17 = (bf16[576,768]{1,0:T(8,128)(2,1)S(1)}, bf16[576,768]{1,0:T(8,128)(2,1)S(1)}, u32[]{:S(2)}, u32[]{:S(2)}) collective-permute-start(bf16[576,768]{1,0:T(8,128)(2,1)S(1)} %collective-permute-done.8.refs_4_), channel_id=1, source_target_pairs={{0,8},{1,9},{2,10},{3,11},{4,12},{5,13},{6,14},{7,15},{8,0},{9,1},... | collective-permute-start | bytes 2654216 | tf_op jit(solution)/shard_map/ppermute | solution.py:848
  68.4 22.4 %collective-permute-start.11 = (bf16[576,768]{1,0:T(8,128)(2,1)S(1)}, bf16[576,768]{1,0:T(8,128)(2,1)}, u32[]{:S(2)}, u32[]{:S(2)}) collective-permute-start(bf16[576,768]{1,0:T(8,128)(2,1)S(1)} %collective-permute-done.8.refs_4_), channel_id=1, source_target_pairs={{0,2},{1,3},{2,6},{3,7},{4,0},{5,1},{6,4},{7,5},{8,10},{9,11},{10,... | collective-permute-start | bytes 2654216 | tf_op jit(solution)/shard_map/ppermute | solution.py:848
  69.3 24.2 %collective-permute-start.10 = (bf16[576,768]{1,0:T(8,128)(2,1)S(1)}, bf16[576,768]{1,0:T(8,128)(2,1)}, u32[]{:S(2)}, u32[]{:S(2)}) collective-permute-start(bf16[576,768]{1,0:T(8,128)(2,1)S(1)} %collective-permute-done.refs_5_), channel_id=1, source_target_pairs={{0,1},{1,0},{2,3},{3,2},{4,5},{5,4},{6,7},{7,6},{8,9},{9,8},{10,11... | collective-permute-start | bytes 2654216 | tf_op jit(solution)/shard_map/ppermute | solution.py:848
  69.3 24.2 %collective-permute-start.15 = (bf16[576,768]{1,0:T(8,128)(2,1)S(1)}, bf16[576,768]{1,0:T(8,128)(2,1)}, u32[]{:S(2)}, u32[]{:S(2)}) collective-permute-start(bf16[576,768]{1,0:T(8,128)(2,1)S(1)} %collective-permute-done.14.refs_12_), channel_id=1, source_target_pairs={{0,1},{1,0},{2,3},{3,2},{4,5},{5,4},{6,7},{7,6},{8,9},{9,8},{10,11... | collective-permute-start | bytes 2654216 | tf_op jit(solution)/shard_map/ppermute | solution.py:848
  69.8 24.2 %collective-permute-start.9 = (bf16[576,768]{1,0:T(8,128)(2,1)S(1)}, bf16[576,768]{1,0:T(8,128)(2,1)}, u32[]{:S(2)}, u32[]{:S(2)}) collective-permute-start(bf16[576,768]{1,0:T(8,128)(2,1)S(1)} %collective-permute-done.8.refs_4_), channel_id=1, source_target_pairs={{0,1},{1,0},{2,3},{3,2},{4,5},{5,4},{6,7},{7,6},{8,9},{9,8},{10,11... | collective-permute-start | bytes 2654216 | tf_op jit(solution)/shard_map/ppermute | solution.py:848
  93.5 20.5 %collective-permute-start.13 = (bf16[576,768]{1,0:T(8,128)(2,1)}, bf16[576,768]{1,0:T(8,128)(2,1)S(1)}, u32[]{:S(2)}, u32[]{:S(2)}) collective-permute-start(bf16[576,768]{1,0:T(8,128)(2,1)} %collective-permute-done.1.refs_9_), channel_id=1, source_target_pairs={{0,1},{1,0},{2,3},{3,2},{4,5},{5,4},{6,7},{7,6},{8,9},{9,8},{10,11... | collective-permute-start | bytes 2654216 | tf_op jit(solution)/shard_map/ppermute | solution.py:848
  108.3 22.8 %collective-permute-start.20 = (bf16[576,768]{1,0:T(8,128)(2,1)}, bf16[576,768]{1,0:T(8,128)(2,1)S(1)}, u32[]{:S(2)}, u32[]{:S(2)}) collective-permute-start(bf16[576,768]{1,0:T(8,128)(2,1)} %collective-permute-done.11.refs_8_), channel_id=1, source_target_pairs={{0,8},{1,9},{2,10},{3,11},{4,12},{5,13},{6,14},{7,15},{8,0},{9,1},... | collective-permute-start | bytes 2654216 | tf_op jit(solution)/shard_map/ppermute | solution.py:848
  110.5 22.8 %collective-permute-start.12 = (bf16[576,768]{1,0:T(8,128)(2,1)}, bf16[576,768]{1,0:T(8,128)(2,1)S(1)}, u32[]{:S(2)}, u32[]{:S(2)}) collective-permute-start(bf16[576,768]{1,0:T(8,128)(2,1)} %collective-permute-done.11.refs_8_), channel_id=1, source_target_pairs={{0,1},{1,0},{2,3},{3,2},{4,5},{5,4},{6,7},{7,6},{8,9},{9,8},{10,11... | collective-permute-start | bytes 2654216 | tf_op jit(solution)/shard_map/ppermute | solution.py:848
  110.5 24.3 %collective-permute-start.27 = (bf16[576,768]{1,0:T(8,128)(2,1)S(1)}, bf16[576,768]{1,0:T(8,128)(2,1)S(1)}, u32[]{:S(2)}, u32[]{:S(2)}) collective-permute-start(bf16[576,768]{1,0:T(8,128)(2,1)S(1)} %get-tuple-element.50), channel_id=1, source_target_pairs={{0,4},{1,5},{2,0},{3,1},{4,6},{5,7},{6,2},{7,3},{8,12},{9,13},{10,... | collective-permute-start | bytes 2654216 | tf_op jit(solution)/shard_map/ppermute | solution.py:848
  114.0 34.8 %collective-permute-start.22 = (bf16[576,768]{1,0:T(8,128)(2,1)}, bf16[576,768]{1,0:T(8,128)(2,1)S(1)}, u32[]{:S(2)}, u32[]{:S(2)}) collective-permute-start(bf16[576,768]{1,0:T(8,128)(2,1)} %collective-permute-done.4.refs_21_), channel_id=1, source_target_pairs={{0,1},{1,0},{2,3},{3,2},{4,5},{5,4},{6,7},{7,6},{8,9},{9,8},{10,11... | collective-permute-start | bytes 2654216 | tf_op jit(solution)/shard_map/ppermute | solution.py:848
  114.2 35.1 %collective-permute-start.25 = (bf16[576,768]{1,0:T(8,128)(2,1)S(1)}, bf16[576,768]{1,0:T(8,128)(2,1)S(1)}, u32[]{:S(2)}, u32[]{:S(2)}) collective-permute-start(bf16[576,768]{1,0:T(8,128)(2,1)S(1)} %collective-permute-done.23.refs_24_), channel_id=1, source_target_pairs={{0,8},{1,9},{2,10},{3,11},{4,12},{5,13},{6,14},{7,15},{8,0},{9,1},... | collective-permute-start | bytes 2654216 | tf_op jit(solution)/shard_map/ppermute | solution.py:848
  131.1 21.4 %collective-permute-start.28 = (bf16[576,768]{1,0:T(8,128)(2,1)S(1)}, bf16[576,768]{1,0:T(8,128)(2,1)S(1)}, u32[]{:S(2)}, u32[]{:S(2)}) collective-permute-start(bf16[576,768]{1,0:T(8,128)(2,1)S(1)} %get-tuple-element.51), channel_id=1, source_target_pairs={{0,4},{1,5},{2,0},{3,1},{4,6},{5,7},{6,2},{7,3},{8,12},{9,13},{10,... | collective-permute-start | bytes 2654216 | tf_op jit(solution)/shard_map/ppermute | solution.py:848
  262.1 55.1 %collective-permute-start.32 = (bf16[512,768]{1,0:T(8,128)(2,1)}, bf16[512,768]{1,0:T(8,128)(2,1)S(1)}, u32[]{:S(2)}, u32[]{:S(2)}) collective-permute-start(bf16[512,768]{1,0:T(8,128)(2,1)} %get-tuple-element.56), channel_id=1, source_target_pairs={{0,16},{1,17},{2,18},{3,19},{4,20},{5,21},{6,22},{7,23},{8,24},{9,... | collective-permute-start | bytes 2359304 | tf_op jit(solution)/shard_map/ppermute | solution.py:848
  300.3 21.1 %collective-permute-start.33 = (bf16[512,768]{1,0:T(8,128)(2,1)}, bf16[512,768]{1,0:T(8,128)(2,1)}, u32[]{:S(2)}, u32[]{:S(2)}) collective-permute-start(bf16[512,768]{1,0:T(8,128)(2,1)} %get-tuple-element.57), channel_id=1, source_target_pairs={{16,0},{17,1},{18,2},{19,3},{20,4},{21,5},{22,6},{23,7},{24,8},{25... | collective-permute-start | bytes 2359304 | tf_op jit(solution)/shard_map/ppermute | solution.py:848
  301.6 62.5 %collective-permute-start.34 = (bf16[512,768]{1,0:T(8,128)(2,1)}, bf16[512,768]{1,0:T(8,128)(2,1)S(1)}, u32[]{:S(2)}, u32[]{:S(2)}) collective-permute-start(bf16[512,768]{1,0:T(8,128)(2,1)} %get-tuple-element.67), channel_id=1, source_target_pairs={{0,8},{1,9},{2,10},{3,11},{4,12},{5,13},{6,14},{7,15},{8,0},{9,1},... | collective-permute-start | bytes 2359304 | tf_op jit(solution)/shard_map/ppermute | solution.py:848
  302.2 61.9 %collective-permute-start.35 = (bf16[512,768]{1,0:T(8,128)(2,1)}, bf16[512,768]{1,0:T(8,128)(2,1)S(1)}, u32[]{:S(2)}, u32[]{:S(2)}) collective-permute-start(bf16[512,768]{1,0:T(8,128)(2,1)} %get-tuple-element.68), channel_id=1, source_target_pairs={{0,8},{1,9},{2,10},{3,11},{4,12},{5,13},{6,14},{7,15},{8,0},{9,1},... | collective-permute-start | bytes 2359304 | tf_op jit(solution)/shard_map/ppermute | solution.py:848
  (50 other events, 848.2 us)

commit v4 on v3

--- a/solution.py
+++ b/solution.py
@@ -242,7 +242,7 @@
     after("end")
 
 
-def backward_layer(l, c_in, c_out, x, w, prm, d_qkv, d_up, state, ready, have, spent, after):
+def backward_layer(l, c_in, c_out, x, w, prm, d_qkv, d_up, state, ready, have, spent, after, together=False):
     qkv, shares, mixed, n, gp, r = state
     length, width = x.shape[1:]
     lane = lax.broadcasted_iota(jnp.int32, (1, 128), 1)
@@ -269,9 +269,12 @@
     d_mixed = dot(d_summed.astype(BF), rows_of(w, l, 3), 1, 1).astype(BF)
     have("mixed")
     have("qkv")
+    if together:
+        for quad in range(3):
+            have(quad)
     low = lane < 64
     for pair in range(width // 128):
-        if pair % 2 == 0:
+        if pair % 2 == 0 and not together:
             have(pair // 2)
         lanes = slice(128 * pair, 128 * pair + 128)
         query, keys, values = qkv[0, :, lanes], qkv[1, :, lanes], qkv[2, :, lanes]
@@ -292,10 +295,10 @@
         d_qkv[:, lanes] = (d_query * 0.125).astype(BF)
         d_qkv[:, width + 128 * pair : width + 128 * pair + 128] = (d_keys * 0.125).astype(BF).T
         d_qkv[:, 2 * width + 128 * pair : 2 * width + 128 * pair + 128] = d_values.astype(BF).T
-        if pair % 2:
+        if pair % 2 and not together:
             spent(pair // 2)
             after(pair // 2)
-    for part in ("r", "mixed", "qkv"):
+    for part in ("r", "mixed", "qkv") + ((0, 1, 2) if together else ()):
         spent(part)
     have("x")
     down = dot(x[l], prm[l, 12:28, :].astype(BF), 1, 1).astype(BF)
@@ -396,23 +399,18 @@
 
             waits = save_calls(state, kept, ssem, l)
 
-            def ahead(places, own):
-                for i in range(2):
-                    if own or i == 0:
-
-                        @pl.when(l == i)
-                        def _():
-                            for place in places:
-                                start_part(scal, pieces, w, wsem, i if own else 1, place)
-
             def after(point):
                 waits(point)
-                if point in OWN_AHEAD:
-                    ahead(OWN_AHEAD[point], True)
-                if point in NEXT_AHEAD:
-                    ahead(NEXT_AHEAD[point], False)
-                for place in OUT_AT.get(point, ()):
-                    out_copy(l, place).start()
+                for layer, loads, outs in ((0, FIRST_LOADS, FIRST_OUTS), (1, SECOND_LOADS, SECOND_OUTS)):
+                    if point in loads or point in outs:
+
+                        @pl.when(l == layer)
+                        def _():
+                            for to, part in loads.get(point, ()):
+                                start_part(scal, pieces, w, wsem, to, part)
+                            for part in outs.get(point, ()):
+                                out_copy(layer, part).start()
+
                 for part in BATCHES.get(point, ()):
                     state_copy(state, kept, ssem, l, part, False).start()
 
@@ -438,7 +436,10 @@
 
 OWN_AHEAD = {"begin": (1,), 1: (2,)}
 NEXT_AHEAD = {"attended": (0,)}
-OUT_AT = {0: (0,), "attended": (1,), "inner": (2,)}
+FIRST_LOADS = {"begin": ((0, 1),), 1: ((0, 2),), "attended": ((1, 0),), "inner": ((1, 1),)}
+SECOND_LOADS = {"begin": ((1, 2),)}
+FIRST_OUTS = {0: (0,), "attended": (1,), "inner": (2,)}
+SECOND_OUTS = {0: (0,), 1: (1,), "attended": (2,)}
 
 
 def load_weights(w_all, w, wsem, l, places):
@@ -457,8 +458,8 @@
 
 
 def middle_kernel(scal, lens, source, arrived, cotangent, early_first, early_second, mine, theirs, w_all, *refs):
-    hop_up, hop_down, acts, acts_other, second, second_other, d_up = refs[:7]
-    kept, refs = refs[7:13], refs[13:]
+    hop, acts, acts_other, second, second_other, d_up = refs[:6]
+    kept, refs = refs[6:12], refs[12:]
     x, w, prm, lanes, act, c, wsem, xsem, hsem, ssem = refs[:10]
     state = refs[10:]
     parity, stage = scal[PARITY], scal[STAGE]
@@ -531,7 +532,7 @@
 
     @pl.when(stage == 0)
     def _():
-        up = pltpu.make_async_copy(x.at[2], hop_up, xsem.at[0])
+        up = pltpu.make_async_copy(x.at[2], hop, xsem.at[0])
         up.start()
         placed(x.at[1], x.at[2], second, second_other, 2)
         up.wait()
@@ -556,12 +557,12 @@
                     state_copy(state, kept, ssem, 0, part, True).start()
 
             backward_layer(
-                l, c.at[i], c.at[1 - i], x, w, prm, act, d_up, state, lambda place: None, have, spent, lambda point: None
+                l, c.at[i], c.at[1 - i], x, w, prm, act, d_up, state, lambda place: None, have, spent, lambda point: None, True
             )
             return carry
 
         lax.fori_loop(0, 2, gradient, 0)
-        down = pltpu.make_async_copy(c.at[0], hop_down, xsem.at[0])
+        down = pltpu.make_async_copy(c.at[0], hop, xsem.at[0])
         down.start()
         placed(c.at[0], c.at[1], second, second_other, 2)
         down.wait()
@@ -570,7 +571,7 @@
     placed_wait(second, second_other, 2)
 
 
-def last_kernel(scal, lens, source, arrived_up, arrived_down, early_first, second, mine, theirs, w_all, *refs):
+def last_kernel(scal, lens, source, arrived, early_first, second, mine, theirs, w_all, *refs):
     kept, refs = refs[:6], refs[6:]
     joined, grads, other, d_up = refs[:4]
     x, w, prm, lanes, act, c, wsem, xsem, hsem, ssem = refs[4:14]
@@ -605,7 +606,7 @@
         def load(l, part):
             return state_copy(state, kept, ssem, l, part, True)
 
-        cot = pltpu.make_async_copy(arrived_down, c.at[0], xsem.at[0])
+        cot = pltpu.make_async_copy(arrived, c.at[0], xsem.at[0])
         start_x = pltpu.make_async_copy(source.at[parity], x.at[0], xsem.at[1])
         middle_x = pltpu.make_async_copy(early_first, x.at[1], xsem.at[2])
         cot.start()
@@ -669,7 +670,7 @@
         query_lanes, key_lanes = label_lanes(lens, parity, x.shape[1])
         lanes[0] = query_lanes
         lanes[1] = key_lanes
-        copy = pltpu.make_async_copy(arrived_up, x.at[0], xsem.at[0])
+        copy = pltpu.make_async_copy(arrived, x.at[0], xsem.at[0])
         copy.start()
         copy.wait()
         carry_in(c.at[0]).start()
@@ -756,13 +757,13 @@
     smem = pl.BlockSpec(memory_space=pltpu.SMEM)
     vmem = pl.BlockSpec(memory_space=pltpu.VMEM)
     row, rows = shape((length, width), BF), shape((2, length, width), BF)
-    outs = [row, row, rows, row, rows, row, shape((2, 16, width), F32)]
+    outs = [row, rows, row, rows, row, shape((2, 16, width), F32)]
     outs += [shape((1,) + dims, kind) for dims, kind in state_shapes(length, width)]
     return pl.pallas_call(
         middle_kernel,
         out_shape=outs,
         in_specs=[smem, smem] + [anywhere] * 5 + [vmem, vmem, anywhere],
-        out_specs=[anywhere] * 6 + [vmem] + [anywhere] * 6,
+        out_specs=[anywhere] * 5 + [vmem] + [anywhere] * 6,
         scratch_shapes=common_scratch(
             length,
             width,
@@ -775,7 +776,7 @@
     )(scal, lens, source, arrived, cotangent, early_first, early_second, mine, theirs, w_all)
 
 
-def run_last(scal, lens, source, arrived_up, arrived_down, early_first, second, mine, theirs, w_all, kept):
+def run_last(scal, lens, source, arrived, early_first, second, mine, theirs, w_all, kept):
     _, length, width = source.shape
     shape = jax.ShapeDtypeStruct
     anywhere = pl.BlockSpec(memory_space=pl.ANY)
@@ -785,7 +786,7 @@
     return pl.pallas_call(
         last_kernel,
         out_shape=[rows, rows, row, shape((2, 16, width), F32)],
-        in_specs=[smem, smem] + [anywhere] * 5 + [vmem, vmem] + [anywhere] * 7,
+        in_specs=[smem, smem] + [anywhere] * 4 + [vmem, vmem] + [anywhere] * 7,
         out_specs=[anywhere] * 3 + [vmem],
         scratch_shapes=common_scratch(
             length,
@@ -796,7 +797,7 @@
         compiler_params=pltpu.CompilerParams(vmem_limit_bytes=VMEM_BYTES),
         cost_estimate=layers_cost(length, width, 0, 1),
         name="last",
-    )(scal, lens, source, arrived_up, arrived_down, early_first, second, mine, theirs, w_all, *kept)
+    )(scal, lens, source, arrived, early_first, second, mine, theirs, w_all, *kept)
 
 
 def tables(sections, copies):
@@ -854,7 +855,7 @@
     other_side = lambda s, q: (s, q ^ 1)
     partner = lambda s, q: (s ^ 1, q)
     upward = lambda s, q: (s + 2, q) if s < 2 else None
-    downward = lambda s, q: (s - 2, q) if s >= 2 else None
+    across_y = lambda s, q: (s ^ 2, q)
 
     w_in, w_out, w_up, w_down = (
         attention_in_weight[0],
@@ -913,7 +914,7 @@
     lens = packed_segment_lengths
     w_all, early_first, early_second, *kept = run_first(scal, lens, inputs, mine, theirs, pieces)
     arrived = permuted(early_second, upward)
-    hop_up, hop_down, acts, acts_other, second, second_other, d_up_late, *_ = run_middle(
+    hop, acts, acts_other, second, second_other, d_up_late, *_ = run_middle(
         scal,
         lens,
         evaluation_input,
@@ -925,12 +926,11 @@
         theirs,
         w_all,
     )
-    arrived_down = permuted(hop_down, downward)
-    arrived_up = permuted(hop_up, upward)
+    passed_on = permuted(hop, across_y)
     acts_row = permuted(acts_other, partner)
     second_row = permuted(second_other, partner)
     joined, grads, last_other, d_up_early = run_last(
-        scal, lens, inputs, arrived_up, arrived_down, early_first, second, mine, theirs, w_all, kept
+        scal, lens, inputs, passed_on, early_first, second, mine, theirs, w_all, kept
     )
     last_other, d_up_early, acts_row, second_row = lax.optimization_barrier(
         (last_other, d_up_early, acts_row, second_row)

time: 386 us -> 379 us (0.982)
  starting transfers between devices: 76.3 us -> 71.2 us
    ppermute x42 -> x41, starting transfers between devices: 76.3 us -> 71.2 us  [permuted(): return lax.ppermute(array, AXES, pairs)]
    ppermute x42 -> x41, waiting for transfers between devices: 165 us -> 164 us  [permuted(): return lax.ppermute(array, AXES, pairs)]
  transfers between devices with their start and end apart: 42 -> 41, of which waited for: 21 -> 20; matrix products, arithmetic and copies ran while one was open for 1% -> 1% of each run, Pallas kernels for 11% -> 11%
where the time goes in v4:
time: 379 us; the launch traced here: 380 us
  waiting for transfers between devices  164 us (43%)
  Pallas kernels  132 us (35%)
  starting transfers between devices  71.2 us (19%)
  local copies, waits for them, and re-layouts  7.46 us (2%)
  other arithmetic  4.29 us (1%)
    ppermute x41, waiting for transfers between devices, permuted(): return lax.ppermute(array, AXES, pairs)  164 us
    ppermute x41, starting transfers between devices, permuted(): return lax.ppermute(array, AXES, pairs)  71.2 us
    pallas_call x1, Pallas kernels, run_middle(): pl.pallas_call(middle_kernel, out_shape=outs, in_specs=[smem, smem] + [an...  46.8 us
    pallas_call x1, Pallas kernels, run_last(): pl.pallas_call(last_kernel, out_shape=[rows, rows, row, shape((2, 16, wid...  42.7 us
    pallas_call x1, Pallas kernels, run_first(): pl.pallas_call(first_kernel, out_shape=outs, in_specs=[smem, smem, anywhe...  38.8 us
  transfers between devices with their start and end apart: 41, of which 20 were waited for; matrix products, arithmetic and copies ran while one was open for 1% of the time, Pallas kernels for 11%

profile of v4, /device:TPU:0, one launch (start us, length us, event | category | flops | bytes accessed | tf_op | source)
XLA Modules:
  0.0 379.7 jit_solution(15115659420560874412)
XLA Ops:
  1.8 3.4 pack.1
  5.2 2.9 collective-permute-start.2
  10.3 2.6 collective-permute-start.8
  12.9 16.0 %collective-permute-done.2.refs_13_ = bf16[576,768]{1,0:T(8,128)(2,1)S(1)} collective-permute-done((bf16[576,768]{1,0:T(8,128)(2,1)}, bf16[576,768]{1,0:T(8,128)(2,1)S(1)}, u32[]{:S(2)}, u32[]{:S(2)}) %collective-permute-start.2) | collective-permute-done | bytes 884768 | tf_op jit(solution)/shard_map/ppermute | solution.py:849
  28.9 3.0 collective-permute-done.refs_5_
  33.3 14.5 %collective-permute-done.14.refs_12_ = bf16[576,768]{1,0:T(8,128)(2,1)S(1)} collective-permute-done((bf16[576,768]{1,0:T(8,128)(2,1)}, bf16[576,768]{1,0:T(8,128)(2,1)S(1)}, u32[]{:S(2)}, u32[]{:S(2)}) %collective-permute-start.14) | collective-permute-done | bytes 884768 | tf_op jit(solution)/shard_map/ppermute | solution.py:849
  47.8 3.0 collective-permute-done.8.refs_4_
  50.8 15.1 %collective-permute-done.3.refs_17_ = bf16[576,768]{1,0:T(8,128)(2,1)S(1)} collective-permute-done((bf16[576,768]{1,0:T(8,128)(2,1)S(1)}, bf16[576,768]{1,0:T(8,128)(2,1)S(1)}, u32[]{:S(2)}, u32[]{:S(2)}) %collective-permute-start.3) | collective-permute-done | bytes 884768 | tf_op jit(solution)/shard_map/ppermute | solution.py:849
  69.9 17.0 %collective-permute-done.17.refs_16_ = bf16[576,768]{1,0:T(8,128)(2,1)S(1)} collective-permute-done((bf16[576,768]{1,0:T(8,128)(2,1)S(1)}, bf16[576,768]{1,0:T(8,128)(2,1)S(1)}, u32[]{:S(2)}, u32[]{:S(2)}) %collective-permute-start.17) | collective-permute-done | bytes 884768 | tf_op jit(solution)/shard_map/ppermute | solution.py:849
  90.8 2.6 collective-permute-start.23
  94.1 14.2 %collective-permute-done.4.refs_21_ = bf16[576,768]{1,0:T(8,128)(2,1)} collective-permute-done((bf16[576,768]{1,0:T(8,128)(2,1)}, bf16[576,768]{1,0:T(8,128)(2,1)}, u32[]{:S(2)}, u32[]{:S(2)}) %collective-permute-start.4) | collective-permute-done | bytes 884768 | tf_op jit(solution)/shard_map/ppermute | solution.py:849
  110.5 3.4 collective-permute-start.27
  115.0 16.1 %collective-permute-done.20.refs_20_ = bf16[576,768]{1,0:T(8,128)(2,1)S(1)} collective-permute-done((bf16[576,768]{1,0:T(8,128)(2,1)}, bf16[576,768]{1,0:T(8,128)(2,1)S(1)}, u32[]{:S(2)}, u32[]{:S(2)}) %collective-permute-start.20) | collective-permute-done | bytes 884768 | tf_op jit(solution)/shard_map/ppermute | solution.py:849
  134.9 13.9 %collective-permute-done.5.theirs = f32[32,768]{1,0:T(8,128)S(1)} collective-permute-done((f32[32,768]{1,0:T(8,128)S(1)}, f32[32,768]{1,0:T(8,128)S(1)}, u32[]{:S(2)}, u32[]{:S(2)}) %collective-permute-start.5) | collective-permute-done | bytes 98336 | tf_op jit(solution)/shard_map/ppermute | solution.py:849
  149.4 3.1 collective-permute-done.28.refs_29_
  155.2 38.8 %first.1 = (bf16[2,8,1152,768]{3,2,1,0:T(8,128)(2,1)}, bf16[512,768]{1,0:T(8,128)(2,1)}, bf16[512,768]{1,0:T(8,128)(2,1)}, bf16[2,3,512,768]{3,2,1,0:T(8,128)(2,...) custom-call(s32[12]{0:T(128)} %fusion.scal, ...), custom_call_target="tpu_custom_call" | custom-call | flops 16106127360 | bytes 28311552 | tf_op jit(solution)/shard_map/first/pallas_call | solution.py:741
  195.3 17.7 %collective-permute-done.31.arrived = bf16[512,768]{1,0:T(8,128)(2,1)S(1)} collective-permute-done((bf16[512,768]{1,0:T(8,128)(2,1)}, bf16[512,768]{1,0:T(8,128)(2,1)S(1)}, u32[]{:S(2)}, u32[]{:S(2)}) %collective-permute-start.31) | collective-permute-done | bytes 786464 | tf_op jit(solution)/shard_map/ppermute | solution.py:849
  213.9 46.8 %middle.1 = (bf16[512,768]{1,0:T(8,128)(2,1)}, bf16[2,512,768]{2,1,0:T(8,128)(2,1)}, bf16[512,768]{1,0:T(8,128)(2,1)}, bf16[2,512,768]{2,1,0:T(8,128)(2,1)}, bf1...) custom-call(s32[12]{0:T(128)} %fusion.scal, ...), custom_call_target="tpu_custom_call" | custom-call | flops 34628173824 | bytes 28311552 | tf_op jit(solution)/shard_map/middle/pallas_call | solution.py:762
  260.8 34.4 %collective-permute-start.32 = (bf16[512,768]{1,0:T(8,128)(2,1)}, bf16[512,768]{1,0:T(8,128)(2,1)S(1)}, u32[]{:S(2)}, u32[]{:S(2)}) collective-permute-start(bf16[512,768]{1,0:T(8,128)(2,1)} %get-tuple-element.55), channel_id=1, source_target_pairs={{0,16},{1,17},{2,18},{3,19},{4,20},{5,21},{6,22},{7,23},{8,24},{9,... | collective-permute-start | bytes 2359304 | tf_op jit(solution)/shard_map/ppermute | solution.py:849
  297.2 15.6 %collective-permute-done.32.arrived = bf16[512,768]{1,0:T(8,128)(2,1)S(1)} collective-permute-done((bf16[512,768]{1,0:T(8,128)(2,1)}, bf16[512,768]{1,0:T(8,128)(2,1)S(1)}, u32[]{:S(2)}, u32[]{:S(2)}) %collective-permute-start.32) | collective-permute-done | bytes 786464 | tf_op jit(solution)/shard_map/ppermute | solution.py:849
  313.7 42.7 %last.1 = (bf16[2,512,768]{2,1,0:T(8,128)(2,1)}, bf16[2,512,768]{2,1,0:T(8,128)(2,1)}, bf16[512,768]{1,0:T(8,128)(2,1)}, f32[2,16,768]{2,1,0:T(8,128)}) custom-call(s32[12]{0:T(128)} %fusion.scal, s32[2,8]{1,0:T(2,128)} %lens.5, bf16[2,512,768]{2,1,0:T(8,128)(2,1)} %source.5, bf16[512,768]{1,0:T(8,128)(2,1)} %copy-done.28, ...), custom_call_target="tpu_custom_call" | custom-call | flops 18522046464 | bytes 28311552 | tf_op jit(solution)/shard_map/last/pallas_call | solution.py:786
  359.5 2.6 collective-permute-done.36
  369.4 2.7 collective-permute-done.39
  372.8 4.4 %collective-permute-done.35 = bf16[512,768]{1,0:T(8,128)(2,1)S(1)} collective-permute-done((bf16[512,768]{1,0:T(8,128)(2,1)}, bf16[512,768]{1,0:T(8,128)(2,1)S(1)}, u32[]{:S(2)}, u32[]{:S(2)}) %collective-permute-start.35) | collective-permute-done | bytes 786464 | tf_op jit(solution)/shard_map/ppermute | solution.py:849
  (135 shorter events, 41.8 us)
Async XLA Ops:
  5.2 23.6 %collective-permute-start.2 = (bf16[576,768]{1,0:T(8,128)(2,1)}, bf16[576,768]{1,0:T(8,128)(2,1)S(1)}, u32[]{:S(2)}, u32[]{:S(2)}) collective-permute-start(bf16[576,768]{1,0:T(8,128)(2,1)} %get-tuple-element.40.refs_1_), channel_id=1, source_target_pairs={{0,8},{1,9},{2,10},{3,11},{4,12},{5,13},{6,14},{7,15},{8,0},{9,1},... | collective-permute-start | bytes 2654216 | tf_op jit(solution)/shard_map/ppermute | solution.py:849
  8.2 23.7 %collective-permute-start = (bf16[576,768]{1,0:T(8,128)(2,1)}, bf16[576,768]{1,0:T(8,128)(2,1)S(1)}, u32[]{:S(2)}, u32[]{:S(2)}) collective-permute-start(bf16[576,768]{1,0:T(8,128)(2,1)} %get-tuple-element.40.refs_1_), channel_id=1, source_target_pairs={{0,2},{1,3},{2,6},{3,7},{4,0},{5,1},{6,4},{7,5},{8,10},{9,11},{10,... | collective-permute-start | bytes 2654216 | tf_op jit(solution)/shard_map/ppermute | solution.py:849
  9.8 38.1 %collective-permute-start.14 = (bf16[576,768]{1,0:T(8,128)(2,1)}, bf16[576,768]{1,0:T(8,128)(2,1)S(1)}, u32[]{:S(2)}, u32[]{:S(2)}) collective-permute-start(bf16[576,768]{1,0:T(8,128)(2,1)} %get-tuple-element.44.refs_0_), channel_id=1, source_target_pairs={{0,8},{1,9},{2,10},{3,11},{4,12},{5,13},{6,14},{7,15},{8,0},{9,1},... | collective-permute-start | bytes 2654216 | tf_op jit(solution)/shard_map/ppermute | solution.py:849
  10.3 40.5 %collective-permute-start.8 = (bf16[576,768]{1,0:T(8,128)(2,1)}, bf16[576,768]{1,0:T(8,128)(2,1)S(1)}, u32[]{:S(2)}, u32[]{:S(2)}) collective-permute-start(bf16[576,768]{1,0:T(8,128)(2,1)} %get-tuple-element.44.refs_0_), channel_id=1, source_target_pairs={{0,2},{1,3},{2,6},{3,7},{4,0},{5,1},{6,4},{7,5},{8,10},{9,11},{10,... | collective-permute-start | bytes 2654216 | tf_op jit(solution)/shard_map/ppermute | solution.py:849
  31.9 34.1 %collective-permute-start.3 = (bf16[576,768]{1,0:T(8,128)(2,1)S(1)}, bf16[576,768]{1,0:T(8,128)(2,1)S(1)}, u32[]{:S(2)}, u32[]{:S(2)}) collective-permute-start(bf16[576,768]{1,0:T(8,128)(2,1)S(1)} %collective-permute-done.refs_5_), channel_id=1, source_target_pairs={{0,8},{1,9},{2,10},{3,11},{4,12},{5,13},{6,14},{7,15},{8,0},{9,1},... | collective-permute-start | bytes 2654216 | tf_op jit(solution)/shard_map/ppermute | solution.py:849
  32.1 36.4 %collective-permute-start.1 = (bf16[576,768]{1,0:T(8,128)(2,1)S(1)}, bf16[576,768]{1,0:T(8,128)(2,1)}, u32[]{:S(2)}, u32[]{:S(2)}) collective-permute-start(bf16[576,768]{1,0:T(8,128)(2,1)S(1)} %collective-permute-done.refs_5_), channel_id=1, source_target_pairs={{0,2},{1,3},{2,6},{3,7},{4,0},{5,1},{6,4},{7,5},{8,10},{9,11},{10,... | collective-permute-start | bytes 2654216 | tf_op jit(solution)/shard_map/ppermute | solution.py:849
  33.3 36.0 %collective-permute-start.7 = (bf16[576,768]{1,0:T(8,128)(2,1)}, bf16[576,768]{1,0:T(8,128)(2,1)S(1)}, u32[]{:S(2)}, u32[]{:S(2)}) collective-permute-start(bf16[576,768]{1,0:T(8,128)(2,1)} %get-tuple-element.40.refs_1_), channel_id=1, source_target_pairs={{0,1},{1,0},{2,3},{3,2},{4,5},{5,4},{6,7},{7,6},{8,9},{9,8},{10,11... | collective-permute-start | bytes 2654216 | tf_op jit(solution)/shard_map/ppermute | solution.py:849
  47.8 21.5 %collective-permute-start.6 = (bf16[576,768]{1,0:T(8,128)(2,1)}, bf16[576,768]{1,0:T(8,128)(2,1)S(1)}, u32[]{:S(2)}, u32[]{:S(2)}) collective-permute-start(bf16[576,768]{1,0:T(8,128)(2,1)} %get-tuple-element.44.refs_0_), channel_id=1, source_target_pairs={{0,1},{1,0},{2,3},{3,2},{4,5},{5,4},{6,7},{7,6},{8,9},{9,8},{10,11... | collective-permute-start | bytes 2654216 | tf_op jit(solution)/shard_map/ppermute | solution.py:849
  66.0 20.9 %collective-permute-start.17 = (bf16[576,768]{1,0:T(8,128)(2,1)S(1)}, bf16[576,768]{1,0:T(8,128)(2,1)S(1)}, u32[]{:S(2)}, u32[]{:S(2)}) collective-permute-start(bf16[576,768]{1,0:T(8,128)(2,1)S(1)} %collective-permute-done.8.refs_4_), channel_id=1, source_target_pairs={{0,8},{1,9},{2,10},{3,11},{4,12},{5,13},{6,14},{7,15},{8,0},{9,1},... | collective-permute-start | bytes 2654216 | tf_op jit(solution)/shard_map/ppermute | solution.py:849
  68.4 22.4 %collective-permute-start.11 = (bf16[576,768]{1,0:T(8,128)(2,1)S(1)}, bf16[576,768]{1,0:T(8,128)(2,1)}, u32[]{:S(2)}, u32[]{:S(2)}) collective-permute-start(bf16[576,768]{1,0:T(8,128)(2,1)S(1)} %collective-permute-done.8.refs_4_), channel_id=1, source_target_pairs={{0,2},{1,3},{2,6},{3,7},{4,0},{5,1},{6,4},{7,5},{8,10},{9,11},{10,... | collective-permute-start | bytes 2654216 | tf_op jit(solution)/shard_map/ppermute | solution.py:849
  69.3 24.2 %collective-permute-start.10 = (bf16[576,768]{1,0:T(8,128)(2,1)S(1)}, bf16[576,768]{1,0:T(8,128)(2,1)}, u32[]{:S(2)}, u32[]{:S(2)}) collective-permute-start(bf16[576,768]{1,0:T(8,128)(2,1)S(1)} %collective-permute-done.refs_5_), channel_id=1, source_target_pairs={{0,1},{1,0},{2,3},{3,2},{4,5},{5,4},{6,7},{7,6},{8,9},{9,8},{10,11... | collective-permute-start | bytes 2654216 | tf_op jit(solution)/shard_map/ppermute | solution.py:849
  69.3 24.2 %collective-permute-start.15 = (bf16[576,768]{1,0:T(8,128)(2,1)S(1)}, bf16[576,768]{1,0:T(8,128)(2,1)}, u32[]{:S(2)}, u32[]{:S(2)}) collective-permute-start(bf16[576,768]{1,0:T(8,128)(2,1)S(1)} %collective-permute-done.14.refs_12_), channel_id=1, source_target_pairs={{0,1},{1,0},{2,3},{3,2},{4,5},{5,4},{6,7},{7,6},{8,9},{9,8},{10,11... | collective-permute-start | bytes 2654216 | tf_op jit(solution)/shard_map/ppermute | solution.py:849
  69.8 24.2 %collective-permute-start.9 = (bf16[576,768]{1,0:T(8,128)(2,1)S(1)}, bf16[576,768]{1,0:T(8,128)(2,1)}, u32[]{:S(2)}, u32[]{:S(2)}) collective-permute-start(bf16[576,768]{1,0:T(8,128)(2,1)S(1)} %collective-permute-done.8.refs_4_), channel_id=1, source_target_pairs={{0,1},{1,0},{2,3},{3,2},{4,5},{5,4},{6,7},{7,6},{8,9},{9,8},{10,11... | collective-permute-start | bytes 2654216 | tf_op jit(solution)/shard_map/ppermute | solution.py:849
  87.8 20.4 %collective-permute-start.4 = (bf16[576,768]{1,0:T(8,128)(2,1)}, bf16[576,768]{1,0:T(8,128)(2,1)}, u32[]{:S(2)}, u32[]{:S(2)}) collective-permute-start(bf16[576,768]{1,0:T(8,128)(2,1)} %collective-permute-done.1.refs_9_), channel_id=1, source_target_pairs={{0,8},{1,9},{2,10},{3,11},{4,12},{5,13},{6,14},{7,15},{8,0},{9,1},... | collective-permute-start | bytes 2654216 | tf_op jit(solution)/shard_map/ppermute | solution.py:849
  93.5 20.5 %collective-permute-start.13 = (bf16[576,768]{1,0:T(8,128)(2,1)}, bf16[576,768]{1,0:T(8,128)(2,1)S(1)}, u32[]{:S(2)}, u32[]{:S(2)}) collective-permute-start(bf16[576,768]{1,0:T(8,128)(2,1)} %collective-permute-done.1.refs_9_), channel_id=1, source_target_pairs={{0,1},{1,0},{2,3},{3,2},{4,5},{5,4},{6,7},{7,6},{8,9},{9,8},{10,11... | collective-permute-start | bytes 2654216 | tf_op jit(solution)/shard_map/ppermute | solution.py:849
  108.3 22.8 %collective-permute-start.20 = (bf16[576,768]{1,0:T(8,128)(2,1)}, bf16[576,768]{1,0:T(8,128)(2,1)S(1)}, u32[]{:S(2)}, u32[]{:S(2)}) collective-permute-start(bf16[576,768]{1,0:T(8,128)(2,1)} %collective-permute-done.11.refs_8_), channel_id=1, source_target_pairs={{0,8},{1,9},{2,10},{3,11},{4,12},{5,13},{6,14},{7,15},{8,0},{9,1},... | collective-permute-start | bytes 2654216 | tf_op jit(solution)/shard_map/ppermute | solution.py:849
  110.5 22.8 %collective-permute-start.12 = (bf16[576,768]{1,0:T(8,128)(2,1)}, bf16[576,768]{1,0:T(8,128)(2,1)S(1)}, u32[]{:S(2)}, u32[]{:S(2)}) collective-permute-start(bf16[576,768]{1,0:T(8,128)(2,1)} %collective-permute-done.11.refs_8_), channel_id=1, source_target_pairs={{0,1},{1,0},{2,3},{3,2},{4,5},{5,4},{6,7},{7,6},{8,9},{9,8},{10,11... | collective-permute-start | bytes 2654216 | tf_op jit(solution)/shard_map/ppermute | solution.py:849
  110.5 24.3 %collective-permute-start.27 = (bf16[576,768]{1,0:T(8,128)(2,1)S(1)}, bf16[576,768]{1,0:T(8,128)(2,1)S(1)}, u32[]{:S(2)}, u32[]{:S(2)}) collective-permute-start(bf16[576,768]{1,0:T(8,128)(2,1)S(1)} %get-tuple-element.49), channel_id=1, source_target_pairs={{0,4},{1,5},{2,0},{3,1},{4,6},{5,7},{6,2},{7,3},{8,12},{9,13},{10,... | collective-permute-start | bytes 2654216 | tf_op jit(solution)/shard_map/ppermute | solution.py:849
  114.0 34.8 %collective-permute-start.22 = (bf16[576,768]{1,0:T(8,128)(2,1)}, bf16[576,768]{1,0:T(8,128)(2,1)S(1)}, u32[]{:S(2)}, u32[]{:S(2)}) collective-permute-start(bf16[576,768]{1,0:T(8,128)(2,1)} %collective-permute-done.4.refs_21_), channel_id=1, source_target_pairs={{0,1},{1,0},{2,3},{3,2},{4,5},{5,4},{6,7},{7,6},{8,9},{9,8},{10,11... | collective-permute-start | bytes 2654216 | tf_op jit(solution)/shard_map/ppermute | solution.py:849
  114.2 35.1 %collective-permute-start.25 = (bf16[576,768]{1,0:T(8,128)(2,1)S(1)}, bf16[576,768]{1,0:T(8,128)(2,1)S(1)}, u32[]{:S(2)}, u32[]{:S(2)}) collective-permute-start(bf16[576,768]{1,0:T(8,128)(2,1)S(1)} %collective-permute-done.23.refs_24_), channel_id=1, source_target_pairs={{0,8},{1,9},{2,10},{3,11},{4,12},{5,13},{6,14},{7,15},{8,0},{9,1},... | collective-permute-start | bytes 2654216 | tf_op jit(solution)/shard_map/ppermute | solution.py:849
  131.1 21.4 %collective-permute-start.28 = (bf16[576,768]{1,0:T(8,128)(2,1)S(1)}, bf16[576,768]{1,0:T(8,128)(2,1)S(1)}, u32[]{:S(2)}, u32[]{:S(2)}) collective-permute-start(bf16[576,768]{1,0:T(8,128)(2,1)S(1)} %get-tuple-element.50), channel_id=1, source_target_pairs={{0,4},{1,5},{2,0},{3,1},{4,6},{5,7},{6,2},{7,3},{8,12},{9,13},{10,... | collective-permute-start | bytes 2654216 | tf_op jit(solution)/shard_map/ppermute | solution.py:849
  260.8 52.1 %collective-permute-start.32 = (bf16[512,768]{1,0:T(8,128)(2,1)}, bf16[512,768]{1,0:T(8,128)(2,1)S(1)}, u32[]{:S(2)}, u32[]{:S(2)}) collective-permute-start(bf16[512,768]{1,0:T(8,128)(2,1)} %get-tuple-element.55), channel_id=1, source_target_pairs={{0,16},{1,17},{2,18},{3,19},{4,20},{5,21},{6,22},{7,23},{8,24},{9,... | collective-permute-start | bytes 2359304 | tf_op jit(solution)/shard_map/ppermute | solution.py:849
  295.2 61.3 %collective-permute-start.33 = (bf16[512,768]{1,0:T(8,128)(2,1)}, bf16[512,768]{1,0:T(8,128)(2,1)S(1)}, u32[]{:S(2)}, u32[]{:S(2)}) collective-permute-start(bf16[512,768]{1,0:T(8,128)(2,1)} %get-tuple-element.65), channel_id=1, source_target_pairs={{0,8},{1,9},{2,10},{3,11},{4,12},{5,13},{6,14},{7,15},{8,0},{9,1},... | collective-permute-start | bytes 2359304 | tf_op jit(solution)/shard_map/ppermute | solution.py:849
  295.9 60.6 %collective-permute-start.34 = (bf16[512,768]{1,0:T(8,128)(2,1)}, bf16[512,768]{1,0:T(8,128)(2,1)S(1)}, u32[]{:S(2)}, u32[]{:S(2)}) collective-permute-start(bf16[512,768]{1,0:T(8,128)(2,1)} %get-tuple-element.66), channel_id=1, source_target_pairs={{0,8},{1,9},{2,10},{3,11},{4,12},{5,13},{6,14},{7,15},{8,0},{9,1},... | collective-permute-start | bytes 2359304 | tf_op jit(solution)/shard_map/ppermute | solution.py:849
  (49 other events, 825.7 us)

commit v5 on v4

--- a/solution.py
+++ b/solution.py
@@ -300,15 +300,15 @@
             after(pair // 2)
     for part in ("r", "mixed", "qkv") + ((0, 1, 2) if together else ()):
         spent(part)
+    total = d_summed
+    for kind in range(3):
+        total = total + dot(d_qkv[:, kind * width : (kind + 1) * width], rows_of(w, l, kind), 1, 1)
+    c_out[...] = total.astype(BF)
     have("x")
     down = dot(x[l], prm[l, 12:28, :].astype(BF), 1, 1).astype(BF)
     rank = down.shape[1] // 2
     d_up[l, 0:rank, :] = 2.0 * dot(down, d_qkv[:, 0:width], 0, 0)[0:rank]
     d_up[l, rank : 2 * rank, :] = 2.0 * dot(down, d_qkv[:, 2 * width : 3 * width], 0, 0)[rank:]
-    total = d_summed
-    for kind in range(3):
-        total = total + dot(d_qkv[:, kind * width : (kind + 1) * width], rows_of(w, l, kind), 1, 1)
-    c_out[...] = total.astype(BF)
 
 
 def state_shapes(length, width):

time: 379 us -> 371 us (0.979); the launches traced: 380 us -> 367 us
  starting transfers between devices: 71.2 us -> 59.6 us
    ppermute x41, starting transfers between devices: 71.2 us -> 59.6 us  [permuted(): return lax.ppermute(array, AXES, pairs)]
where the time goes in v5:
time: 371 us; the launch traced here: 367 us
  waiting for transfers between devices  164 us (44%)
  Pallas kernels  130 us (35%)
  starting transfers between devices  59.6 us (16%)
  local copies, waits for them, and re-layouts  7.46 us (2%)
  other arithmetic  4.29 us (1%)
    ppermute x41, waiting for transfers between devices, permuted(): return lax.ppermute(array, AXES, pairs)  164 us
    ppermute x41, starting transfers between devices, permuted(): return lax.ppermute(array, AXES, pairs)  59.6 us
    pallas_call x1, Pallas kernels, run_middle(): pl.pallas_call(middle_kernel, out_shape=outs, in_specs=[smem, smem] + [an...  46.3 us
    pallas_call x1, Pallas kernels, run_last(): pl.pallas_call(last_kernel, out_shape=[rows, rows, row, shape((2, 16, wid...  41.8 us
    pallas_call x1, Pallas kernels, run_first(): pl.pallas_call(first_kernel, out_shape=outs, in_specs=[smem, smem, anywhe...  38.8 us
  transfers between devices with their start and end apart: 41, of which 20 were waited for; matrix products, arithmetic and copies ran while one was open for 1% of the time, Pallas kernels for 11%

profile of v5, /device:TPU:0, one launch (start us, length us, event | category | flops | bytes accessed | tf_op | source)
XLA Modules:
  0.0 366.7 jit_solution(3391195563445669827)
XLA Ops:
  1.8 3.4 pack.1
  5.2 2.9 collective-permute-start.2
  10.3 2.6 collective-permute-start.8
  12.9 16.0 %collective-permute-done.2.refs_13_ = bf16[576,768]{1,0:T(8,128)(2,1)S(1)} collective-permute-done((bf16[576,768]{1,0:T(8,128)(2,1)}, bf16[576,768]{1,0:T(8,128)(2,1)S(1)}, u32[]{:S(2)}, u32[]{:S(2)}) %collective-permute-start.2) | collective-permute-done | bytes 884768 | tf_op jit(solution)/shard_map/ppermute | solution.py:849
  28.9 3.0 collective-permute-done.refs_5_
  33.3 14.5 %collective-permute-done.14.refs_12_ = bf16[576,768]{1,0:T(8,128)(2,1)S(1)} collective-permute-done((bf16[576,768]{1,0:T(8,128)(2,1)}, bf16[576,768]{1,0:T(8,128)(2,1)S(1)}, u32[]{:S(2)}, u32[]{:S(2)}) %collective-permute-start.14) | collective-permute-done | bytes 884768 | tf_op jit(solution)/shard_map/ppermute | solution.py:849
  47.8 3.0 collective-permute-done.8.refs_4_
  50.8 15.1 %collective-permute-done.3.refs_17_ = bf16[576,768]{1,0:T(8,128)(2,1)S(1)} collective-permute-done((bf16[576,768]{1,0:T(8,128)(2,1)S(1)}, bf16[576,768]{1,0:T(8,128)(2,1)S(1)}, u32[]{:S(2)}, u32[]{:S(2)}) %collective-permute-start.3) | collective-permute-done | bytes 884768 | tf_op jit(solution)/shard_map/ppermute | solution.py:849
  69.9 17.0 %collective-permute-done.17.refs_16_ = bf16[576,768]{1,0:T(8,128)(2,1)S(1)} collective-permute-done((bf16[576,768]{1,0:T(8,128)(2,1)S(1)}, bf16[576,768]{1,0:T(8,128)(2,1)S(1)}, u32[]{:S(2)}, u32[]{:S(2)}) %collective-permute-start.17) | collective-permute-done | bytes 884768 | tf_op jit(solution)/shard_map/ppermute | solution.py:849
  90.8 2.6 collective-permute-start.23
  94.1 14.2 %collective-permute-done.4.refs_21_ = bf16[576,768]{1,0:T(8,128)(2,1)} collective-permute-done((bf16[576,768]{1,0:T(8,128)(2,1)}, bf16[576,768]{1,0:T(8,128)(2,1)}, u32[]{:S(2)}, u32[]{:S(2)}) %collective-permute-start.4) | collective-permute-done | bytes 884768 | tf_op jit(solution)/shard_map/ppermute | solution.py:849
  110.5 3.4 collective-permute-start.27
  115.0 16.1 %collective-permute-done.20.refs_20_ = bf16[576,768]{1,0:T(8,128)(2,1)S(1)} collective-permute-done((bf16[576,768]{1,0:T(8,128)(2,1)}, bf16[576,768]{1,0:T(8,128)(2,1)S(1)}, u32[]{:S(2)}, u32[]{:S(2)}) %collective-permute-start.20) | collective-permute-done | bytes 884768 | tf_op jit(solution)/shard_map/ppermute | solution.py:849
  134.9 13.9 %collective-permute-done.5.theirs = f32[32,768]{1,0:T(8,128)S(1)} collective-permute-done((f32[32,768]{1,0:T(8,128)S(1)}, f32[32,768]{1,0:T(8,128)S(1)}, u32[]{:S(2)}, u32[]{:S(2)}) %collective-permute-start.5) | collective-permute-done | bytes 98336 | tf_op jit(solution)/shard_map/ppermute | solution.py:849
  149.4 3.1 collective-permute-done.28.refs_29_
  155.2 38.8 %first.1 = (bf16[2,8,1152,768]{3,2,1,0:T(8,128)(2,1)}, bf16[512,768]{1,0:T(8,128)(2,1)}, bf16[512,768]{1,0:T(8,128)(2,1)}, bf16[2,3,512,768]{3,2,1,0:T(8,128)(2,...) custom-call(s32[12]{0:T(128)} %fusion.scal, ...), custom_call_target="tpu_custom_call" | custom-call | flops 16106127360 | bytes 28311552 | tf_op jit(solution)/shard_map/first/pallas_call | solution.py:741
  195.3 17.7 %collective-permute-done.31.arrived = bf16[512,768]{1,0:T(8,128)(2,1)S(1)} collective-permute-done((bf16[512,768]{1,0:T(8,128)(2,1)}, bf16[512,768]{1,0:T(8,128)(2,1)S(1)}, u32[]{:S(2)}, u32[]{:S(2)}) %collective-permute-start.31) | collective-permute-done | bytes 786464 | tf_op jit(solution)/shard_map/ppermute | solution.py:849
  213.9 46.3 %middle.1 = (bf16[512,768]{1,0:T(8,128)(2,1)}, bf16[2,512,768]{2,1,0:T(8,128)(2,1)}, bf16[512,768]{1,0:T(8,128)(2,1)}, bf16[2,512,768]{2,1,0:T(8,128)(2,1)}, bf1...) custom-call(s32[12]{0:T(128)} %fusion.scal, ...), custom_call_target="tpu_custom_call" | custom-call | flops 34628173824 | bytes 28311552 | tf_op jit(solution)/shard_map/middle/pallas_call | solution.py:762
  260.3 22.9 %collective-permute-start.32 = (bf16[512,768]{1,0:T(8,128)(2,1)}, bf16[512,768]{1,0:T(8,128)(2,1)S(1)}, u32[]{:S(2)}, u32[]{:S(2)}) collective-permute-start(bf16[512,768]{1,0:T(8,128)(2,1)} %get-tuple-element.55), channel_id=1, source_target_pairs={{0,16},{1,17},{2,18},{3,19},{4,20},{5,21},{6,22},{7,23},{8,24},{9,... | collective-permute-start | bytes 2359304 | tf_op jit(solution)/shard_map/ppermute | solution.py:849
  285.2 15.6 %collective-permute-done.32.arrived = bf16[512,768]{1,0:T(8,128)(2,1)S(1)} collective-permute-done((bf16[512,768]{1,0:T(8,128)(2,1)}, bf16[512,768]{1,0:T(8,128)(2,1)S(1)}, u32[]{:S(2)}, u32[]{:S(2)}) %collective-permute-start.32) | collective-permute-done | bytes 786464 | tf_op jit(solution)/shard_map/ppermute | solution.py:849
  301.7 41.8 %last.1 = (bf16[2,512,768]{2,1,0:T(8,128)(2,1)}, bf16[2,512,768]{2,1,0:T(8,128)(2,1)}, bf16[512,768]{1,0:T(8,128)(2,1)}, f32[2,16,768]{2,1,0:T(8,128)}) custom-call(s32[12]{0:T(128)} %fusion.scal, s32[2,8]{1,0:T(2,128)} %lens.5, bf16[2,512,768]{2,1,0:T(8,128)(2,1)} %source.5, bf16[512,768]{1,0:T(8,128)(2,1)} %copy-done.28, ...), custom_call_target="tpu_custom_call" | custom-call | flops 18522046464 | bytes 28311552 | tf_op jit(solution)/shard_map/last/pallas_call | solution.py:786
  346.5 2.6 collective-permute-done.36
  356.4 2.7 collective-permute-done.39
  359.8 4.4 %collective-permute-done.35 = bf16[512,768]{1,0:T(8,128)(2,1)S(1)} collective-permute-done((bf16[512,768]{1,0:T(8,128)(2,1)}, bf16[512,768]{1,0:T(8,128)(2,1)S(1)}, u32[]{:S(2)}, u32[]{:S(2)}) %collective-permute-start.35) | collective-permute-done | bytes 786464 | tf_op jit(solution)/shard_map/ppermute | solution.py:849
  (135 shorter events, 41.8 us)
Async XLA Ops:
  5.2 23.6 %collective-permute-start.2 = (bf16[576,768]{1,0:T(8,128)(2,1)}, bf16[576,768]{1,0:T(8,128)(2,1)S(1)}, u32[]{:S(2)}, u32[]{:S(2)}) collective-permute-start(bf16[576,768]{1,0:T(8,128)(2,1)} %get-tuple-element.40.refs_1_), channel_id=1, source_target_pairs={{0,8},{1,9},{2,10},{3,11},{4,12},{5,13},{6,14},{7,15},{8,0},{9,1},... | collective-permute-start | bytes 2654216 | tf_op jit(solution)/shard_map/ppermute | solution.py:849
  8.2 23.7 %collective-permute-start = (bf16[576,768]{1,0:T(8,128)(2,1)}, bf16[576,768]{1,0:T(8,128)(2,1)S(1)}, u32[]{:S(2)}, u32[]{:S(2)}) collective-permute-start(bf16[576,768]{1,0:T(8,128)(2,1)} %get-tuple-element.40.refs_1_), channel_id=1, source_target_pairs={{0,2},{1,3},{2,6},{3,7},{4,0},{5,1},{6,4},{7,5},{8,10},{9,11},{10,... | collective-permute-start | bytes 2654216 | tf_op jit(solution)/shard_map/ppermute | solution.py:849
  9.8 38.1 %collective-permute-start.14 = (bf16[576,768]{1,0:T(8,128)(2,1)}, bf16[576,768]{1,0:T(8,128)(2,1)S(1)}, u32[]{:S(2)}, u32[]{:S(2)}) collective-permute-start(bf16[576,768]{1,0:T(8,128)(2,1)} %get-tuple-element.44.refs_0_), channel_id=1, source_target_pairs={{0,8},{1,9},{2,10},{3,11},{4,12},{5,13},{6,14},{7,15},{8,0},{9,1},... | collective-permute-start | bytes 2654216 | tf_op jit(solution)/shard_map/ppermute | solution.py:849
  10.3 40.5 %collective-permute-start.8 = (bf16[576,768]{1,0:T(8,128)(2,1)}, bf16[576,768]{1,0:T(8,128)(2,1)S(1)}, u32[]{:S(2)}, u32[]{:S(2)}) collective-permute-start(bf16[576,768]{1,0:T(8,128)(2,1)} %get-tuple-element.44.refs_0_), channel_id=1, source_target_pairs={{0,2},{1,3},{2,6},{3,7},{4,0},{5,1},{6,4},{7,5},{8,10},{9,11},{10,... | collective-permute-start | bytes 2654216 | tf_op jit(solution)/shard_map/ppermute | solution.py:849
  31.9 34.1 %collective-permute-start.3 = (bf16[576,768]{1,0:T(8,128)(2,1)S(1)}, bf16[576,768]{1,0:T(8,128)(2,1)S(1)}, u32[]{:S(2)}, u32[]{:S(2)}) collective-permute-start(bf16[576,768]{1,0:T(8,128)(2,1)S(1)} %collective-permute-done.refs_5_), channel_id=1, source_target_pairs={{0,8},{1,9},{2,10},{3,11},{4,12},{5,13},{6,14},{7,15},{8,0},{9,1},... | collective-permute-start | bytes 2654216 | tf_op jit(solution)/shard_map/ppermute | solution.py:849
  32.1 36.4 %collective-permute-start.1 = (bf16[576,768]{1,0:T(8,128)(2,1)S(1)}, bf16[576,768]{1,0:T(8,128)(2,1)}, u32[]{:S(2)}, u32[]{:S(2)}) collective-permute-start(bf16[576,768]{1,0:T(8,128)(2,1)S(1)} %collective-permute-done.refs_5_), channel_id=1, source_target_pairs={{0,2},{1,3},{2,6},{3,7},{4,0},{5,1},{6,4},{7,5},{8,10},{9,11},{10,... | collective-permute-start | bytes 2654216 | tf_op jit(solution)/shard_map/ppermute | solution.py:849
  33.3 36.0 %collective-permute-start.7 = (bf16[576,768]{1,0:T(8,128)(2,1)}, bf16[576,768]{1,0:T(8,128)(2,1)S(1)}, u32[]{:S(2)}, u32[]{:S(2)}) collective-permute-start(bf16[576,768]{1,0:T(8,128)(2,1)} %get-tuple-element.40.refs_1_), channel_id=1, source_target_pairs={{0,1},{1,0},{2,3},{3,2},{4,5},{5,4},{6,7},{7,6},{8,9},{9,8},{10,11... | collective-permute-start | bytes 2654216 | tf_op jit(solution)/shard_map/ppermute | solution.py:849
  47.8 21.5 %collective-permute-start.6 = (bf16[576,768]{1,0:T(8,128)(2,1)}, bf16[576,768]{1,0:T(8,128)(2,1)S(1)}, u32[]{:S(2)}, u32[]{:S(2)}) collective-permute-start(bf16[576,768]{1,0:T(8,128)(2,1)} %get-tuple-element.44.refs_0_), channel_id=1, source_target_pairs={{0,1},{1,0},{2,3},{3,2},{4,5},{5,4},{6,7},{7,6},{8,9},{9,8},{10,11... | collective-permute-start | bytes 2654216 | tf_op jit(solution)/shard_map/ppermute | solution.py:849
  66.0 20.9 %collective-permute-start.17 = (bf16[576,768]{1,0:T(8,128)(2,1)S(1)}, bf16[576,768]{1,0:T(8,128)(2,1)S(1)}, u32[]{:S(2)}, u32[]{:S(2)}) collective-permute-start(bf16[576,768]{1,0:T(8,128)(2,1)S(1)} %collective-permute-done.8.refs_4_), channel_id=1, source_target_pairs={{0,8},{1,9},{2,10},{3,11},{4,12},{5,13},{6,14},{7,15},{8,0},{9,1},... | collective-permute-start | bytes 2654216 | tf_op jit(solution)/shard_map/ppermute | solution.py:849
  68.4 22.4 %collective-permute-start.11 = (bf16[576,768]{1,0:T(8,128)(2,1)S(1)}, bf16[576,768]{1,0:T(8,128)(2,1)}, u32[]{:S(2)}, u32[]{:S(2)}) collective-permute-start(bf16[576,768]{1,0:T(8,128)(2,1)S(1)} %collective-permute-done.8.refs_4_), channel_id=1, source_target_pairs={{0,2},{1,3},{2,6},{3,7},{4,0},{5,1},{6,4},{7,5},{8,10},{9,11},{10,... | collective-permute-start | bytes 2654216 | tf_op jit(solution)/shard_map/ppermute | solution.py:849
  69.3 24.2 %collective-permute-start.10 = (bf16[576,768]{1,0:T(8,128)(2,1)S(1)}, bf16[576,768]{1,0:T(8,128)(2,1)}, u32[]{:S(2)}, u32[]{:S(2)}) collective-permute-start(bf16[576,768]{1,0:T(8,128)(2,1)S(1)} %collective-permute-done.refs_5_), channel_id=1, source_target_pairs={{0,1},{1,0},{2,3},{3,2},{4,5},{5,4},{6,7},{7,6},{8,9},{9,8},{10,11... | collective-permute-start | bytes 2654216 | tf_op jit(solution)/shard_map/ppermute | solution.py:849
  69.3 24.2 %collective-permute-start.15 = (bf16[576,768]{1,0:T(8,128)(2,1)S(1)}, bf16[576,768]{1,0:T(8,128)(2,1)}, u32[]{:S(2)}, u32[]{:S(2)}) collective-permute-start(bf16[576,768]{1,0:T(8,128)(2,1)S(1)} %collective-permute-done.14.refs_12_), channel_id=1, source_target_pairs={{0,1},{1,0},{2,3},{3,2},{4,5},{5,4},{6,7},{7,6},{8,9},{9,8},{10,11... | collective-permute-start | bytes 2654216 | tf_op jit(solution)/shard_map/ppermute | solution.py:849
  69.8 24.2 %collective-permute-start.9 = (bf16[576,768]{1,0:T(8,128)(2,1)S(1)}, bf16[576,768]{1,0:T(8,128)(2,1)}, u32[]{:S(2)}, u32[]{:S(2)}) collective-permute-start(bf16[576,768]{1,0:T(8,128)(2,1)S(1)} %collective-permute-done.8.refs_4_), channel_id=1, source_target_pairs={{0,1},{1,0},{2,3},{3,2},{4,5},{5,4},{6,7},{7,6},{8,9},{9,8},{10,11... | collective-permute-start | bytes 2654216 | tf_op jit(solution)/shard_map/ppermute | solution.py:849
  87.8 20.4 %collective-permute-start.4 = (bf16[576,768]{1,0:T(8,128)(2,1)}, bf16[576,768]{1,0:T(8,128)(2,1)}, u32[]{:S(2)}, u32[]{:S(2)}) collective-permute-start(bf16[576,768]{1,0:T(8,128)(2,1)} %collective-permute-done.1.refs_9_), channel_id=1, source_target_pairs={{0,8},{1,9},{2,10},{3,11},{4,12},{5,13},{6,14},{7,15},{8,0},{9,1},... | collective-permute-start | bytes 2654216 | tf_op jit(solution)/shard_map/ppermute | solution.py:849
  93.5 20.5 %collective-permute-start.13 = (bf16[576,768]{1,0:T(8,128)(2,1)}, bf16[576,768]{1,0:T(8,128)(2,1)S(1)}, u32[]{:S(2)}, u32[]{:S(2)}) collective-permute-start(bf16[576,768]{1,0:T(8,128)(2,1)} %collective-permute-done.1.refs_9_), channel_id=1, source_target_pairs={{0,1},{1,0},{2,3},{3,2},{4,5},{5,4},{6,7},{7,6},{8,9},{9,8},{10,11... | collective-permute-start | bytes 2654216 | tf_op jit(solution)/shard_map/ppermute | solution.py:849
  108.3 22.8 %collective-permute-start.20 = (bf16[576,768]{1,0:T(8,128)(2,1)}, bf16[576,768]{1,0:T(8,128)(2,1)S(1)}, u32[]{:S(2)}, u32[]{:S(2)}) collective-permute-start(bf16[576,768]{1,0:T(8,128)(2,1)} %collective-permute-done.11.refs_8_), channel_id=1, source_target_pairs={{0,8},{1,9},{2,10},{3,11},{4,12},{5,13},{6,14},{7,15},{8,0},{9,1},... | collective-permute-start | bytes 2654216 | tf_op jit(solution)/shard_map/ppermute | solution.py:849
  110.5 22.8 %collective-permute-start.12 = (bf16[576,768]{1,0:T(8,128)(2,1)}, bf16[576,768]{1,0:T(8,128)(2,1)S(1)}, u32[]{:S(2)}, u32[]{:S(2)}) collective-permute-start(bf16[576,768]{1,0:T(8,128)(2,1)} %collective-permute-done.11.refs_8_), channel_id=1, source_target_pairs={{0,1},{1,0},{2,3},{3,2},{4,5},{5,4},{6,7},{7,6},{8,9},{9,8},{10,11... | collective-permute-start | bytes 2654216 | tf_op jit(solution)/shard_map/ppermute | solution.py:849
  110.5 24.3 %collective-permute-start.27 = (bf16[576,768]{1,0:T(8,128)(2,1)S(1)}, bf16[576,768]{1,0:T(8,128)(2,1)S(1)}, u32[]{:S(2)}, u32[]{:S(2)}) collective-permute-start(bf16[576,768]{1,0:T(8,128)(2,1)S(1)} %get-tuple-element.49), channel_id=1, source_target_pairs={{0,4},{1,5},{2,0},{3,1},{4,6},{5,7},{6,2},{7,3},{8,12},{9,13},{10,... | collective-permute-start | bytes 2654216 | tf_op jit(solution)/shard_map/ppermute | solution.py:849
  114.0 34.8 %collective-permute-start.22 = (bf16[576,768]{1,0:T(8,128)(2,1)}, bf16[576,768]{1,0:T(8,128)(2,1)S(1)}, u32[]{:S(2)}, u32[]{:S(2)}) collective-permute-start(bf16[576,768]{1,0:T(8,128)(2,1)} %collective-permute-done.4.refs_21_), channel_id=1, source_target_pairs={{0,1},{1,0},{2,3},{3,2},{4,5},{5,4},{6,7},{7,6},{8,9},{9,8},{10,11... | collective-permute-start | bytes 2654216 | tf_op jit(solution)/shard_map/ppermute | solution.py:849
  114.2 35.1 %collective-permute-start.25 = (bf16[576,768]{1,0:T(8,128)(2,1)S(1)}, bf16[576,768]{1,0:T(8,128)(2,1)S(1)}, u32[]{:S(2)}, u32[]{:S(2)}) collective-permute-start(bf16[576,768]{1,0:T(8,128)(2,1)S(1)} %collective-permute-done.23.refs_24_), channel_id=1, source_target_pairs={{0,8},{1,9},{2,10},{3,11},{4,12},{5,13},{6,14},{7,15},{8,0},{9,1},... | collective-permute-start | bytes 2654216 | tf_op jit(solution)/shard_map/ppermute | solution.py:849
  131.1 21.4 %collective-permute-start.28 = (bf16[576,768]{1,0:T(8,128)(2,1)S(1)}, bf16[576,768]{1,0:T(8,128)(2,1)S(1)}, u32[]{:S(2)}, u32[]{:S(2)}) collective-permute-start(bf16[576,768]{1,0:T(8,128)(2,1)S(1)} %get-tuple-element.50), channel_id=1, source_target_pairs={{0,4},{1,5},{2,0},{3,1},{4,6},{5,7},{6,2},{7,3},{8,12},{9,13},{10,... | collective-permute-start | bytes 2654216 | tf_op jit(solution)/shard_map/ppermute | solution.py:849
  260.3 40.5 %collective-permute-start.32 = (bf16[512,768]{1,0:T(8,128)(2,1)}, bf16[512,768]{1,0:T(8,128)(2,1)S(1)}, u32[]{:S(2)}, u32[]{:S(2)}) collective-permute-start(bf16[512,768]{1,0:T(8,128)(2,1)} %get-tuple-element.55), channel_id=1, source_target_pairs={{0,16},{1,17},{2,18},{3,19},{4,20},{5,21},{6,22},{7,23},{8,24},{9,... | collective-permute-start | bytes 2359304 | tf_op jit(solution)/shard_map/ppermute | solution.py:849
  283.1 60.3 %collective-permute-start.33 = (bf16[512,768]{1,0:T(8,128)(2,1)}, bf16[512,768]{1,0:T(8,128)(2,1)S(1)}, u32[]{:S(2)}, u32[]{:S(2)}) collective-permute-start(bf16[512,768]{1,0:T(8,128)(2,1)} %get-tuple-element.65), channel_id=1, source_target_pairs={{0,8},{1,9},{2,10},{3,11},{4,12},{5,13},{6,14},{7,15},{8,0},{9,1},... | collective-permute-start | bytes 2359304 | tf_op jit(solution)/shard_map/ppermute | solution.py:849
  283.8 59.7 %collective-permute-start.34 = (bf16[512,768]{1,0:T(8,128)(2,1)}, bf16[512,768]{1,0:T(8,128)(2,1)S(1)}, u32[]{:S(2)}, u32[]{:S(2)}) collective-permute-start(bf16[512,768]{1,0:T(8,128)(2,1)} %get-tuple-element.66), channel_id=1, source_target_pairs={{0,8},{1,9},{2,10},{3,11},{4,12},{5,13},{6,14},{7,15},{8,0},{9,1},... | collective-permute-start | bytes 2359304 | tf_op jit(solution)/shard_map/ppermute | solution.py:849
  (49 other events, 824.8 us)
